TPU v7x, 128 devices: a whole 4x4x4 slice. The times are simulated.
128 devices in a mesh: grp: 4 (over z_hi, core), dom: 32 (over x, y, z_lo).
Axes of the slice: x: 4, y: 4, z: 4 (z_hi: 2, z_lo: 2; z = z_hi * 2 + z_lo), core: 2. Of those that a mesh axis runs over, the one named last changes fastest.
Arguments:
- state: float32 [4, 3, 32, 65536], P('grp', None, None, 'dom'), may hold values from -4 to 4, as said below
- kappa: float32 [4, 65536], P('grp', 'dom'), may hold values from 0.02 to 0.3
- neighbours: int32 [4, 3, 65536], P('grp', None, 'dom'), may hold values from 0 to 2111, as said below
- parent: int32 [4, 65536], P('grp', 'dom'), may hold values from 0 to 511, as said below
- cos_zenith: float32 [4, 16384], P('grp', 'dom'), may hold values from -1 to 1
- routes: int32 [128, 32, 1], P(('grp', 'dom')), may hold values from 0 to 31; in each aligned block of 32 rows (0 to 31, 32 to 63, ..., all dimensions but the last counted through in order) at most 2 rows name the same one
- rad_albedo: float32 [4, 98304], P('grp', 'dom'), may hold values from 0.05 to 0.8
- aerosol_depth: float32 [4, 32, 14, 98304], P('grp', None, None, 'dom'), may hold values from 0.01 to 0.5
- aerosol_ssa: float32 [4, 32, 14, 98304], P('grp', None, None, 'dom'), may hold values from 0.3 to 0.99
- gas_table: float32 [112, 32], replicated, may hold values from 0.002 to 0.3
- cloud_ext: float32 [112], replicated, may hold values from 0.05 to 1
- cloud_ssa: float32 [112], replicated, may hold values from 0.5 to 0.99
- rayleigh: float32 [112], replicated, may hold values from 0.01 to 0.25
- solar_weight: float32 [112], replicated, may hold values from 0.1 to 1
Outputs:
- new_state: float32 [4, 3, 32, 65536], P('grp', None, None, 'dom')
Inputs may be any that keep to these rules, and one draw needn't show every extreme that they name: `state`: field 0 is a temperature anomaly; fields 1 and 2 are positive. `neighbours`: every neighbour lies within 32 cells of the cell's own position. Within each domain every coarse column is the parent of exactly four fine cells. `routes`: among the blocks of one device at most 2 go to one radiation domain.
All inputs are finite; a program needn't handle non-finite values.
Results may differ from a plain program's by a relative error of at most 0.0001.
Values sent between devices are 32-bit elements; how exact they have to be, the bound alone decides.
No kernel may reach another device: no remote copies, remote signals or barrier semaphores. Data moves between devices by JAX's collectives and lax.ppermute only.
A program may use at most 192 MiB of HBM per device.

v0:
```python
import jax
import jax.numpy as jnp
from jax import lax
from jax.sharding import PartitionSpec as P

HALO = 32


def padded(block, sides, width):
    for axis, dim in sides:
        count = lax.axis_size(axis)
        forward = [(i, i + 1) for i in range(count - 1)]
        forward.append((count - 1, 0))
        backward = [(target, source) for source, target in forward]
        low = lax.ppermute(
            lax.slice_in_dim(block, block.shape[dim] - width, None, axis=dim), axis, forward
        )
        high = lax.ppermute(lax.slice_in_dim(block, 0, width, axis=dim), axis, backward)
        block = jnp.concatenate([low, block, high], axis=dim)
    return block


def substep(fields, extended, rates, index):
    near = jnp.take(extended, index.reshape(-1), axis=2)
    near = near.reshape(fields.shape[0], fields.shape[1], 3, fields.shape[2])
    return fields + rates * (jnp.sum(near, axis=2) - 3.0 * fields)


def radiate(
    stacked_layer_values,
    sun_cosine,
    albedo,
    aero_depth,
    aero_ssa,
    gas_table,
    cloud_ext,
    cloud_ssa,
    rayleigh,
    solar_weight,
):
    thermal_state_kelvin = stacked_layer_values[0]
    humidity_mixing_ratio = stacked_layer_values[1]
    droplet_mixing_ratio = stacked_layer_values[2]
    levels = stacked_layer_values.shape[1]
    band_count = gas_table.shape[0]
    node_count = gas_table.shape[1]
    per_band = band_count // aero_depth.shape[1]
    aero_wide = jnp.repeat(aero_depth, per_band, axis=1)
    aero_scatter = jnp.repeat(aero_ssa, per_band, axis=1) * aero_wide
    mesh_spacing = 8.0 / (node_count - 1)
    polygon_midpoints = -4.0 + mesh_spacing * jnp.arange(node_count).astype(jnp.float32)
    quadrature_multipliers = jnp.maximum(
        0.0,
        1.0
        - jnp.abs(thermal_state_kelvin[:, None, :] - polygon_midpoints[None, :, None])
        / mesh_spacing,
    )
    basis = humidity_mixing_ratio[:, None, :] * quadrature_multipliers
    gas_depth = jnp.einsum("gb,lbn->lgn", gas_table, basis, precision=lax.Precision.HIGHEST)
    cloud_depth = cloud_ext[None, :, None] * droplet_mixing_ratio[:, None, :]
    optical = gas_depth + cloud_depth + rayleigh[None, :, None] + aero_wide
    single_albedo = (
        cloud_ssa[None, :, None] * cloud_depth + rayleigh[None, :, None] + aero_scatter
    ) / optical
    path_cosine = jnp.maximum(sun_cosine, 0.1)
    direct = jnp.exp(-optical / path_cosine[None, None, :])
    spread = 0.5 * single_albedo * (1.0 - direct)
    diffuse = jnp.exp(-1.66 * optical * (1.0 - single_albedo))
    incoming = jnp.broadcast_to(jnp.maximum(sun_cosine, 0.0)[None, :], direct.shape[1:])

    def downward(carry, layer_in):
        direct_flux, diffuse_flux = carry
        through, spread_layer, diffuse_layer = layer_in
        return (
            (direct_flux * through, diffuse_flux * diffuse_layer + direct_flux * spread_layer),
            (direct_flux, diffuse_flux),
        )

    (direct_floor, diffuse_floor), (direct_fluxes, diffuse_fluxes) = lax.scan(
        downward, (incoming, jnp.zeros_like(incoming)), (direct, spread, diffuse)
    )
    ground = albedo[None, :] * (direct_floor + diffuse_floor)

    def upward(rising, layer_in):
        direct_layer, spread_layer, diffuse_layer = layer_in
        updated = rising * diffuse_layer + direct_layer * spread_layer
        return (updated, updated)

    top_rising, risings = lax.scan(upward, ground, (direct_fluxes, spread, diffuse), reverse=True)
    net_upper = direct_fluxes + diffuse_fluxes - risings
    net_floor = direct_floor + diffuse_floor - ground
    net_lower = jnp.concatenate([net_upper[1:], net_floor[None]], axis=0)
    absorbed = net_upper - net_lower
    return (
        levels
        / band_count
        * jnp.einsum("g,lgn->ln", solar_weight, absorbed, precision=lax.Precision.HIGHEST)
    )


def radiate_blocks(
    stacked_layer_values,
    sun_cosine,
    albedo,
    aero_depth,
    aero_ssa,
    gas_table,
    cloud_ext,
    cloud_ssa,
    rayleigh,
    solar_weight,
    senders,
    slot_len,
):
    per_block = 1
    for divisor in range(1, senders + 1):
        if senders % divisor == 0 and divisor * slot_len <= 512:
            per_block = divisor
    pieces = senders // per_block
    span_cols = per_block * slot_len
    profile_blocks = jnp.transpose(
        stacked_layer_values.reshape(
            stacked_layer_values.shape[0], stacked_layer_values.shape[1], pieces, span_cols
        ),
        (2, 0, 1, 3),
    )
    aero_blocks = jnp.transpose(
        aero_depth.reshape(aero_depth.shape[0], aero_depth.shape[1], pieces, span_cols),
        (2, 0, 1, 3),
    )
    aero_ssa_blocks = jnp.transpose(
        aero_ssa.reshape(aero_ssa.shape[0], aero_ssa.shape[1], pieces, span_cols), (2, 0, 1, 3)
    )
    heating = lax.map(
        lambda operand: radiate(
            operand[0],
            operand[1],
            operand[2],
            operand[3],
            operand[4],
            gas_table,
            cloud_ext,
            cloud_ssa,
            rayleigh,
            solar_weight,
        ),
        (
            profile_blocks,
            sun_cosine.reshape(pieces, span_cols),
            albedo.reshape(pieces, span_cols),
            aero_blocks,
            aero_ssa_blocks,
        ),
    )
    return jnp.transpose(heating, (1, 0, 2)).reshape(heating.shape[1], pieces * span_cols)


def per_device(
    state,
    kappa,
    neighbours,
    parent,
    cos_zenith,
    routes,
    rad_albedo,
    aerosol_depth,
    aerosol_ssa,
    gas_table,
    cloud_ext,
    cloud_ssa,
    rayleigh,
    solar_weight,
):
    fields = state[0]
    rates = kappa[0]
    table = neighbours[0]
    lineage = parent[0]
    field_count, levels, cells = fields.shape
    slots = lax.axis_size("grp")
    domains = lax.axis_size("dom")
    senders = (slots - 1) * domains
    coarse_count = cells // 4
    blocks = routes.shape[1]
    block_len = coarse_count // blocks
    most = max(2, 2 * blocks // domains)
    slot_len = most * block_len
    is_radiation = lax.axis_index("grp") == slots - 1
    coarse = (
        jnp.zeros((field_count, levels, coarse_count), jnp.float32).at[:, :, lineage].add(fields)
        * 0.25
    )
    target = routes[0, :, 0]
    ordinal = jnp.arange(blocks, dtype=jnp.int32)
    earlier = (target[:, None] == target[None, :]) & (ordinal[None, :] < ordinal[:, None])
    arrival = jnp.sum(earlier.astype(jnp.int32), axis=1)
    placed = target * most + arrival
    packer = (placed[:, None] == jnp.arange(domains * most, dtype=jnp.int32)[None, :]).astype(
        jnp.float32
    )
    packed = jnp.einsum(
        "flbj,bs->flsj",
        coarse.reshape(field_count, levels, blocks, block_len),
        packer,
        precision=lax.Precision.HIGHEST,
    ).reshape(field_count, levels, domains, slot_len)
    sun_packed = jnp.einsum(
        "bj,bs->sj",
        cos_zenith[0].reshape(blocks, block_len),
        packer,
        precision=lax.Precision.HIGHEST,
    ).reshape(1, 1, domains, slot_len)
    empty_fields = jnp.zeros((field_count, levels, senders, slot_len), jnp.float32)
    empty_sun = jnp.zeros((1, 1, senders, slot_len), jnp.float32)
    outgoing = jnp.concatenate([empty_fields, packed], axis=2)
    outgoing_sun = jnp.concatenate([empty_sun, sun_packed], axis=2)
    arrived, arrived_sun = (
        lax.all_to_all(outgoing, ("grp", "dom"), split_axis=2, concat_axis=2, tiled=True),
        lax.all_to_all(outgoing_sun, ("grp", "dom"), split_axis=2, concat_axis=2, tiled=True),
    )
    received = arrived[:, :, :senders, :].reshape(field_count, levels, senders * slot_len)
    sun_received = arrived_sun[0, 0, :senders, :].reshape(senders * slot_len)

    def compute(operand):
        return radiate_blocks(
            operand[0],
            operand[1],
            rad_albedo[0],
            aerosol_depth[0],
            aerosol_ssa[0],
            gas_table,
            cloud_ext,
            cloud_ssa,
            rayleigh,
            solar_weight,
            senders,
            slot_len,
        )

    def nothing(operand):
        return jnp.zeros((levels, senders * slot_len), jnp.float32)

    heating = lax.cond(is_radiation, compute, nothing, (received, sun_received))
    returning = jnp.concatenate(
        [
            heating.reshape(levels, senders, slot_len),
            jnp.zeros((levels, domains, slot_len), jnp.float32),
        ],
        axis=1,
    )
    came_back = lax.all_to_all(returning, ("grp", "dom"), split_axis=1, concat_axis=1, tiled=True)
    mine = came_back[:, senders:, :]
    coarse_heating = jnp.einsum(
        "lsj,bs->lbj",
        mine.reshape(levels, domains * most, block_len),
        packer,
        precision=lax.Precision.HIGHEST,
    ).reshape(levels, coarse_count)
    fine_heating = jnp.take(coarse_heating, lineage, axis=1)
    current = fields
    for substep_no in range(2):
        extended = padded(current, (("dom", 2),), HALO)
        current = substep(current, extended, rates, table)
    warmed = jnp.concatenate([(current[0] + 0.5 * fine_heating)[None], current[1:]], axis=0)
    return jnp.where(is_radiation, jnp.zeros_like(warmed), warmed)[None]


def solution(mesh):
    return jax.shard_map(
        per_device,
        mesh=mesh,
        in_specs=(
            P("grp", None, None, "dom"),
            P("grp", "dom"),
            P("grp", None, "dom"),
            P("grp", "dom"),
            P("grp", "dom"),
            P(("grp", "dom"), None, None),
            P("grp", "dom"),
            P("grp", None, None, "dom"),
            P("grp", None, None, "dom"),
            P(),
            P(),
            P(),
            P(),
            P(),
        ),
        out_specs=P("grp", None, None, "dom"),
        check_vma=False,
    )
```

profile of v0, /device:TPU:1, one launch (start us, length us, event | category | flops | bytes accessed | tf_op | source)
XLA Modules:
  0.0 1642.9 jit_solution(16147175118173529171)
XLA Ops:
  0.0 4.5 copy.104
  4.5 0.9 fusion.40
  5.4 2.5 collective-permute-start
  7.9 4.7 collective-permute-start.1
  12.7 0.7 compare_select_fusion.1
  13.5 132.1 %scatter_fusion = f32[3,32,512]{1,0,2:T(4,128)S(1)} fusion(f32[3,32,512]{1,0,2:T(4,128)S(1)} %broadcast_in_dim.116, s32[2048]{0:T(1024)S(1)} %bitcast.228, f32[2048,3,32]{2,1,0:T(4,128)} %bitcast.205), kind=kCustom, calls=%fused_computation.3 | custom fusion | flops 196608 | bytes 2367488 | tf_op jit(solution)/shard_map/scatter-add | solution.py:189
  146.1 1.1 convolution_bitcast_fusion
  147.1 0.7 copy.106
  147.9 3.4 pad_bitcast_fusion
  151.3 6.1 reshape.255
  157.4 7.4 all-to-all-start
  164.9 0.5 broadcast.296
  165.4 0.7 reduce.7
  166.4 0.6 broadcast_clamp_fusion
  167.1 7.1 pad_maximum_fusion
  174.2 46.9 %gather_fusion.1 = f32[6144,3,32]{2,1,0:T(4,128)} fusion(f32[3,32,2112]{1,0,2:T(4,128)} %pad_maximum_fusion, s32[6144]{0:T(1024)S(1)} %fusion.29), kind=kCustom, calls=%fused_computation.clone | custom fusion | bytes 4743168 | tf_op jit(solution)/shard_map/jit(_take)/gather | solution.py:24
  221.1 24.0 %broadcast_select_fusion.1 = f32[6144,3,32]{2,1,0:T(4,128)} fusion(f32[6144,3,32]{2,1,0:T(4,128)} %gather_fusion.1, pred[6144]{0:T(1024)(128)(4,1)S(1)} %compare_and_fusion), kind=kLoop, calls=%fused_computation.68 | loop fusion | flops 589824 | bytes 4724736 | tf_op jit(solution)/shard_map/jit(_take)/select_n | solution.py:24
  245.1 11.2 reduce_sum.27
  256.3 7.7 multiply_add_fusion.3
  264.0 2.0 copy-done
  266.0 1.6 collective-permute-start.2
  267.6 4.6 collective-permute-start.3
  272.1 0.6 compare_and_fusion.1
  272.8 0.6 concatenate.41
  273.7 7.1 pad_maximum_fusion.1
  280.9 46.9 %gather_fusion.2 = f32[6144,3,32]{2,1,0:T(4,128)} fusion(f32[3,32,2112]{1,0,2:T(4,128)} %pad_maximum_fusion.1, s32[6144]{0:T(1024)S(1)} %fusion.29), kind=kCustom, calls=%fused_computation.1.clone | custom fusion | bytes 4743168 | tf_op jit(solution)/shard_map/jit(_take)/gather | solution.py:24
  327.8 27.3 %all-to-all-start.1 = ((f32[1,1,128,32]{3,1,0,2:T(1,128)}), f32[1,1,128,32]{3,1,0,2:T(1,128)S(1)}, u32[]{:S(2)}, u32[]{:S(2)}) async-start(f32[1,1,128,32]{3,1,0,2:T(1,128)} %bitcast.42), calls=%async_computation.1 | async-start | bytes 131072 | tf_op jit(solution)/shard_map/all_to_all | solution.py:218
  355.0 24.0 %broadcast_select_fusion = f32[6144,3,32]{2,1,0:T(4,128)} fusion(f32[6144,3,32]{2,1,0:T(4,128)} %gather_fusion.2, pred[6144]{0:T(1024)(128)(4,1)S(1)} %compare_and_fusion), kind=kLoop, calls=%fused_computation.67 | loop fusion | flops 589824 | bytes 4724736 | tf_op jit(solution)/shard_map/jit(_take)/select_n | solution.py:24
  379.1 11.2 reduce_sum.28
  390.3 0.6 broadcast.303
  390.9 4.4 reduce.8
  395.3 3.7 reshape.256
  399.3 0.7 copy-done.2
  400.0 1.5 reshape.191
  401.6 0.9 copy.125
  402.7 1.7 reshape.257
  404.4 1202.9 %all-to-all-start.2 = ((f32[128,1,1024]{2,1,0:T(1,128)}), f32[128,1,1024]{2,1,0:T(1,128)}, u32[]{:S(2)}, u32[]{:S(2)}) async-start(f32[128,1,1024]{2,1,0:T(1,128)} %reshape.257), calls=%async_computation.2 | async-start | bytes 1048576 | tf_op jit(solution)/shard_map/all_to_all | solution.py:250
  1607.3 7.7 multiply_add_fusion.2
  1615.0 1.9 copy-done.1
  1617.0 1.1 slice_bitcast_fusion
  1618.1 0.9 copy.117
  1618.9 1.9 all-to-all-done.2
  1620.9 3.0 reduce.9
  1623.8 0.7 reshape.258
  1624.8 0.5 convolution_bitcast_fusion.1
  1625.4 5.5 gather_fusion
  1630.9 10.4 slice_add_fusion
  1641.6 0.9 maximum_select_fusion
  (48 shorter events, 2.6 us)
Async XLA Ops:
  0.0 145.8 %copy-start.15 = (s32[1,32,1]{1,2,0:T(1,128)S(1)}, s32[1,32,1]{1,2,0:T(1,128)}, u32[]{:S(2)}) copy-start(s32[1,32,1]{1,2,0:T(1,128)} %param.29) | copy-start | bytes 388
  5.4 161.6 %collective-permute-start = (f32[3,32,32]{1,0,2:T(4,128)S(1)}, f32[3,32,32]{1,0,2:T(4,128)S(1)}, u32[]{:S(2)}, u32[]{:S(2)}) collective-permute-start(f32[3,32,32]{1,0,2:T(4,128)S(1)} %get-tuple-element.682), channel_id=1, source_target_pairs={{0,1},{1,2},{2,3},{3,4},{4,5},{5,6},{6,7},{7,8},{8,9},{9,10},{10,1... | collective-permute-start | bytes 36872 | tf_op jit(solution)/shard_map/ppermute | solution.py:15
  7.9 159.1 %collective-permute-start.1 = (f32[3,32,32]{1,0,2:T(4,128)S(1)}, f32[3,32,32]{1,0,2:T(4,128)S(1)}, u32[]{:S(2)}, u32[]{:S(2)}) collective-permute-start(f32[3,32,32]{1,0,2:T(4,128)S(1)} %get-tuple-element.683), channel_id=1, source_target_pairs={{1,0},{2,1},{3,2},{4,3},{5,4},{6,5},{7,6},{8,7},{9,8},{10,9},{11,1... | collective-permute-start | bytes 36872 | tf_op jit(solution)/shard_map/ppermute | solution.py:18
  146.0 20.1 %copy-start.12 = (s32[32]{0:T(128)}, s32[32]{0:T(128)S(1)}, u32[]{:S(2)}) copy-start(s32[32]{0:T(128)S(1)} %multiply_add_fusion.4) | copy-start | bytes 388
  151.3 13.5 copy-start.3
  151.3 14.1 copy-start.11
  157.4 170.4 %all-to-all-start = ((f32[128,1,3072]{2,1,0:T(1,128)}), f32[128,1,3072]{2,1,0:T(1,128)S(1)}, u32[]{:S(2)}, u32[]{:S(2)}) async-start(f32[128,1,3072]{2,1,0:T(1,128)} %reshape.255), calls=%async_computation | async-start | bytes 3145728 | tf_op jit(solution)/shard_map/all_to_all | solution.py:217
  245.1 11.2 copy-start.6
  256.3 15.8 copy-start.5
  264.0 2.0 copy-start
  266.0 7.7 collective-permute-start.2
  267.6 6.1 collective-permute-start.3
  327.8 71.3 %all-to-all-start.1 = ((f32[1,1,128,32]{3,1,0,2:T(1,128)}), f32[1,1,128,32]{3,1,0,2:T(1,128)S(1)}, u32[]{:S(2)}, u32[]{:S(2)}) async-start(f32[1,1,128,32]{3,1,0,2:T(1,128)} %bitcast.42), calls=%async_computation.1 | async-start | bytes 131072 | tf_op jit(solution)/shard_map/all_to_all | solution.py:218
  390.3 8.7 copy-start.9
  399.3 0.7 copy-start.2
  400.0 1207.3 %copy-start.7 = (f32[1,2048]{1,0:T(1,128)S(1)}, f32[1,2048]{1,0:T(1,128)}, u32[]{:S(2)}) copy-start(f32[1,2048]{1,0:T(1,128)} %param.25) | copy-start | bytes 24580
  404.4 1216.4 %all-to-all-start.2 = ((f32[128,1,1024]{2,1,0:T(1,128)}), f32[128,1,1024]{2,1,0:T(1,128)}, u32[]{:S(2)}, u32[]{:S(2)}) async-start(f32[128,1,1024]{2,1,0:T(1,128)} %reshape.257), calls=%async_computation.2 | async-start | bytes 1048576 | tf_op jit(solution)/shard_map/all_to_all | solution.py:250
  1615.0 1.9 copy-start.1
  1617.0 7.8 copy-start.13
  1617.0 8.4 copy-start.4
  1617.0 13.9 copy-start.10
where the time goes:
time: 1670 us; the launch traced here: 1640 us
  starting transfers between devices  1250 us (75%)
  other arithmetic  254 us (15%)
  local copies, waits for them, and re-layouts  133 us (8%)
    all_to_all x1, starting transfers between devices, per_device(): lax.all_to_all(returning, ('grp', 'dom'), split_axis=1, concat_axis=1, ti...  1200 us
    scatter-add x1, other arithmetic, per_device(): jnp.zeros((field_count, levels, coarse_count), jnp.float32)  132 us
    gather x2, local copies, waits for them, and re-layouts, substep(): near = jnp.take(extended, index.reshape(-1), axis=2)  93.8 us
    select_n x2, other arithmetic, substep(): near = jnp.take(extended, index.reshape(-1), axis=2)  48 us
  transfers between devices with their start and end apart: 7, of which 2 were waited for; matrix products, arithmetic and copies ran while one was open for 21% of the time, Pallas kernels for 0%

commit v1 on v0

v1 whole, which is shorter than its diff:
```python
import jax
import jax.numpy as jnp
from jax import lax
from jax.experimental import pallas as pl
from jax.experimental.pallas import tpu as pltpu
from jax.sharding import PartitionSpec as P

F32 = jnp.float32
BF16 = jnp.bfloat16
I32 = jnp.int32
HALO = 32
FIELDS, LEVELS, GPOINTS, BANDS, NODES = 3, 32, 112, 14, 32
ROWS = FIELDS * LEVELS
CELLS, COARSE = 2048, 512
BLOCKS, BLOCK_COLS, MOST = 32, 16, 2
DOMAINS, SLOTS = 32, 4
SLOT_COLS = BLOCK_COLS * MOST
LANES = 128
PER_TILE = LANES // SLOT_COLS
TILES = CELLS // LANES
UNIT = 256
UNIT_SENDERS = UNIT // SLOT_COLS
KEPT = 16
LEVEL_BLOCK = 8
LOG2E = 1.4426950408889634
VMEM_LIMIT = 56 * 1024 * 1024


def halves(x):
    high = x.astype(BF16)
    return high, (x - high.astype(F32)).astype(BF16)


def thirds(x):
    high = x.astype(BF16)
    rest = x - high.astype(F32)
    middle = rest.astype(BF16)
    return high, middle, (rest - middle.astype(F32)).astype(BF16)


def exact_dot(x, chosen, contract):
    rows = x.shape[0]
    stacked = jnp.concatenate(thirds(x), axis=0)
    product = lax.dot_general(
        stacked, chosen, (((1,), (contract,)), ((), ())), preferred_element_type=F32
    )
    return product[:rows] + product[rows : 2 * rows] + product[2 * rows :]


def iota(shape, dim):
    return lax.broadcasted_iota(I32, shape, dim)


def ones_where(mask):
    return jnp.where(mask, 1.0, 0.0).astype(BF16)


def regroup(pieces, shift_of):
    group = iota(pieces[0].shape, 1) // SLOT_COLS
    result = None
    for k, piece in enumerate(pieces):
        shift = (shift_of(k) % PER_TILE) * SLOT_COLS
        moved = pltpu.roll(piece, shift, 1) if shift else piece
        result = moved if result is None else jnp.where(group == k, moved, result)
    return result


def column(row):
    n = row.shape[1]
    return jnp.sum(jnp.where(iota((n, n), 0) == iota((n, n), 1), row, 0.0), axis=1, keepdims=True)


def coarsen_kernel(
    routes, state, parent, sun, kappa, near, gas, ext, ssa, ray, solar,
    message, edges, slots_out, weights, solar_out,
):
    block = iota((1, COARSE), 1) // BLOCK_COLS
    target = jnp.zeros((1, COARSE), I32)
    for b in range(BLOCKS):
        target = jnp.where(block == b, routes[0, b, 0], target)
    arrival = jnp.zeros((1, COARSE), I32)
    for b in range(BLOCKS):
        same = (target == routes[0, b, 0]) & (block > b)
        arrival = arrival + jnp.where(same, 1, 0)
    place = (target * MOST + arrival) * BLOCK_COLS + iota((1, COARSE), 1) % BLOCK_COLS
    slots_out[...] = place

    lineage = ones_where(iota((COARSE, CELLS), 0) == parent[...])
    coarse = 0.25 * exact_dot(state[...], lineage, 1)
    sun_rows = jnp.where(iota((8, COARSE), 0) == 0, sun[...], 0.0)
    columns = jnp.concatenate([coarse, sun_rows], axis=0)
    placed = ones_where(iota((DOMAINS * SLOT_COLS, COARSE), 0) == place)
    packed = exact_dot(columns, placed, 1)
    span = ROWS // PER_TILE
    for tile in range(DOMAINS // PER_TILE):
        part = packed[:, tile * LANES : (tile + 1) * LANES]
        for e in range(PER_TILE):
            pieces = [part[a * span : (a + 1) * span] for a in range(PER_TILE)]
            message[tile * PER_TILE + e, 0:span, :] = regroup(pieces, lambda a: a - e)
            moved = pltpu.roll(part[ROWS:], ((-e) % PER_TILE) * SLOT_COLS, 1) if e else part[ROWS:]
            message[tile * PER_TILE + e, span : span + 8, :] = moved

    for side, start in ((0, CELLS - LANES), (1, 0)):
        edges[side, 0:ROWS, :] = state[:, start : start + LANES]
        edges[side, ROWS : ROWS + 8, :] = jnp.concatenate(
            [
                kappa[:, start : start + LANES],
                near[:, start : start + LANES].astype(F32),
                jnp.zeros((4, LANES), F32),
            ],
            axis=0,
        )

    band = jnp.where(iota((GPOINTS, 16), 0) // 8 == iota((GPOINTS, 16), 1), 1.0, 0.0)
    spot = iota((GPOINTS, 16), 1)
    ext_col, ssa_col, ray_col = column(ext[...]), column(ssa[...]), column(ray[...])
    scatter_w = jnp.where(spot == BANDS, ray_col, jnp.where(spot == BANDS + 1, ssa_col * ext_col, 0.0))
    optical_w = jnp.where(spot == BANDS, ray_col, jnp.where(spot == BANDS + 1, ext_col, band))
    gas_hi, gas_lo = halves(gas[...])
    opt_hi, opt_lo = halves(optical_w)
    sca_hi, sca_lo = halves(scatter_w)
    none = jnp.zeros((GPOINTS, 16), F32)
    wide = jnp.zeros((GPOINTS, NODES), F32)
    upper = [gas_hi, gas_lo, gas_hi, opt_hi, opt_lo, opt_hi, none, none]
    lower = [wide, wide, wide, sca_hi, sca_lo, sca_hi, band, band]
    weights[0:GPOINTS, :] = (-jnp.concatenate([p.astype(F32) for p in upper], axis=1)).astype(BF16)
    weights[GPOINTS:, :] = jnp.concatenate([p.astype(F32) for p in lower], axis=1).astype(BF16)
    solar_out[...] = jnp.broadcast_to(column(solar[...]), (GPOINTS, LANES))


def diffuse_kernel(role, state, kappa, near, left, right, out, fields, rates, goal, chosen):
    for ref, start, width, shift in (
        (left, 0, LANES, LANES - HALO - CELLS),
        (right, LANES + CELLS, LANES, LANES - HALO + CELLS),
    ):
        fields[:, start : start + width] = ref[0:ROWS, :]
        rates[:, start : start + width] = ref[ROWS : ROWS + 1, :]
        goal[0:3, start : start + width] = ref[ROWS + 1 : ROWS + 4, :].astype(I32) + shift
    fields[:, LANES : LANES + CELLS] = state[...]
    rates[:, LANES : LANES + CELLS] = kappa[...]
    goal[0:3, LANES : LANES + CELLS] = near[...] + (LANES - HALO)
    window = 3 * LANES
    rows = iota((window, LANES), 0)

    def spread(tile):
        first = min(max(tile - 1, 0), TILES - 1)
        return first * LANES

    results = []
    for tile in range(TILES + 2):
        here = slice(tile * LANES, (tile + 1) * LANES)
        place = rows + spread(tile)
        count = jnp.zeros((window, LANES), F32)
        for n in range(3):
            count = count + jnp.where(place == goal[n : n + 1, here], 1.0, 0.0)
        picked = count.astype(BF16)
        chosen[tile] = picked
        own = fields[:, here]
        total = exact_dot(fields[:, spread(tile) : spread(tile) + window], picked, 0)
        results.append(own + rates[:, here] * (total - 3.0 * own))
    for tile, value in enumerate(results):
        fields[:, tile * LANES : (tile + 1) * LANES] = value
    dynamic = role[0] != SLOTS - 1
    for tile in range(1, TILES + 1):
        here = slice(tile * LANES, (tile + 1) * LANES)
        own = fields[:, here]
        total = exact_dot(fields[:, spread(tile) : spread(tile) + window], chosen[tile], 0)
        value = own + rates[:, here] * (total - 3.0 * own)
        out[:, (tile - 1) * LANES : tile * LANES] = jnp.where(dynamic, value, 0.0)


def radiation_kernel(
    role, weights, solar, received, from_first, from_second, depth, ssa, albedo,
    aero_two, aero_first, aero_second, out,
    profile, columns, aero, optics, scatter_q, decay, beam, glow, net, sems,
):
    step = pl.program_id(0)
    steps = pl.num_programs(0)
    is_first, is_second, is_third, is_last = (role[0] == k for k in range(4))
    kept = KEPT // UNIT_SENDERS
    active = (step < kept) | is_third | is_last

    def copies(unit, slot):
        lanes = pl.ds(pl.multiple_of(unit * UNIT, UNIT), UNIT)
        begin = jnp.where(unit < kept, KEPT * SLOT_COLS, 2 * KEPT * SLOT_COLS)
        own = pl.ds(pl.multiple_of(begin + unit * UNIT, UNIT), UNIT)
        target = aero.at[slot]
        return (
            (is_first, [pltpu.make_async_copy(aero_first.at[:, :, lanes], target, sems.at[slot, 0])]),
            (is_second, [pltpu.make_async_copy(aero_second.at[:, :, lanes], target, sems.at[slot, 0])]),
            (is_third, [pltpu.make_async_copy(aero_two.at[:, :, lanes], target, sems.at[slot, 0])]),
            (
                is_last,
                [
                    pltpu.make_async_copy(
                        depth.at[0, :, :, own], target.at[pl.ds(0, LEVELS)], sems.at[slot, 0]
                    ),
                    pltpu.make_async_copy(
                        ssa.at[0, :, :, own], target.at[pl.ds(LEVELS, LEVELS)], sems.at[slot, 1]
                    ),
                    pltpu.make_async_copy(
                        albedo.at[:, own], target.at[2 * LEVELS, pl.ds(0, 1)], sems.at[slot, 2]
                    ),
                ],
            ),
        )

    def has(unit):
        return (unit < kept) | is_third | is_last

    def begin(unit, slot):
        for chosen, descriptors in copies(unit, slot):
            @pl.when(chosen & has(unit))
            def _():
                for descriptor in descriptors:
                    descriptor.start()

    slot = step % 2

    @pl.when(step == 0)
    def _():
        begin(step, slot)

    @pl.when(step + 1 < steps)
    def _():
        begin(step + 1, 1 - slot)

    for chosen, ref in (
        (~is_last, received),
        (is_last & (step < kept), from_first),
        (is_last & (step >= kept), from_second),
    ):
        @pl.when(chosen)
        def _():
            profile[...] = ref[...]

    @pl.when(jnp.logical_not(active))
    def _():
        out[...] = jnp.zeros_like(out)

    @pl.when(active)
    def _():
        span = ROWS // PER_TILE
        for tile in range(UNIT // LANES):
            lanes = slice(tile * LANES, (tile + 1) * LANES)
            parts = [profile[tile * PER_TILE + e] for e in range(PER_TILE)]
            for a in range(PER_TILE):
                pieces = [part[0:span] for part in parts]
                columns[a * span : (a + 1) * span, lanes] = regroup(pieces, lambda e: e - a)
            pieces = [part[span : span + 8] for part in parts]
            columns[ROWS : ROWS + 8, lanes] = regroup(pieces, lambda e: e)
        for chosen, descriptors in copies(step, slot):
            @pl.when(chosen)
            def _():
                for descriptor in descriptors:
                    descriptor.wait()
        radiate(weights, solar, columns, aero, slot, optics, scatter_q, decay, beam, glow, net)
        heat = (net[0:LEVELS] - net[1 : LEVELS + 1]).sum(axis=1) * (LEVELS / GPOINTS)
        span = LEVELS // PER_TILE
        for tile in range(UNIT // LANES):
            part = heat[:, tile * LANES : (tile + 1) * LANES]
            for e in range(PER_TILE):
                pieces = [part[a * span : (a + 1) * span] for a in range(PER_TILE)]
                out[tile * PER_TILE + e] = regroup(pieces, lambda a: a - e)


def radiate(weights, solar, columns, aero, slot, optics, scatter_q, decay, beam, glow, net):
    cosine = columns[ROWS : ROWS + 1, :]
    path = jnp.maximum(cosine, 0.1)
    scale = LOG2E / path
    beam[...] = solar[:, 0:1] * (0.5 * jnp.maximum(cosine, 0.0))
    glow[...] = jnp.zeros_like(glow)
    node = iota((NODES, UNIT), 0).astype(F32)
    half = GPOINTS // 2

    def down(block, _):
        first = block * LEVEL_BLOCK
        for j in range(LEVEL_BLOCK):
            level = first + j
            warmth = (columns[pl.ds(level, 1), :] + 4.0) * ((NODES - 1) / 8.0)
            vapour = columns[pl.ds(level + LEVELS, 1), :] * scale
            cloud = columns[pl.ds(level + 2 * LEVELS, 1), :] * scale
            hat = jnp.maximum(0.0, 1.0 - jnp.abs(warmth - node)) * vapour
            depth = aero[slot, level] * scale
            share = depth * aero[slot, level + LEVELS]
            hat_hi, hat_lo = halves(hat)
            opt_hi, opt_lo = halves(jnp.concatenate([depth, scale, cloud], axis=0))
            sca_hi, sca_lo = halves(jnp.concatenate([share, jnp.zeros((2, UNIT), F32)], axis=0))
            stacked = jnp.concatenate(
                [hat_hi, hat_hi, hat_lo, opt_hi, opt_hi, opt_lo, sca_hi, sca_lo], axis=0
            )
            optics[j] = jnp.dot(weights[...], stacked, preferred_element_type=F32)
        for lane in range(0, UNIT, LANES):
            lanes = slice(lane, lane + LANES)
            back = jnp.broadcast_to(1.66 * path[:, lanes], (half, LANES))
            for row in range(0, GPOINTS, half):
                rows = slice(row, row + half)
                straight = beam[rows, lanes]
                spread = glow[rows, lanes]
                for j in range(LEVEL_BLOCK):
                    loss = optics[j, rows, lanes]
                    part = optics[j, GPOINTS + row : GPOINTS + row + half, lanes]
                    through = straight * jnp.exp2(loss)
                    kept = jnp.exp2(back * (loss + part))
                    source = (through - straight) * (part * pl.reciprocal(loss, approx=True))
                    scatter_q[first + j, rows, lanes] = source
                    decay[first + j, rows, lanes] = kept
                    total = (straight + straight + spread).reshape(half // 8, 8, LANES).sum(axis=0)
                    if row == 0:
                        net[first + j, :, lanes] = total
                    else:
                        net[first + j, :, lanes] += total
                    spread = spread * kept + source
                    straight = through
                beam[rows, lanes] = straight
                glow[rows, lanes] = spread
        return 0

    lax.fori_loop(0, LEVELS // LEVEL_BLOCK, down, 0)
    ground = aero[slot, 2 * LEVELS, 0:1, :]
    for lane in range(0, UNIT, LANES):
        lanes = slice(lane, lane + LANES)
        floor = 2.0 * beam[:, lanes] + glow[:, lanes]
        rising = ground[:, lanes] * floor
        net[LEVELS, :, lanes] = (floor - rising).reshape(GPOINTS // 8, 8, LANES).sum(axis=0)

        def up(i, rising):
            for k in range(4):
                level = LEVELS - 1 - (i * 4 + k)
                rising = rising * decay[level, :, lanes] + scatter_q[level, :, lanes]
                net[level, :, lanes] -= rising.reshape(GPOINTS // 8, 8, LANES).sum(axis=0)
            return rising

        lax.fori_loop(0, LEVELS // 4, up, rising)


def warm_kernel(role, mine, parent, slots_in, stepped, out):
    span = LEVELS // PER_TILE
    tiles = []
    for tile in range(DOMAINS // PER_TILE):
        parts = [mine[tile * PER_TILE + e] for e in range(PER_TILE)]
        tiles.append(
            jnp.concatenate([regroup(parts, lambda e: e - a) for a in range(PER_TILE)], axis=0)
        )
    heat = jnp.concatenate(tiles, axis=1)
    placed = ones_where(iota((DOMAINS * SLOT_COLS, COARSE), 0) == slots_in[...])
    coarse = exact_dot(heat, placed, 0)
    lineage = ones_where(iota((COARSE, CELLS), 0) == parent[...])
    fine = exact_dot(coarse, lineage, 0)
    out[...] = jnp.where(role[0] != SLOTS - 1, stepped[...] + 0.5 * fine, 0.0)


def params():
    return pltpu.CompilerParams(vmem_limit_bytes=VMEM_LIMIT)


SMEM = pl.BlockSpec(memory_space=pltpu.SMEM)
VMEM = pl.BlockSpec(memory_space=pltpu.VMEM)
HBM = pl.BlockSpec(memory_space=pl.ANY)


def per_device(
    state, kappa, neighbours, parent, cos_zenith, routes, rad_albedo, aerosol_depth, aerosol_ssa,
    gas_table, cloud_ext, cloud_ssa, rayleigh, solar_weight,
):
    fields = state.reshape(ROWS, CELLS)
    near = neighbours[0]
    slot = lax.axis_index("grp").astype(I32).reshape(1)
    last = SLOTS - 1

    def aerosol(begin, count):
        cut = slice(begin, begin + count)
        ground = jnp.broadcast_to(rad_albedo[0, cut], (1, BANDS, count))
        return jnp.concatenate(
            [aerosol_depth[0, :, :, cut], aerosol_ssa[0, :, :, cut], ground], axis=0
        )

    slot_span = DOMAINS * SLOT_COLS
    kept_cols = KEPT * SLOT_COLS
    aero_first = lax.ppermute(aerosol(0, kept_cols), "grp", [(last, 0)])
    aero_second = lax.ppermute(aerosol(slot_span, kept_cols), "grp", [(last, 1)])
    aero_two = lax.ppermute(aerosol(2 * slot_span, slot_span), "grp", [(last, 2)])

    message, edges, places, weights, solar = pl.pallas_call(
        coarsen_kernel,
        in_specs=[SMEM] + [VMEM] * 10,
        out_specs=[VMEM] * 5,
        out_shape=[
            jax.ShapeDtypeStruct((DOMAINS, 32, LANES), F32),
            jax.ShapeDtypeStruct((2, ROWS + 8, LANES), F32),
            jax.ShapeDtypeStruct((1, COARSE), I32),
            jax.ShapeDtypeStruct((2 * GPOINTS, 176), BF16),
            jax.ShapeDtypeStruct((GPOINTS, LANES), F32),
        ],
        compiler_params=params(),
        name="coarsen",
    )(
        routes, fields, parent, cos_zenith, kappa, near, gas_table, cloud_ext[None],
        cloud_ssa[None], rayleigh[None], solar_weight[None],
    )

    forward = [(i, (i + 1) % DOMAINS) for i in range(DOMAINS)]
    backward = [(target, source) for source, target in forward]
    left = lax.ppermute(edges[0], "dom", forward)
    right = lax.ppermute(edges[1], "dom", backward)
    received = lax.all_to_all(message, "dom", 0, 0, tiled=True)
    beyond = received[KEPT:]
    from_first = lax.ppermute(beyond, "grp", [(0, last)])
    from_second = lax.ppermute(beyond, "grp", [(1, last)])

    extended = CELLS + 2 * LANES
    stepped = pl.pallas_call(
        diffuse_kernel,
        in_specs=[SMEM] + [VMEM] * 5,
        out_specs=VMEM,
        out_shape=jax.ShapeDtypeStruct((ROWS, CELLS), F32),
        scratch_shapes=[
            pltpu.VMEM((ROWS, extended), F32),
            pltpu.VMEM((1, extended), F32),
            pltpu.VMEM((8, extended), I32),
            pltpu.VMEM((TILES + 2, 3 * LANES, LANES), BF16),
        ],
        compiler_params=params(),
        name="diffuse",
    )(slot, fields, kappa, near, left, right)

    units = DOMAINS // UNIT_SENDERS
    kept = KEPT // UNIT_SENDERS
    prof_block = (UNIT_SENDERS, 32, LANES)

    def own_block(i, role):
        return (jnp.where(role[0] == last, 0, jnp.where(role[0] < 2, jnp.minimum(i, kept - 1), i)), 0, 0)

    def first_block(i, role):
        return (jnp.where(role[0] == last, jnp.minimum(i, kept - 1), 0), 0, 0)

    def second_block(i, role):
        return (jnp.where(role[0] == last, jnp.maximum(i - kept, 0), 0), 0, 0)

    heat = pl.pallas_call(
        radiation_kernel,
        grid_spec=pltpu.PrefetchScalarGridSpec(
            num_scalar_prefetch=1,
            grid=(units,),
            in_specs=[
                pl.BlockSpec((2 * GPOINTS, 176), lambda i, role: (0, 0)),
                pl.BlockSpec((GPOINTS, LANES), lambda i, role: (0, 0)),
                pl.BlockSpec(prof_block, own_block),
                pl.BlockSpec(prof_block, first_block),
                pl.BlockSpec(prof_block, second_block),
                HBM, HBM, HBM, HBM, HBM, HBM,
            ],
            out_specs=pl.BlockSpec((UNIT_SENDERS, 8, LANES), lambda i, role: (i, 0, 0)),
            scratch_shapes=[
                pltpu.VMEM(prof_block, F32),
                pltpu.VMEM((ROWS + 8, UNIT), F32),
                pltpu.VMEM((2, 2 * LEVELS + 1, BANDS, UNIT), F32),
                pltpu.VMEM((LEVEL_BLOCK, 2 * GPOINTS, UNIT), F32),
                pltpu.VMEM((LEVELS, GPOINTS, UNIT), F32),
                pltpu.VMEM((LEVELS, GPOINTS, UNIT), F32),
                pltpu.VMEM((GPOINTS, UNIT), F32),
                pltpu.VMEM((GPOINTS, UNIT), F32),
                pltpu.VMEM((LEVELS + 1, 8, UNIT), F32),
                pltpu.SemaphoreType.DMA((2, 3)),
            ],
        ),
        out_shape=jax.ShapeDtypeStruct((DOMAINS, 8, LANES), F32),
        compiler_params=params(),
        name="radiation",
    )(
        slot, weights, solar, received, from_first, from_second, aerosol_depth, aerosol_ssa,
        rad_albedo, aero_two, aero_first, aero_second,
    )

    to_first = lax.ppermute(heat[:KEPT], "grp", [(last, 0)])
    to_second = lax.ppermute(heat[KEPT:], "grp", [(last, 1)])
    returning = jnp.concatenate([heat[:KEPT], heat[KEPT:] + (to_first + to_second)], axis=0)
    mine = lax.all_to_all(returning, "dom", 0, 0, tiled=True)

    warmed = pl.pallas_call(
        warm_kernel,
        grid=(1,),
        in_specs=[
            SMEM,
            pl.BlockSpec((DOMAINS, 8, LANES), lambda i: (0, 0, 0)),
            pl.BlockSpec((1, CELLS), lambda i: (0, 0)),
            pl.BlockSpec((1, COARSE), lambda i: (0, 0)),
            pl.BlockSpec((LEVELS, CELLS), lambda i: (0, 0)),
        ],
        out_specs=pl.BlockSpec((LEVELS, CELLS), lambda i: (0, 0)),
        out_shape=jax.ShapeDtypeStruct((ROWS, CELLS), F32),
        input_output_aliases={4: 0},
        compiler_params=params(),
        name="warm",
    )(slot, mine, parent, places, stepped)
    return warmed.reshape(1, FIELDS, LEVELS, CELLS)


def solution(mesh):
    return jax.shard_map(
        per_device,
        mesh=mesh,
        in_specs=(
            P("grp", None, None, "dom"),
            P("grp", "dom"),
            P("grp", None, "dom"),
            P("grp", "dom"),
            P("grp", "dom"),
            P(("grp", "dom"), None, None),
            P("grp", "dom"),
            P("grp", None, None, "dom"),
            P("grp", None, None, "dom"),
            P(),
            P(),
            P(),
            P(),
            P(),
        ),
        out_specs=P("grp", None, None, "dom"),
        check_vma=False,
    )
```

time: 1670 us -> 155 us (0.09); the launches traced: 1640 us -> 154 us
  starting transfers between devices: 1250 us -> 53.7 us
  other arithmetic: 254 us -> 5.56 us
  local copies, waits for them, and re-layouts: 133 us -> 39.3 us
  Pallas kernels: 0 us -> 22.8 us
  blocking collectives: 0 us -> 19.9 us
    all_to_all x3 -> x1, starting transfers between devices: 1240 us -> 7.04 us  [per_device(): mine = lax.all_to_all(returning, 'dom', 0, 0, tiled=True)]
    scatter-add x1 -> x0, other arithmetic: 132 us -> none  [per_device(): jnp.zeros((field_count, levels, coarse_count), jnp.float32)]
    gather x3 -> x0, local copies, waits for them, and re-layouts: 99.3 us -> none  [the longest x2 93.8 us: substep(): near = jnp.take(extended, index.reshape(-1), axis=2)]
    select_n x4 -> x0, other arithmetic: 49.7 us -> none  [the longest x2 48 us: substep(): near = jnp.take(extended, index.reshape(-1), axis=2)]
    ppermute x4 -> x9, starting transfers between devices: 13.4 us -> 46.7 us  [the longest x1 32.1 us: per_device(): from_second = lax.ppermute(beyond, 'grp', [(1, last)])]
    add x4 -> x1, other arithmetic: 25.8 us -> 0.86 us  [per_device(): heat[KEPT:] + (to_first + to_second)]
    pallas_call x0 -> x4, Pallas kernels: none -> 22.8 us  [the longest x1 11.5 us: per_device(): pl.pallas_call(radiation_kernel, grid_spec=pltpu.PrefetchScalarGridSpec(n...]
    reduce_sum x3 -> x0, other arithmetic: 22.6 us -> none  [the longest x2 22.4 us: substep(): return fields + rates * (jnp.sum(near, axis=2) - 3.0 * fields)]
  transfers between devices with their start and end apart: 7 -> 10, of which waited for: 2 -> 2; matrix products, arithmetic and copies ran while one was open for 21% -> 23% of each run, Pallas kernels for 0% -> 6%
where the time goes in v1:
time: 155 us; the launch traced here: 154 us
  starting transfers between devices  53.7 us (35%)
  local copies, waits for them, and re-layouts  39.3 us (25%)
  Pallas kernels  22.8 us (15%)
  blocking collectives  19.9 us (13%)
  waiting for transfers between devices  12.6 us (8%)
  other arithmetic  5.56 us (4%)
    ppermute x1, starting transfers between devices, per_device(): from_second = lax.ppermute(beyond, 'grp', [(1, last)])  32.1 us
    all_to_all x1, blocking collectives, per_device(): received = lax.all_to_all(message, 'dom', 0, 0, tiled=True)  19.9 us
    unnamed x31, local copies, waits for them, and re-layouts  19.1 us
    pallas_call x1, Pallas kernels, per_device(): pl.pallas_call(radiation_kernel, grid_spec=pltpu.PrefetchScalarGridSpec(n...  11.5 us
    ppermute x1, waiting for transfers between devices, per_device(): to_second = lax.ppermute(heat[KEPT:], 'grp', [(last, 1)])  9.04 us
    all_to_all x1, starting transfers between devices, per_device(): mine = lax.all_to_all(returning, 'dom', 0, 0, tiled=True)  7.04 us
    ppermute x1, local copies, waits for them, and re-layouts, per_device(): lax.ppermute(aerosol(2 * slot_span, slot_span), 'grp', [(last, 2)])  6.3 us
    pallas_call x1, Pallas kernels, per_device(): pl.pallas_call(diffuse_kernel, in_specs=[SMEM] + [VMEM] * 5, out_specs=VM...  4.97 us
  transfers between devices with their start and end apart: 10, of which 2 were waited for; matrix products, arithmetic and copies ran while one was open for 23% of the time, Pallas kernels for 6%

profile of v1, /device:TPU:1, one launch (start us, length us, event | category | flops | bytes accessed | tf_op | source)
XLA Modules:
  0.0 154.1 jit_solution(7310996750468411197)
XLA Ops:
  0.0 2.3 %slice_bitcast_fusion = (f32[32,14,1024]{2,0,1:T(8,128)S(1)}, f32[32,14,1024]{2,0,1:T(8,128)S(1)}) fusion(f32[1,32,14,3072]{3,1,2,0:T(8,128)} %param.22, f32[1,32,14,3072]{3,1,2,0:T(8,128)} %param.21), kind=kLoop, calls=%fused_computation.3 | loop fusion | bytes 7340032 | tf_op jit(solution)/shard_map/squeeze | solution.py:375
  2.4 0.0 copy-start.7
  2.4 2.2 %pad_maximum_fusion = f32[65,14,1024]{2,0,1:T(8,128)} fusion(f32[1,14,1024]{2,0,1:T(1,128)S(1)} %broadcast_in_dim.25, f32[32,14,1024]{2,0,1:T(8,128)S(1)} %get-tuple-element.25, f32[32,14,1024]{2,0,1:T(8,128)S(1)} %get-tuple-element.26), kind=kLoop, calls=%fused_computation | loop fusion | flops 1863680 | bytes 7454720 | tf_op jit(solution)/shard_map/concatenate | solution.py:374
  4.6 2.6 %collective-permute-start.2 = (f32[65,14,1024]{2,0,1:T(8,128)}, f32[65,14,1024]{2,0,1:T(8,128)}, u32[]{:S(2)}, u32[]{:S(2)}) collective-permute-start(f32[65,14,1024]{2,0,1:T(8,128)} %pad_maximum_fusion), channel_id=1, source_target_pairs={{96,64},{97,65},{98,66},{99,67},{100,68},{101,69},{102,70},{103,71... | collective-permute-start | bytes 11182088 | tf_op jit(solution)/shard_map/ppermute | solution.py:382
  7.2 2.4 %slice_bitcast_fusion.2 = (f32[32,14,512]{2,0,1:T(8,128)S(1)}, f32[32,14,512]{2,0,1:T(8,128)S(1)}, f32[32,14,512]{2,0,1:T(8,128)S(1)}, f32[32,14,512]{2,0,1:T(8,128)S(1)}) fusion(f32[1,32,14,3072]{3,1,2,0:T(8,128)} %param.22, f32[1,32,14,3072]{3,1,2,0:T(8,128)} %param.21), kind=kLoop, calls=%fused_computation.5 | loop fusion | bytes 7340032 | tf_op jit(solution)/shard_map/squeeze | solution.py:375
  9.7 0.2 pad_maximum_fusion.1
  9.9 0.0 copy-start.8
  9.9 0.0 copy-start.9
  10.0 0.0 copy-start.10
  10.0 2.2 %collective-permute-start.3 = (f32[65,14,512]{2,0,1:T(8,128)S(1)}, f32[65,14,512]{2,0,1:T(8,128)}, u32[]{:S(2)}, u32[]{:S(2)}) collective-permute-start(f32[65,14,512]{2,0,1:T(8,128)S(1)} %pad_maximum_fusion.1), channel_id=1, source_target_pairs={{96,0},{97,1},{98,2},{99,3},{100,4},{101,5},{102,6},{103,7},{104,8... | collective-permute-start | bytes 5591048 | tf_op jit(solution)/shard_map/ppermute | solution.py:380
  12.2 1.6 %pad_maximum_fusion.2 = f32[65,14,512]{2,0,1:T(8,128)} fusion(f32[1,14,512]{2,0,1:T(1,128)S(1)} %broadcast_in_dim.27, f32[32,14,512]{2,0,1:T(8,128)S(1)} %get-tuple-element.17, f32[32,14,512]{2,0,1:T(8,128)S(1)} %get-tuple-element.28), kind=kLoop, calls=%fused_computation.2 | loop fusion | flops 931840 | bytes 3727360 | tf_op jit(solution)/shard_map/concatenate | solution.py:374
  13.8 1.3 collective-permute-start.4
  15.1 0.6 copy.35
  15.7 0.7 copy.27.gas
  16.4 0.7 copy.26.routes
  17.1 3.6 %coarsen.1 = (f32[32,32,128]{2,1,0:T(8,128)}, f32[2,104,128]{2,1,0:T(8,128)}, s32[1,512]{1,0:T(1,128)}, bf16[224,176]{1,0:T(8,128)(2,1)}, f32[112,128]{1,0:T(8,128)}) custom-call(s32[1,32,1]{2,1,0:T(8,128)} %copy.26.routes, f32[96,2048]{1,0:T(8,128)} %bitcast.31, s32[1,2048]{1,0:T(1,128)} %parent.3, f32[1,512]{1,0:T(1,128)} %sun.1, f32[1,2048]{1,0:T(1,128)} %kappa.3, ...), custom_call_target="tpu_custom_call" | custom-call | tf_op jit(solution)/shard_map/coarsen/pallas_call | solution.py:384
  20.7 19.9 %all_to_all.10.received = f32[32,32,128]{2,1,0:T(8,128)S(1)} all-to-all(f32[32,32,128]{2,1,0:T(8,128)} %get-tuple-element.12), channel_id=1, replica_groups=mesh['grp'=4,'dom'=32] {'dom'}, dimensions={0} | all-to-all | bytes 1048576 | tf_op jit(solution)/shard_map/all_to_all | solution.py:406
  40.6 0.8 collective-permute-start
  41.5 32.1 %collective-permute-start.1 = (f32[16,32,128]{2,1,0:T(8,128)S(1)}, f32[16,32,128]{2,1,0:T(8,128)S(1)}, u32[]{:S(2)}, u32[]{:S(2)}) collective-permute-start(f32[16,32,128]{2,1,0:T(8,128)S(1)} %slice.58), channel_id=1, source_target_pairs={{32,96},{33,97},{34,98},{35,99},{36,100},{37,101},{38,102},{39,103... | collective-permute-start | bytes 786440 | tf_op jit(solution)/shard_map/ppermute | solution.py:409
  73.6 0.0 slice-start.1
  73.6 8.5 %copy.28.depth = f32[1,32,14,3072]{3,2,1,0:T(8,128)} copy(f32[1,32,14,3072]{3,1,2,0:T(8,128)} %param.21) | data formatting | bytes 11010048 | tf_op args[7]
  82.1 5.9 %copy.29.ssa = f32[1,32,14,3072]{3,2,1,0:T(8,128)} copy(f32[1,32,14,3072]{3,1,2,0:T(8,128)S(1)} %bitcast.30) | data formatting | bytes 11010048 | tf_op args[8]
  88.0 0.0 collective-permute-done.3
  88.0 4.1 %copy.31.aero_first = f32[65,14,512]{2,1,0:T(8,128)} copy(f32[65,14,512]{2,0,1:T(8,128)} %collective-permute-done.3) | data formatting | bytes 3727360 | tf_op jit(solution)/shard_map/ppermute | solution.py:380
  92.1 0.0 collective-permute-done.4
  92.1 4.1 %copy.32.aero_second = f32[65,14,512]{2,1,0:T(8,128)} copy(f32[65,14,512]{2,0,1:T(8,128)} %collective-permute-done.4) | data formatting | bytes 3727360 | tf_op jit(solution)/shard_map/ppermute | solution.py:381
  96.1 0.0 collective-permute-done.2
  96.1 6.3 %copy.30.aero_two = f32[65,14,1024]{2,1,0:T(8,128)} copy(f32[65,14,1024]{2,0,1:T(8,128)} %collective-permute-done.2) | data formatting | bytes 7454720 | tf_op jit(solution)/shard_map/ppermute | solution.py:382
  102.4 0.0 collective-permute-done.from_first
  102.5 0.7 copy-done.2
  103.1 0.1 copy-done.3
  103.2 11.5 %radiation.1 = f32[32,8,128]{2,1,0:T(8,128)} custom-call(s32[1]{0:T(128)} %bitcast.role, bf16[224,176]{1,0:T(8,128)(2,1)} %get-tuple-element.10.weights, f32[112,128]{1,0:T(8,128)} %get-tuple-element.11.solar, f32[32,32,128]{2,1,0:T(8,128)} %copy-done, f32[16,32,128]{2,1,0:T(8,128)} %copy-done.2, f32[16,32,128]{2,1,0:T(8,128)} %copy-done.3, ...), custom_call_target="tpu_custom_call" | custom-call | tf_op jit(solution)/shard_map/radiation/pallas_call | solution.py:440
  114.7 0.9 fusion
  115.6 0.7 collective-permute-start.5
  116.3 1.3 collective-permute-start.6
  117.6 9.0 %collective-permute-done.6 = f32[16,8,128]{2,1,0:T(8,128)S(1)} collective-permute-done((f32[16,8,128]{2,1,0:T(8,128)S(1)}, f32[16,8,128]{2,1,0:T(8,128)S(1)}, u32[]{:S(2)}, u32[]{:S(2)}) %collective-permute-start.6) | collective-permute-done | bytes 65568 | tf_op jit(solution)/shard_map/ppermute | solution.py:476
  126.7 0.9 add_add_fusion
  127.5 0.7 pad_maximum_fusion.3
  128.2 7.0 %all-to-all-start.1 = ((f32[32,8,128]{2,1,0:T(8,128)}), f32[32,8,128]{2,1,0:T(8,128)S(1)}, u32[]{:S(2)}, u32[]{:S(2)}) async-start(f32[32,8,128]{2,1,0:T(8,128)} %pad_maximum_fusion.3), calls=%async_computation.1 | async-start | bytes 262144 | tf_op jit(solution)/shard_map/all_to_all | solution.py:478
  135.2 1.3 collective-permute-start.7
  136.5 4.5 %collective-permute-start.8 = (f32[104,128]{1,0:T(8,128)S(1)}, f32[104,128]{1,0:T(8,128)S(1)}, u32[]{:S(2)}, u32[]{:S(2)}) collective-permute-start(f32[104,128]{1,0:T(8,128)S(1)} %get-tuple-element.21), channel_id=1, source_target_pairs={{1,0},{2,1},{3,2},{4,3},{5,4},{6,5},{7,6},{8,7},{9,8},{10,9},{11,1... | collective-permute-start | bytes 159752 | tf_op jit(solution)/shard_map/ppermute | solution.py:405
  141.0 3.5 %collective-permute-done.7.left = f32[104,128]{1,0:T(8,128)S(1)} collective-permute-done((f32[104,128]{1,0:T(8,128)S(1)}, f32[104,128]{1,0:T(8,128)S(1)}, u32[]{:S(2)}, u32[]{:S(2)}) %collective-permute-start.7) | collective-permute-done | bytes 53280 | tf_op jit(solution)/shard_map/ppermute | solution.py:404
  144.5 0.0 collective-permute-done.8.right
  144.5 0.6 copy-done.5
  145.1 0.6 copy-done.6
  145.8 5.0 %diffuse.1.stepped = f32[96,2048]{1,0:T(8,128)} custom-call(s32[1]{0:T(128)} %bitcast.role, f32[96,2048]{1,0:T(8,128)} %bitcast.32, f32[1,2048]{1,0:T(1,128)} %kappa.3, s32[3,2048]{1,0:T(4,128)} %bitcast.34, f32[104,128]{1,0:T(8,128)} %copy-done.5, f32[104,128]{1,0:T(8,128)} %copy-done.6), custom_call_target="tpu_custom_call" | custom-call | tf_op jit(solution)/shard_map/diffuse/pallas_call | solution.py:412
  150.7 0.7 copy-done.1
  151.4 2.7 %warm.1 = f32[96,2048]{1,0:T(8,128)} custom-call(s32[1]{0:T(128)} %bitcast.role, f32[32,8,128]{2,1,0:T(8,128)} %copy-done.1, s32[1,2048]{1,0:T(1,128)} %parent.3, s32[1,512]{1,0:T(1,128)} %get-tuple-element.13.slots_in, f32[96,2048]{1,0:T(8,128)} %diffuse.1.stepped), custom_call_target="tpu_custom_call", output_to_operand_aliasing={{}: (4, {})} | custom-call | tf_op jit(solution)/shard_map/warm/pallas_call | solution.py:480
  (28 shorter events, 0.1 us)
Async XLA Ops:
  0.0 2.3 %slice-start.2 = ((f32[1,3072]{1,0:T(1,128)}), f32[1,1024]{1,0:T(1,128)S(1)}, s32[]{:S(2)}) async-start(f32[1,3072]{1,0:T(1,128)} %albedo.1), calls=%async_computation.4 | async-start | bytes 8192 | tf_op jit(solution)/shard_map/slice | solution.py:373
  2.4 4.9 %copy-start.7 = (f32[1,3072]{1,0:T(1,128)S(1)}, f32[1,3072]{1,0:T(1,128)}, u32[]{:S(2)}) copy-start(f32[1,3072]{1,0:T(1,128)} %albedo.1) | copy-start | bytes 36868
  4.6 91.5 %collective-permute-start.2 = (f32[65,14,1024]{2,0,1:T(8,128)}, f32[65,14,1024]{2,0,1:T(8,128)}, u32[]{:S(2)}, u32[]{:S(2)}) collective-permute-start(f32[65,14,1024]{2,0,1:T(8,128)} %pad_maximum_fusion), channel_id=1, source_target_pairs={{96,64},{97,65},{98,66},{99,67},{100,68},{101,69},{102,70},{103,71... | collective-permute-start | bytes 11182088 | tf_op jit(solution)/shard_map/ppermute | solution.py:382
  9.9 5.1 %copy-start.8 = (s32[1,3,2048]{2,0,1:T(1,128)S(1)}, s32[1,3,2048]{2,0,1:T(1,128)}, u32[]{:S(2)}) copy-start(s32[1,3,2048]{2,0,1:T(1,128)} %param.16) | copy-start | bytes 73732
  9.9 5.7 %copy-start.9 = (f32[112,32]{0,1:T(8,128)S(1)}, f32[112,32]{0,1:T(8,128)}, u32[]{:S(2)}) copy-start(f32[112,32]{0,1:T(8,128)} %param.23) | copy-start | bytes 43012
  10.0 6.4 %copy-start.10 = (s32[1,32,1]{1,2,0:T(1,128)S(1)}, s32[1,32,1]{1,2,0:T(1,128)}, u32[]{:S(2)}) copy-start(s32[1,32,1]{1,2,0:T(1,128)} %param.19) | copy-start | bytes 388
  10.0 78.0 %collective-permute-start.3 = (f32[65,14,512]{2,0,1:T(8,128)S(1)}, f32[65,14,512]{2,0,1:T(8,128)}, u32[]{:S(2)}, u32[]{:S(2)}) collective-permute-start(f32[65,14,512]{2,0,1:T(8,128)S(1)} %pad_maximum_fusion.1), channel_id=1, source_target_pairs={{96,0},{97,1},{98,2},{99,3},{100,4},{101,5},{102,6},{103,7},{104,8... | collective-permute-start | bytes 5591048 | tf_op jit(solution)/shard_map/ppermute | solution.py:380
  13.8 78.3 %collective-permute-start.4 = (f32[65,14,512]{2,0,1:T(8,128)}, f32[65,14,512]{2,0,1:T(8,128)}, u32[]{:S(2)}, u32[]{:S(2)}) collective-permute-start(f32[65,14,512]{2,0,1:T(8,128)} %pad_maximum_fusion.2), channel_id=1, source_target_pairs={{96,32},{97,33},{98,34},{99,35},{100,36},{101,37},{102,38},{103,39... | collective-permute-start | bytes 5591048 | tf_op jit(solution)/shard_map/ppermute | solution.py:381
  40.6 41.5 %copy-start = (f32[32,32,128]{2,1,0:T(8,128)}, f32[32,32,128]{2,1,0:T(8,128)S(1)}, u32[]{:S(2)}) copy-start(f32[32,32,128]{2,1,0:T(8,128)S(1)} %all_to_all.10.received) | copy-start | bytes 1572868
  40.6 41.5 %slice-start = ((s8[5505024]{0:T(1024)(128)(4,1)}), s8[4194304]{0:T(1024)(128)(4,1)S(1)}, s32[]{:S(2)}) async-start(s8[5505024]{0:T(1024)(128)(4,1)} %bitcast.29), calls=%async_computation.2 | async-start | bytes 8388608
  40.6 61.8 %collective-permute-start = (f32[16,32,128]{2,1,0:T(8,128)S(1)}, f32[16,32,128]{2,1,0:T(8,128)S(1)}, u32[]{:S(2)}, u32[]{:S(2)}) collective-permute-start(f32[16,32,128]{2,1,0:T(8,128)S(1)} %slice.58), channel_id=1, source_target_pairs={{0,96},{1,97},{2,98},{3,99},{4,100},{5,101},{6,102},{7,103},{8,104... | collective-permute-start | bytes 786440 | tf_op jit(solution)/shard_map/ppermute | solution.py:408
  41.5 61.0 %collective-permute-start.1 = (f32[16,32,128]{2,1,0:T(8,128)S(1)}, f32[16,32,128]{2,1,0:T(8,128)S(1)}, u32[]{:S(2)}, u32[]{:S(2)}) collective-permute-start(f32[16,32,128]{2,1,0:T(8,128)S(1)} %slice.58), channel_id=1, source_target_pairs={{32,96},{33,97},{34,98},{35,99},{36,100},{37,101},{38,102},{39,103... | collective-permute-start | bytes 786440 | tf_op jit(solution)/shard_map/ppermute | solution.py:409
  73.6 8.6 %slice-start.1 = ((s8[5505024]{0:T(1024)(128)(4,1)}), s8[1310720]{0:T(1024)(128)(4,1)S(1)}, s32[]{:S(2)}) async-start(s8[5505024]{0:T(1024)(128)(4,1)} %bitcast.29), calls=%async_computation.3 | async-start | bytes 2621440
  102.5 0.7 copy-start.2
  102.5 0.8 copy-start.3
  103.2 32.0 %copy-start.4 = (f32[2,104,128]{2,1,0:T(8,128)S(1)}, f32[2,104,128]{2,1,0:T(8,128)}, u32[]{:S(2)}) copy-start(f32[2,104,128]{2,1,0:T(8,128)} %get-tuple-element.14) | copy-start | bytes 319492
  115.6 2.0 %collective-permute-start.5 = (f32[16,8,128]{2,1,0:T(8,128)S(1)}, f32[16,8,128]{2,1,0:T(8,128)S(1)}, u32[]{:S(2)}, u32[]{:S(2)}) collective-permute-start(f32[16,8,128]{2,1,0:T(8,128)S(1)} %get-tuple-element.20), channel_id=1, source_target_pairs={{96,0},{97,1},{98,2},{99,3},{100,4},{101,5},{102,6},{103,7},{104,8... | collective-permute-start | bytes 196616 | tf_op jit(solution)/shard_map/ppermute | solution.py:475
  116.3 10.4 %collective-permute-start.6 = (f32[16,8,128]{2,1,0:T(8,128)S(1)}, f32[16,8,128]{2,1,0:T(8,128)S(1)}, u32[]{:S(2)}, u32[]{:S(2)}) collective-permute-start(f32[16,8,128]{2,1,0:T(8,128)S(1)} %get-tuple-element.19), channel_id=1, source_target_pairs={{96,32},{97,33},{98,34},{99,35},{100,36},{101,37},{102,38},{103,39... | collective-permute-start | bytes 196616 | tf_op jit(solution)/shard_map/ppermute | solution.py:476
  128.2 22.6 %all-to-all-start.1 = ((f32[32,8,128]{2,1,0:T(8,128)}), f32[32,8,128]{2,1,0:T(8,128)S(1)}, u32[]{:S(2)}, u32[]{:S(2)}) async-start(f32[32,8,128]{2,1,0:T(8,128)} %pad_maximum_fusion.3), calls=%async_computation.1 | async-start | bytes 262144 | tf_op jit(solution)/shard_map/all_to_all | solution.py:478
  135.2 9.3 %collective-permute-start.7 = (f32[104,128]{1,0:T(8,128)S(1)}, f32[104,128]{1,0:T(8,128)S(1)}, u32[]{:S(2)}, u32[]{:S(2)}) collective-permute-start(f32[104,128]{1,0:T(8,128)S(1)} %get-tuple-element.22), channel_id=1, source_target_pairs={{0,1},{1,2},{2,3},{3,4},{4,5},{5,6},{6,7},{7,8},{8,9},{9,10},{10,1... | collective-permute-start | bytes 159752 | tf_op jit(solution)/shard_map/ppermute | solution.py:404
  136.5 8.0 %collective-permute-start.8 = (f32[104,128]{1,0:T(8,128)S(1)}, f32[104,128]{1,0:T(8,128)S(1)}, u32[]{:S(2)}, u32[]{:S(2)}) collective-permute-start(f32[104,128]{1,0:T(8,128)S(1)} %get-tuple-element.21), channel_id=1, source_target_pairs={{1,0},{2,1},{3,2},{4,3},{5,4},{6,5},{7,6},{8,7},{9,8},{10,9},{11,1... | collective-permute-start | bytes 159752 | tf_op jit(solution)/shard_map/ppermute | solution.py:405
  144.5 0.6 copy-start.5
  145.1 0.6 copy-start.6
  150.7 0.7 copy-start.1

commit v2 on v1

v2 whole, which is shorter than its diff:
```python
import jax
import jax.numpy as jnp
from jax import lax
from jax.experimental import pallas as pl
from jax.experimental.pallas import tpu as pltpu
from jax.sharding import PartitionSpec as P

F32 = jnp.float32
BF16 = jnp.bfloat16
I32 = jnp.int32
HALO = 32
FIELDS, LEVELS, GPOINTS, BANDS, NODES = 3, 32, 112, 14, 32
ROWS = FIELDS * LEVELS
CELLS, COARSE = 2048, 512
BLOCKS, BLOCK_COLS, MOST = 32, 16, 2
DOMAINS, SLOTS = 32, 4
SLOT_COLS = BLOCK_COLS * MOST
LANES = 128
PER_TILE = LANES // SLOT_COLS
TILES = CELLS // LANES
UNIT = 256
UNIT_SENDERS = UNIT // SLOT_COLS
STAY = 16
MOVED = DOMAINS - STAY
LEVEL_BLOCK = 8
LOG2E = 1.4426950408889634
VMEM_LIMIT = 28 * 1024 * 1024


def halves(x):
    high = x.astype(BF16)
    return high, (x - high.astype(F32)).astype(BF16)


def thirds(x):
    high = x.astype(BF16)
    rest = x - high.astype(F32)
    middle = rest.astype(BF16)
    return high, middle, (rest - middle.astype(F32)).astype(BF16)


def exact_dot(x, chosen, contract):
    rows = x.shape[0]
    stacked = jnp.concatenate(thirds(x), axis=0)
    product = lax.dot_general(
        stacked, chosen, (((1,), (contract,)), ((), ())), preferred_element_type=F32
    )
    return product[:rows] + product[rows : 2 * rows] + product[2 * rows :]


def iota(shape, dim):
    return lax.broadcasted_iota(I32, shape, dim)


def ones_where(mask):
    return jnp.where(mask, 1.0, 0.0).astype(BF16)


def regroup(pieces, shift_of):
    group = iota(pieces[0].shape, 1) // SLOT_COLS
    result = None
    for k, piece in enumerate(pieces):
        shift = (shift_of(k) % PER_TILE) * SLOT_COLS
        moved = pltpu.roll(piece, shift, 1) if shift else piece
        result = moved if result is None else jnp.where(group == k, moved, result)
    return result


def column(row):
    n = row.shape[1]
    return jnp.sum(jnp.where(iota((n, n), 0) == iota((n, n), 1), row, 0.0), axis=1, keepdims=True)


def aerosol_copies(depth, ssa, albedo, target, begin, count, sems):
    lanes = pl.ds(begin, count)
    height = BANDS * LEVELS
    return [
        pltpu.make_async_copy(depth.at[:, lanes], target.at[pl.ds(0, height)], sems.at[0]),
        pltpu.make_async_copy(ssa.at[:, lanes], target.at[pl.ds(height, height)], sems.at[1]),
        pltpu.make_async_copy(albedo.at[:, lanes], target.at[pl.ds(2 * height, 1)], sems.at[2]),
    ]


def edge_kernel(role, low_state, low_kappa, low_near, high_state, high_kappa, high_near, low, high):
    @pl.when(role[0] != SLOTS - 1)
    def _():
        for state, kappa, near, edge in (
            (low_state, low_kappa, low_near, low), (high_state, high_kappa, high_near, high)
        ):
            edge[0:ROWS, :] = state[...]
            others = [near[n].astype(F32) for n in range(3)]
            edge[ROWS : ROWS + 8, :] = jnp.concatenate(
                [kappa[...]] + others + [jnp.zeros((4, LANES), F32)], axis=0
            )


def stage_kernel(
    role, gas, ext, ssa, ray, solar, aero_depth, aero_ssa, albedo,
    weights, solar_out, aero_two, staged, sems,
):
    is_last = role[0] == SLOTS - 1
    tail = (DOMAINS + MOVED) * SLOT_COLS
    total = (SLOTS - 1) * DOMAINS * SLOT_COLS
    copies = aerosol_copies(aero_depth, aero_ssa, albedo, staged, total - tail, tail, sems)
    onward = pltpu.make_async_copy(staged, aero_two, sems.at[3])

    @pl.when(is_last)
    def _():
        for copy in copies:
            copy.start()

    @pl.when(role[0] >= SLOTS - 2)
    def _():
        radiation_weights(gas, ext, ssa, ray, solar, weights, solar_out)

    @pl.when(is_last)
    def _():
        for copy in copies:
            copy.wait()
        onward.start()
        onward.wait()


def coarsen_kernel(role, routes, state, parent, sun, _, message, slots_out):
    @pl.when(role[0] != SLOTS - 1)
    def _():
        pack_columns(routes, state, parent, sun, message, slots_out)


def pack_columns(routes, state, parent, sun, message, slots_out):
    block = iota((1, COARSE), 1) // BLOCK_COLS
    target = jnp.zeros((1, COARSE), I32)
    for b in range(BLOCKS):
        target = jnp.where(block == b, routes[0, 0, b], target)
    arrival = jnp.zeros((1, COARSE), I32)
    for b in range(BLOCKS):
        same = (target == routes[0, 0, b]) & (block > b)
        arrival = arrival + jnp.where(same, 1, 0)
    place = (target * MOST + arrival) * BLOCK_COLS + iota((1, COARSE), 1) % BLOCK_COLS
    slots_out[...] = place

    lineage = ones_where(iota((COARSE, CELLS), 0) == parent[...])
    coarse = 0.25 * exact_dot(state[...], lineage, 1)
    sun_rows = jnp.where(iota((8, COARSE), 0) == 0, sun[...], 0.0)
    columns = jnp.concatenate([coarse, sun_rows], axis=0)
    placed = ones_where(iota((DOMAINS * SLOT_COLS, COARSE), 0) == place)
    packed = exact_dot(columns, placed, 1)
    span = ROWS // PER_TILE
    for tile in range(DOMAINS // PER_TILE):
        part = packed[:, tile * LANES : (tile + 1) * LANES]
        for e in range(PER_TILE):
            pieces = [part[a * span : (a + 1) * span] for a in range(PER_TILE)]
            message[tile * PER_TILE + e, 0:span, :] = regroup(pieces, lambda a: a - e)
            moved = pltpu.roll(part[ROWS:], ((-e) % PER_TILE) * SLOT_COLS, 1) if e else part[ROWS:]
            message[tile * PER_TILE + e, span : span + 8, :] = moved


def radiation_weights(gas, ext, ssa, ray, solar, weights, solar_out):
    band = jnp.where(iota((GPOINTS, 16), 0) // 8 == iota((GPOINTS, 16), 1), 1.0, 0.0)
    spot = iota((GPOINTS, 16), 1)
    ext_col, ssa_col, ray_col = column(ext[...]), column(ssa[...]), column(ray[...])
    scatter_w = jnp.where(spot == BANDS, ray_col, jnp.where(spot == BANDS + 1, ssa_col * ext_col, 0.0))
    optical_w = jnp.where(spot == BANDS, ray_col, jnp.where(spot == BANDS + 1, ext_col, band))
    gas_hi, gas_lo = halves(gas[...].T)
    opt_hi, opt_lo = halves(optical_w)
    sca_hi, sca_lo = halves(scatter_w)
    none = jnp.zeros((GPOINTS, 16), F32)
    wide = jnp.zeros((GPOINTS, NODES), F32)
    upper = [gas_hi, gas_lo, gas_hi, opt_hi, opt_lo, opt_hi, none, none]
    lower = [wide, wide, wide, sca_hi, sca_lo, sca_hi, band, band]
    weights[0:GPOINTS, :] = (-jnp.concatenate([p.astype(F32) for p in upper], axis=1)).astype(BF16)
    weights[GPOINTS:, :] = jnp.concatenate([p.astype(F32) for p in lower], axis=1).astype(BF16)
    solar_out[...] = jnp.broadcast_to(column(solar[...]), (GPOINTS, LANES))


def diffuse_kernel(role, state, kappa, near, left, right, _, out, fields, rates, goal, chosen):
    @pl.when(role[0] == SLOTS - 1)
    def _():
        out[...] = jnp.zeros_like(out)

    @pl.when(role[0] != SLOTS - 1)
    def _():
        for ref, start, width, shift in (
            (left, 0, LANES, LANES - HALO - CELLS),
            (right, LANES + CELLS, LANES, LANES - HALO + CELLS),
        ):
            fields[:, start : start + width] = ref[0:ROWS, :]
            rates[:, start : start + width] = ref[ROWS : ROWS + 1, :]
            goal[0:3, start : start + width] = ref[ROWS + 1 : ROWS + 4, :].astype(I32) + shift
        fields[:, LANES : LANES + CELLS] = state[...]
        rates[:, LANES : LANES + CELLS] = kappa[...]
        for n in range(3):
            goal[n : n + 1, LANES : LANES + CELLS] = near[n] + (LANES - HALO)
        window = 3 * LANES
        rows = iota((window, LANES), 0)

        def spread(tile):
            first = min(max(tile - 1, 0), TILES - 1)
            return first * LANES

        results = []
        for tile in range(TILES + 2):
            here = slice(tile * LANES, (tile + 1) * LANES)
            place = rows + spread(tile)
            count = jnp.zeros((window, LANES), F32)
            for n in range(3):
                count = count + jnp.where(place == goal[n : n + 1, here], 1.0, 0.0)
            picked = count.astype(BF16)
            chosen[tile] = picked
            own = fields[:, here]
            total = exact_dot(fields[:, spread(tile) : spread(tile) + window], picked, 0)
            results.append(own + rates[:, here] * (total - 3.0 * own))
        for tile, value in enumerate(results):
            fields[:, tile * LANES : (tile + 1) * LANES] = value
        for tile in range(1, TILES + 1):
            here = slice(tile * LANES, (tile + 1) * LANES)
            own = fields[:, here]
            total = exact_dot(fields[:, spread(tile) : spread(tile) + window], chosen[tile], 0)
            value = own + rates[:, here] * (total - 3.0 * own)
            out[:, (tile - 1) * LANES : tile * LANES] = value


def radiation_kernel(
    role, weights, solar, received, from_first, from_second, from_moved, _left, _right, depth, ssa, albedo,
    aero_two, early, late,
    profile, columns, aero, optics, scatter_q, decay, beam, glow, net, sems,
):
    step = pl.program_id(0)
    steps = pl.num_programs(0)
    is_third, is_last = role[0] == SLOTS - 2, role[0] == SLOTS - 1
    ahead = DOMAINS // UNIT_SENDERS
    active = is_third | is_last

    def copies(unit, slot):
        two = jnp.where(unit < ahead, unit + MOVED // UNIT_SENDERS, unit - ahead) * UNIT
        third, fourth = [], []
        for tile in range(UNIT // LANES):
            lanes = pl.ds(pl.multiple_of(two + tile * LANES, LANES), LANES)
            third.append(
                pltpu.make_async_copy(
                    aero_two.at[:, lanes],
                    aero.at[slot, tile, pl.ds(0, 2 * BANDS * LEVELS + 8)],
                    sems.at[slot, tile, 0],
                )
            )
            fourth += aerosol_copies(
                depth, ssa, albedo, aero.at[slot, tile],
                pl.multiple_of(unit * UNIT + tile * LANES, LANES), LANES, sems.at[slot, tile],
            )
        return (is_third, third), (is_last, fourth)

    def begin(unit, slot):
        for chosen, descriptors in copies(unit, slot):
            @pl.when(chosen)
            def _():
                for descriptor in descriptors:
                    descriptor.start()

    slot = step % 2

    @pl.when(step == 0)
    def _():
        begin(step, slot)

    @pl.when(step + 1 < steps)
    def _():
        begin(step + 1, 1 - slot)

    for chosen, ref, first in (
        (is_third & (step < ahead), received, 0),
        (is_last & (step < ahead), from_first, 0),
        (is_last & (step >= ahead), from_second, ahead),
        (is_third & (step >= ahead), from_moved, ahead),
    ):
        @pl.when(chosen)
        def _():
            profile[...] = ref[pl.ds((step - first) * UNIT_SENDERS, UNIT_SENDERS)]

    @pl.when(active)
    def _():
        span = ROWS // PER_TILE
        for tile in range(UNIT // LANES):
            lanes = slice(tile * LANES, (tile + 1) * LANES)
            parts = [profile[tile * PER_TILE + e] for e in range(PER_TILE)]
            for a in range(PER_TILE):
                pieces = [part[0:span] for part in parts]
                columns[a * span : (a + 1) * span, lanes] = regroup(pieces, lambda e: e - a)
            pieces = [part[span : span + 8] for part in parts]
            columns[ROWS : ROWS + 8, lanes] = regroup(pieces, lambda e: e)
        for chosen, descriptors in copies(step, slot):
            @pl.when(chosen)
            def _():
                for descriptor in descriptors:
                    descriptor.wait()
        radiate(weights, solar, columns, aero, slot, optics, scatter_q, decay, beam, glow, net)
        heat = (net[0:LEVELS] - net[1 : LEVELS + 1]).sum(axis=1) * (LEVELS / GPOINTS)
        span = LEVELS // PER_TILE
        messages = []
        for tile in range(UNIT // LANES):
            part = heat[:, tile * LANES : (tile + 1) * LANES]
            pieces = [part[a * span : (a + 1) * span] for a in range(PER_TILE)]
            messages += [regroup(pieces, lambda a: a - e) for e in range(PER_TILE)]

        @pl.when(step < ahead)
        def _():
            for e, message in enumerate(messages):
                early[e] = message

        @pl.when(step >= ahead)
        def _():
            for e, message in enumerate(messages):
                late[e] = message


def radiate(weights, solar, columns, aero, slot, optics, scatter_q, decay, beam, glow, net):
    cosine = columns[ROWS : ROWS + 1, :]
    path = jnp.maximum(cosine, 0.1)
    scale = LOG2E / path
    beam[...] = solar[:, 0:1] * (0.5 * jnp.maximum(cosine, 0.0))
    glow[...] = jnp.zeros_like(glow)
    node = iota((NODES, UNIT), 0).astype(F32)
    spot = iota((16, UNIT), 0)
    half = GPOINTS // 2

    def bands_of(first):
        tiles = range(UNIT // LANES)
        rows = pl.ds(first, 16, stride=LEVELS)
        return jnp.concatenate([aero[slot, tile, rows, :] for tile in tiles], axis=1)

    def down(block, _):
        first = block * LEVEL_BLOCK
        for j in range(LEVEL_BLOCK):
            level = first + j
            warmth = (columns[pl.ds(level, 1), :] + 4.0) * ((NODES - 1) / 8.0)
            vapour = columns[pl.ds(level + LEVELS, 1), :] * scale
            cloud = columns[pl.ds(level + 2 * LEVELS, 1), :] * scale
            hat = jnp.maximum(0.0, 1.0 - jnp.abs(warmth - node)) * vapour
            depth = bands_of(level) * scale
            share = depth * bands_of(level + BANDS * LEVELS)
            hat_hi, hat_lo = halves(hat)
            opt_hi, opt_lo = halves(
                jnp.where(spot < BANDS, depth, jnp.where(spot == BANDS, scale, cloud))
            )
            sca_hi, sca_lo = halves(jnp.where(spot < BANDS, share, 0.0))
            stacked = jnp.concatenate(
                [hat_hi, hat_hi, hat_lo, opt_hi, opt_hi, opt_lo, sca_hi, sca_lo], axis=0
            )
            optics[j] = jnp.dot(weights[...], stacked, preferred_element_type=F32)
        for lane in range(0, UNIT, LANES):
            lanes = slice(lane, lane + LANES)
            back = jnp.broadcast_to(1.66 * path[:, lanes], (half, LANES))
            for row in range(0, GPOINTS, half):
                rows = slice(row, row + half)
                straight = beam[rows, lanes]
                spread = glow[rows, lanes]
                for j in range(LEVEL_BLOCK):
                    loss = optics[j, rows, lanes]
                    part = optics[j, GPOINTS + row : GPOINTS + row + half, lanes]
                    through = straight * jnp.exp2(loss)
                    kept = jnp.exp2(back * (loss + part))
                    source = (through - straight) * (part * pl.reciprocal(loss, approx=True))
                    scatter_q[first + j, rows, lanes] = source
                    decay[first + j, rows, lanes] = kept
                    total = (straight + straight + spread).reshape(half // 8, 8, LANES).sum(axis=0)
                    if row == 0:
                        net[first + j, :, lanes] = total
                    else:
                        net[first + j, :, lanes] += total
                    spread = spread * kept + source
                    straight = through
                beam[rows, lanes] = straight
                glow[rows, lanes] = spread
        return 0

    lax.fori_loop(0, LEVELS // LEVEL_BLOCK, down, 0)
    for lane in range(0, UNIT, LANES):
        lanes = slice(lane, lane + LANES)
        floor = 2.0 * beam[:, lanes] + glow[:, lanes]
        ground = 2 * BANDS * LEVELS
        rising = aero[slot, lane // LANES, ground : ground + 1, :] * floor
        net[LEVELS, :, lanes] = (floor - rising).reshape(GPOINTS // 8, 8, LANES).sum(axis=0)

        def up(i, rising):
            for k in range(4):
                level = LEVELS - 1 - (i * 4 + k)
                rising = rising * decay[level, :, lanes] + scatter_q[level, :, lanes]
                net[level, :, lanes] -= rising.reshape(GPOINTS // 8, 8, LANES).sum(axis=0)
            return rising

        lax.fori_loop(0, LEVELS // 4, up, rising)


def rad_scratch():
    return [
        pltpu.VMEM((ROWS + 8, UNIT), F32),
        pltpu.VMEM((2, UNIT // LANES, (2 * BANDS + 2) * LEVELS, LANES), F32),
        pltpu.VMEM((LEVEL_BLOCK, 2 * GPOINTS, UNIT), F32),
        pltpu.VMEM((LEVELS, GPOINTS, UNIT), F32),
        pltpu.VMEM((LEVELS, GPOINTS, UNIT), F32),
        pltpu.VMEM((GPOINTS, UNIT), F32),
        pltpu.VMEM((GPOINTS, UNIT), F32),
        pltpu.VMEM((LEVELS + 1, 8, UNIT), F32),
    ]


def warm_kernel(role, mine, parent, slots_in, stepped, out):
    span = LEVELS // PER_TILE
    tiles = []
    for tile in range(DOMAINS // PER_TILE):
        parts = [mine[tile * PER_TILE + e] for e in range(PER_TILE)]
        tiles.append(
            jnp.concatenate([regroup(parts, lambda e: e - a) for a in range(PER_TILE)], axis=0)
        )
    heat = jnp.concatenate(tiles, axis=1)
    placed = ones_where(iota((DOMAINS * SLOT_COLS, COARSE), 0) == slots_in[...])
    coarse = exact_dot(heat, placed, 0)
    lineage = ones_where(iota((COARSE, CELLS), 0) == parent[...])
    fine = exact_dot(coarse, lineage, 0)
    out[...] = jnp.where(role[0] != SLOTS - 1, stepped[...] + 0.5 * fine, 0.0)


def near_core(x):
    return pltpu.with_memory_space_constraint(x, pltpu.VMEM)


def far(x):
    return pltpu.with_memory_space_constraint(x, pltpu.HBM)


def params():
    return pltpu.CompilerParams(vmem_limit_bytes=VMEM_LIMIT)


SMEM = pl.BlockSpec(memory_space=pltpu.SMEM)
VMEM = pl.BlockSpec(memory_space=pltpu.VMEM)
HBM = pl.BlockSpec(memory_space=pl.ANY)


def per_device(
    state, kappa, neighbours, parent, cos_zenith, routes, rad_albedo, aerosol_depth, aerosol_ssa,
    gas_table, cloud_ext, cloud_ssa, rayleigh, solar_weight,
):
    fields = state.reshape(ROWS, CELLS)
    near = jnp.transpose(neighbours, (1, 0, 2))
    slot = lax.axis_index("grp").astype(I32).reshape(1)
    last = SLOTS - 1
    depth = jnp.transpose(aerosol_depth[0], (1, 0, 2)).reshape(BANDS * LEVELS, -1)
    ssa = jnp.transpose(aerosol_ssa[0], (1, 0, 2)).reshape(BANDS * LEVELS, -1)
    aero_rows = 2 * BANDS * LEVELS + 8

    def edges(tile):
        return [
            pl.BlockSpec((ROWS, LANES), lambda i: (0, tile)),
            pl.BlockSpec((1, LANES), lambda i: (0, tile)),
            pl.BlockSpec((3, 1, LANES), lambda i: (0, 0, tile)),
        ]

    edge_low, edge_high = pl.pallas_call(
        edge_kernel,
        grid=(1,),
        in_specs=[SMEM] + edges(0) + edges(TILES - 1),
        out_specs=[pl.BlockSpec((ROWS + 8, LANES), lambda i: (0, 0))] * 2,
        out_shape=[jax.ShapeDtypeStruct((ROWS + 8, LANES), F32)] * 2,
        compiler_params=params(),
        name="edge",
    )(slot, far(fields), far(kappa), far(near), far(fields), far(kappa), far(near))
    forward = [
        (s * DOMAINS + i, s * DOMAINS + (i + 1) % DOMAINS) for s in range(last) for i in range(DOMAINS)
    ]
    backward = [(target, source) for source, target in forward]
    left = lax.ppermute(edge_high, ("grp", "dom"), forward)
    right = lax.ppermute(edge_low, ("grp", "dom"), backward)

    weights, solar, aero_two = pl.pallas_call(
        stage_kernel,
        in_specs=[SMEM] + [VMEM] * 5 + [HBM] * 3,
        out_specs=[VMEM] * 2 + [HBM],
        out_shape=[
            jax.ShapeDtypeStruct((2 * GPOINTS, 176), BF16),
            jax.ShapeDtypeStruct((GPOINTS, LANES), F32),
            jax.ShapeDtypeStruct((aero_rows, (DOMAINS + MOVED) * SLOT_COLS), F32),
        ],
        scratch_shapes=[
            pltpu.VMEM((aero_rows, (DOMAINS + MOVED) * SLOT_COLS), F32),
            pltpu.SemaphoreType.DMA((4,)),
        ],
        compiler_params=params(),
        name="stage",
    )(
        slot, far(gas_table.T), far(cloud_ext[None]), far(cloud_ssa[None]), far(rayleigh[None]),
        far(solar_weight[None]), far(depth), far(ssa), far(rad_albedo),
    )
    aero_two = lax.ppermute(aero_two, "grp", [(last, last - 1)])

    message, places = pl.pallas_call(
        coarsen_kernel,
        in_specs=[SMEM, SMEM] + [VMEM] * 3 + [HBM],
        out_specs=[VMEM] * 2,
        out_shape=[
            jax.ShapeDtypeStruct((DOMAINS, 32, LANES), F32),
            jax.ShapeDtypeStruct((1, COARSE), I32),
        ],
        compiler_params=params(),
        name="coarsen",
    )(slot, far(jnp.transpose(routes, (0, 2, 1))), far(fields), far(parent), far(cos_zenith), weights)
    received = lax.all_to_all(message, "dom", 0, 0, tiled=True)
    from_first = lax.ppermute(received, "grp", [(0, last)])
    from_second = lax.ppermute(received[:STAY], "grp", [(1, last)])
    from_moved = lax.ppermute(received[STAY:], "grp", [(1, 2)])

    ahead = DOMAINS // UNIT_SENDERS
    units = ahead + STAY // UNIT_SENDERS

    early, late = pl.pallas_call(
        radiation_kernel,
        grid_spec=pltpu.PrefetchScalarGridSpec(
            num_scalar_prefetch=1,
            grid=(units,),
            in_specs=[
                pl.BlockSpec((2 * GPOINTS, 176), lambda i, role: (0, 0)),
                pl.BlockSpec((GPOINTS, LANES), lambda i, role: (0, 0)),
                VMEM, VMEM, VMEM, VMEM, VMEM, VMEM, HBM, HBM, HBM, VMEM,
            ],
            out_specs=[
                pl.BlockSpec(
                    (UNIT_SENDERS, 8, LANES), lambda i, role: (jnp.minimum(i, ahead - 1), 0, 0)
                ),
                pl.BlockSpec(
                    (UNIT_SENDERS, 8, LANES), lambda i, role: (jnp.maximum(i - ahead, 0), 0, 0)
                ),
            ],
            scratch_shapes=[
                pltpu.VMEM((UNIT_SENDERS, 32, LANES), F32),
                *rad_scratch(),
                pltpu.SemaphoreType.DMA((2, UNIT // LANES, 3)),
            ],
        ),
        out_shape=[
            jax.ShapeDtypeStruct((ahead * UNIT_SENDERS, 8, LANES), F32),
            jax.ShapeDtypeStruct(((units - ahead) * UNIT_SENDERS, 8, LANES), F32),
        ],
        compiler_params=params(),
        name="radiation",
    )(
        slot, weights, solar, near_core(received), near_core(from_first), near_core(from_second),
        near_core(from_moved), near_core(left), near_core(right), far(depth), far(ssa), far(rad_albedo),
        near_core(aero_two),
    )

    extended = CELLS + 2 * LANES
    stepped = pl.pallas_call(
        diffuse_kernel,
        in_specs=[SMEM] + [VMEM] * 5 + [HBM],
        out_specs=VMEM,
        out_shape=jax.ShapeDtypeStruct((ROWS, CELLS), F32),
        scratch_shapes=[
            pltpu.VMEM((ROWS, extended), F32),
            pltpu.VMEM((1, extended), F32),
            pltpu.VMEM((8, extended), I32),
            pltpu.VMEM((TILES + 2, 3 * LANES, LANES), BF16),
        ],
        compiler_params=params(),
        name="diffuse",
    )(slot, far(fields), far(kappa), far(near), near_core(left), near_core(right), early)

    to_first = lax.ppermute(early, "grp", [(last, 0)])
    to_second = lax.ppermute(late, "grp", [(last, 1)])
    moved_back = lax.ppermute(late, "grp", [(2, 1)])
    away = to_first + jnp.concatenate([to_second, moved_back], axis=0)
    returning = jnp.where(slot[0] == last - 1, early, away)
    mine = lax.all_to_all(returning, "dom", 0, 0, tiled=True)

    warmed = pl.pallas_call(
        warm_kernel,
        grid=(1,),
        in_specs=[
            SMEM,
            VMEM,
            pl.BlockSpec((1, CELLS), lambda i: (0, 0)),
            pl.BlockSpec((1, COARSE), lambda i: (0, 0)),
            pl.BlockSpec((LEVELS, CELLS), lambda i: (0, 0)),
        ],
        out_specs=pl.BlockSpec((LEVELS, CELLS), lambda i: (0, 0)),
        out_shape=jax.ShapeDtypeStruct((ROWS, CELLS), F32),
        input_output_aliases={4: 0},
        compiler_params=params(),
        name="warm",
    )(slot, near_core(mine), far(parent), places, stepped)
    return warmed.reshape(1, FIELDS, LEVELS, CELLS)


def solution(mesh):
    return jax.shard_map(
        per_device,
        mesh=mesh,
        in_specs=(
            P("grp", None, None, "dom"),
            P("grp", "dom"),
            P("grp", None, "dom"),
            P("grp", "dom"),
            P("grp", "dom"),
            P(("grp", "dom"), None, None),
            P("grp", "dom"),
            P("grp", None, None, "dom"),
            P("grp", None, None, "dom"),
            P(),
            P(),
            P(),
            P(),
            P(),
        ),
        out_specs=P("grp", None, None, "dom"),
        check_vma=False,
    )
```

time: 155 us -> 97.8 us (0.63)
  local copies, waits for them, and re-layouts: 39.3 us -> 0.04 us
  starting transfers between devices: 53.7 us -> 27.3 us
  waiting for transfers between devices: 12.6 us -> 36.9 us
  Pallas kernels: 22.8 us -> 12.5 us
  other arithmetic: 5.56 us -> 0.69 us
    ppermute x9, starting transfers between devices: 46.7 us -> 22.3 us  [the longest x1 9.5 us: per_device(): from_second = lax.ppermute(received[:STAY], 'grp', [(1, last)])]
    ppermute x9, waiting for transfers between devices: 12.6 us -> 34.5 us  [the longest x1 25.1 us: per_device(): moved_back = lax.ppermute(late, 'grp', [(2, 1)])]
    unnamed x31 -> x0, local copies, waits for them, and re-layouts: 19.1 us -> none
    ppermute x3 -> x0, local copies, waits for them, and re-layouts: 14.4 us -> none  [the longest x1 6.3 us: per_device(): lax.ppermute(aerosol(2 * slot_span, slot_span), 'grp', [(last, 2)])]
    pallas_call x1, Pallas kernels: 11.5 us -> 0.53 us  [per_device(): pl.pallas_call(radiation_kernel, grid_spec=pltpu.PrefetchScalarGridSpec(n...]
    squeeze x3 -> x0, local copies, waits for them, and re-layouts: 4.77 us -> none  [the longest x2 4.76 us: aerosol(): aerosol_ssa[0, :, :, cut]]
    concatenate x4 -> x0, other arithmetic: 4.7 us -> none  [the longest x3 4.04 us: aerosol(): jnp.concatenate([aerosol_depth[0, :, :, cut], aerosol_ssa[0, :, :, cut],...]
    all_to_all x1, waiting for transfers between devices: 0.01 us -> 2.38 us  [per_device(): mine = lax.all_to_all(returning, 'dom', 0, 0, tiled=True)]
  transfers between devices with their start and end apart: 10 -> 10, of which waited for: 2 -> 4; matrix products, arithmetic and copies ran while one was open for 23% -> 0% of each run, Pallas kernels for 6% -> 9%
where the time goes in v2:
time: 97.8 us; the launch traced here: 97.3 us
  waiting for transfers between devices  36.9 us (38%)
  starting transfers between devices  27.3 us (28%)
  blocking collectives  19.7 us (20%)
  Pallas kernels  12.5 us (13%)
    ppermute x1, waiting for transfers between devices, per_device(): moved_back = lax.ppermute(late, 'grp', [(2, 1)])  25.1 us
    all_to_all x1, blocking collectives, per_device(): received = lax.all_to_all(message, 'dom', 0, 0, tiled=True)  19.7 us
    ppermute x1, starting transfers between devices, per_device(): from_second = lax.ppermute(received[:STAY], 'grp', [(1, last)])  9.5 us
    ppermute x1, waiting for transfers between devices, per_device(): left = lax.ppermute(edge_high, ('grp', 'dom'), forward)  7.97 us
    all_to_all x1, starting transfers between devices, per_device(): mine = lax.all_to_all(returning, 'dom', 0, 0, tiled=True)  5.01 us
    pallas_call x1, Pallas kernels, per_device(): pl.pallas_call(diffuse_kernel, in_specs=[SMEM] + [VMEM] * 5 + [HBM], out_...  4.93 us
    ppermute x1, starting transfers between devices, per_device(): right = lax.ppermute(edge_low, ('grp', 'dom'), backward)  4.64 us
    pallas_call x1, Pallas kernels, per_device(): pl.pallas_call(coarsen_kernel, in_specs=[SMEM, SMEM] + [VMEM] * 3 + [HBM]...  2.75 us
  transfers between devices with their start and end apart: 10, of which 4 were waited for; matrix products, arithmetic and copies ran while one was open for 0% of the time, Pallas kernels for 9%

profile of v2, /device:TPU:1, one launch (start us, length us, event | category | flops | bytes accessed | tf_op | source)
XLA Modules:
  0.0 97.3 jit_solution(10664035432886270481)
XLA Ops:
  0.0 0.8 stage.1
  0.8 1.0 %collective-permute-start.5 = (f32[904,1536]{1,0:T(8,128)S(1)}, f32[904,1536]{1,0:T(8,128)S(1)}, u32[]{:S(2)}, u32[]{:S(2)}) collective-permute-start(f32[904,1536]{1,0:T(8,128)S(1)} %get-tuple-element.19), channel_id=1, source_target_pairs={{96,64},{97,65},{98,66},{99,67},{100,68},{101,69},{102,70},{103,71... | collective-permute-start | bytes 16662536 | tf_op jit(solution)/shard_map/ppermute | solution.py:493
  1.8 2.7 %coarsen.1 = (f32[32,32,128]{2,1,0:T(8,128)S(1)}, s32[1,512]{1,0:T(1,128)S(1)}) custom-call(s32[1]{0:T(128)} %bitcast.role, s32[1,1,32]{2,1,0:T(1,128)} %bitcast.36, f32[96,2048]{1,0:T(8,128)} %bitcast.24, s32[1,2048]{1,0:T(1,128)} %parent.3, f32[1,512]{1,0:T(1,128)} %sun.1, bf16[224,176]{1,0:T(8,128)(2,1)S(1)} %get-tuple-element.14._.weights), custom_call_target="tpu_custom_call" | custom-call | tf_op jit(solution)/shard_map/coarsen/pallas_call | solution.py:495
  4.6 19.7 %all_to_all.10.received = f32[32,32,128]{2,1,0:T(8,128)S(1)} all-to-all(f32[32,32,128]{2,1,0:T(8,128)S(1)} %get-tuple-element.16), channel_id=1, replica_groups=mesh['grp'=4,'dom'=32] {'dom'}, dimensions={0} | all-to-all | bytes 1048576 | tf_op jit(solution)/shard_map/all_to_all | solution.py:506
  24.3 0.7 collective-permute-start
  25.0 9.5 %collective-permute-start.1 = (f32[16,32,128]{2,1,0:T(8,128)S(1)}, f32[16,32,128]{2,1,0:T(8,128)S(1)}, u32[]{:S(2)}, u32[]{:S(2)}) collective-permute-start(f32[16,32,128]{2,1,0:T(8,128)S(1)} %get-tuple-element.24), channel_id=1, source_target_pairs={{32,96},{33,97},{34,98},{35,99},{36,100},{37,101},{38,102},{39,103... | collective-permute-start | bytes 786440 | tf_op jit(solution)/shard_map/ppermute | solution.py:508
  34.5 1.3 %collective-permute-start.2 = (f32[16,32,128]{2,1,0:T(8,128)S(1)}, f32[16,32,128]{2,1,0:T(8,128)S(1)}, u32[]{:S(2)}, u32[]{:S(2)}) collective-permute-start(f32[16,32,128]{2,1,0:T(8,128)S(1)} %get-tuple-element.23), channel_id=1, source_target_pairs={{32,64},{33,65},{34,66},{35,67},{36,68},{37,69},{38,70},{39,71},{4... | collective-permute-start | bytes 786440 | tf_op jit(solution)/shard_map/ppermute | solution.py:509
  35.9 0.9 edge.1
  36.7 1.9 %collective-permute-start.3 = (f32[104,128]{1,0:T(8,128)S(1)}, f32[104,128]{1,0:T(8,128)S(1)}, u32[]{:S(2)}, u32[]{:S(2)}) collective-permute-start(f32[104,128]{1,0:T(8,128)S(1)} %get-tuple-element.17), channel_id=1, source_target_pairs={{0,1},{1,2},{2,3},{3,4},{4,5},{5,6},{6,7},{7,8},{8,9},{9,10},{10,1... | collective-permute-start | bytes 159752 | tf_op jit(solution)/shard_map/ppermute | solution.py:471
  38.7 8.0 %collective-permute-done.3._left.left = f32[104,128]{1,0:T(8,128)S(1)} collective-permute-done((f32[104,128]{1,0:T(8,128)S(1)}, f32[104,128]{1,0:T(8,128)S(1)}, u32[]{:S(2)}, u32[]{:S(2)}) %collective-permute-start.3) | collective-permute-done | bytes 53280 | tf_op jit(solution)/shard_map/ppermute | solution.py:471
  46.6 4.6 %collective-permute-start.4 = (f32[104,128]{1,0:T(8,128)S(1)}, f32[104,128]{1,0:T(8,128)S(1)}, u32[]{:S(2)}, u32[]{:S(2)}) collective-permute-start(f32[104,128]{1,0:T(8,128)S(1)} %get-tuple-element.18), channel_id=1, source_target_pairs={{1,0},{2,1},{3,2},{4,3},{5,4},{6,5},{7,6},{8,7},{9,8},{10,9},{11,1... | collective-permute-start | bytes 159752 | tf_op jit(solution)/shard_map/ppermute | solution.py:472
  51.3 1.4 %collective-permute-done.4._right.right = f32[104,128]{1,0:T(8,128)S(1)} collective-permute-done((f32[104,128]{1,0:T(8,128)S(1)}, f32[104,128]{1,0:T(8,128)S(1)}, u32[]{:S(2)}, u32[]{:S(2)}) %collective-permute-start.4) | collective-permute-done | bytes 53280 | tf_op jit(solution)/shard_map/ppermute | solution.py:472
  52.7 0.0 collective-permute-done.1.from_second
  52.7 0.0 collective-permute-done.2.from_moved
  52.7 0.0 collective-permute-done.from_first
  52.7 0.0 collective-permute-done.5.aero_two
  52.7 0.5 radiation.1
  53.2 0.7 collective-permute-start.6
  53.9 1.3 %collective-permute-start.8 = (f32[16,8,128]{2,1,0:T(8,128)S(1)}, f32[16,8,128]{2,1,0:T(8,128)S(1)}, u32[]{:S(2)}, u32[]{:S(2)}) collective-permute-start(f32[16,8,128]{2,1,0:T(8,128)S(1)} %get-tuple-element.21), channel_id=1, source_target_pairs={{64,32},{65,33},{66,34},{67,35},{68,36},{69,37},{70,38},{71,39},{7... | collective-permute-start | bytes 196616 | tf_op jit(solution)/shard_map/ppermute | solution.py:568
  55.2 1.3 %collective-permute-start.7 = (f32[16,8,128]{2,1,0:T(8,128)S(1)}, f32[16,8,128]{2,1,0:T(8,128)S(1)}, u32[]{:S(2)}, u32[]{:S(2)}) collective-permute-start(f32[16,8,128]{2,1,0:T(8,128)S(1)} %get-tuple-element.21), channel_id=1, source_target_pairs={{96,32},{97,33},{98,34},{99,35},{100,36},{101,37},{102,38},{103,39... | collective-permute-start | bytes 196616 | tf_op jit(solution)/shard_map/ppermute | solution.py:567
  56.5 25.1 %collective-permute-done.8 = f32[16,8,128]{2,1,0:T(8,128)S(1)} collective-permute-done((f32[16,8,128]{2,1,0:T(8,128)S(1)}, f32[16,8,128]{2,1,0:T(8,128)S(1)}, u32[]{:S(2)}, u32[]{:S(2)}) %collective-permute-start.8) | collective-permute-done | bytes 65568 | tf_op jit(solution)/shard_map/ppermute | solution.py:568
  81.6 0.0 collective-permute-done.7
  81.7 0.0 collective-permute-done.6
  81.7 0.7 fusion
  82.3 5.0 %all-to-all-start.1 = ((f32[32,8,128]{2,1,0:T(8,128)}), f32[32,8,128]{2,1,0:T(8,128)S(1)}, u32[]{:S(2)}, u32[]{:S(2)}) async-start(f32[32,8,128]{2,1,0:T(8,128)} %fusion), calls=%async_computation.1 | async-start | bytes 262144 | tf_op jit(solution)/shard_map/all_to_all | solution.py:571
  87.4 4.9 %diffuse.1.stepped = f32[96,2048]{1,0:T(8,128)} custom-call(s32[1]{0:T(128)} %bitcast.role, f32[96,2048]{1,0:T(8,128)} %bitcast.27, f32[1,2048]{1,0:T(1,128)} %kappa.1, s32[3,1,2048]{2,1,0:T(1,128)} %bitcast.30, f32[104,128]{1,0:T(8,128)S(1)} %collective-permute-done.3._left.left, f32[104,128]{1,0:T(8,128)S(1)} %collective-permute-done.4._right.right, ...), custom_call_target="tpu_custom_call" | custom-call | tf_op jit(solution)/shard_map/diffuse/pallas_call | solution.py:551
  92.3 2.4 %all-to-all-done.1.mine = f32[32,8,128]{2,1,0:T(8,128)S(1)} async-done(((f32[32,8,128]{2,1,0:T(8,128)}), f32[32,8,128]{2,1,0:T(8,128)S(1)}, u32[]{:S(2)}, u32[]{:S(2)}) %all-to-all-start.1) | async-done | bytes 131104 | tf_op jit(solution)/shard_map/all_to_all | solution.py:571
  94.7 2.6 %warm.1 = f32[96,2048]{1,0:T(8,128)} custom-call(s32[1]{0:T(128)} %bitcast.role, f32[32,8,128]{2,1,0:T(8,128)S(1)} %all-to-all-done.1.mine, s32[1,2048]{1,0:T(1,128)} %parent.3, s32[1,512]{1,0:T(1,128)S(1)} %get-tuple-element.22.slots_in, f32[96,2048]{1,0:T(8,128)} %diffuse.1.stepped), custom_call_target="tpu_custom_call", output_to_operand_aliasing={{}: (4, {})} | custom-call | tf_op jit(solution)/shard_map/warm/pallas_call | solution.py:573
  (1 shorter events, 0.0 us)
Async XLA Ops:
  0.8 51.9 %collective-permute-start.5 = (f32[904,1536]{1,0:T(8,128)S(1)}, f32[904,1536]{1,0:T(8,128)S(1)}, u32[]{:S(2)}, u32[]{:S(2)}) collective-permute-start(f32[904,1536]{1,0:T(8,128)S(1)} %get-tuple-element.19), channel_id=1, source_target_pairs={{96,64},{97,65},{98,66},{99,67},{100,68},{101,69},{102,70},{103,71... | collective-permute-start | bytes 16662536 | tf_op jit(solution)/shard_map/ppermute | solution.py:493
  24.3 28.4 %collective-permute-start = (f32[32,32,128]{2,1,0:T(8,128)S(1)}, f32[32,32,128]{2,1,0:T(8,128)S(1)}, u32[]{:S(2)}, u32[]{:S(2)}) collective-permute-start(f32[32,32,128]{2,1,0:T(8,128)S(1)} %all_to_all.10.received), channel_id=1, source_target_pairs={{0,96},{1,97},{2,98},{3,99},{4,100},{5,101},{6,102},{7,103},{8,104... | collective-permute-start | bytes 1572872 | tf_op jit(solution)/shard_map/ppermute | solution.py:507
  25.0 27.6 %collective-permute-start.1 = (f32[16,32,128]{2,1,0:T(8,128)S(1)}, f32[16,32,128]{2,1,0:T(8,128)S(1)}, u32[]{:S(2)}, u32[]{:S(2)}) collective-permute-start(f32[16,32,128]{2,1,0:T(8,128)S(1)} %get-tuple-element.24), channel_id=1, source_target_pairs={{32,96},{33,97},{34,98},{35,99},{36,100},{37,101},{38,102},{39,103... | collective-permute-start | bytes 786440 | tf_op jit(solution)/shard_map/ppermute | solution.py:508
  34.5 18.1 %collective-permute-start.2 = (f32[16,32,128]{2,1,0:T(8,128)S(1)}, f32[16,32,128]{2,1,0:T(8,128)S(1)}, u32[]{:S(2)}, u32[]{:S(2)}) collective-permute-start(f32[16,32,128]{2,1,0:T(8,128)S(1)} %get-tuple-element.23), channel_id=1, source_target_pairs={{32,64},{33,65},{34,66},{35,67},{36,68},{37,69},{38,70},{39,71},{4... | collective-permute-start | bytes 786440 | tf_op jit(solution)/shard_map/ppermute | solution.py:509
  36.7 9.9 %collective-permute-start.3 = (f32[104,128]{1,0:T(8,128)S(1)}, f32[104,128]{1,0:T(8,128)S(1)}, u32[]{:S(2)}, u32[]{:S(2)}) collective-permute-start(f32[104,128]{1,0:T(8,128)S(1)} %get-tuple-element.17), channel_id=1, source_target_pairs={{0,1},{1,2},{2,3},{3,4},{4,5},{5,6},{6,7},{7,8},{8,9},{9,10},{10,1... | collective-permute-start | bytes 159752 | tf_op jit(solution)/shard_map/ppermute | solution.py:471
  46.6 6.1 %collective-permute-start.4 = (f32[104,128]{1,0:T(8,128)S(1)}, f32[104,128]{1,0:T(8,128)S(1)}, u32[]{:S(2)}, u32[]{:S(2)}) collective-permute-start(f32[104,128]{1,0:T(8,128)S(1)} %get-tuple-element.18), channel_id=1, source_target_pairs={{1,0},{2,1},{3,2},{4,3},{5,4},{6,5},{7,6},{8,7},{9,8},{10,9},{11,1... | collective-permute-start | bytes 159752 | tf_op jit(solution)/shard_map/ppermute | solution.py:472
  53.2 28.4 %collective-permute-start.6 = (f32[32,8,128]{2,1,0:T(8,128)S(1)}, f32[32,8,128]{2,1,0:T(8,128)S(1)}, u32[]{:S(2)}, u32[]{:S(2)}) collective-permute-start(f32[32,8,128]{2,1,0:T(8,128)S(1)} %get-tuple-element.20._), channel_id=1, source_target_pairs={{96,0},{97,1},{98,2},{99,3},{100,4},{101,5},{102,6},{103,7},{104,8... | collective-permute-start | bytes 393224 | tf_op jit(solution)/shard_map/ppermute | solution.py:566
  53.9 27.7 %collective-permute-start.8 = (f32[16,8,128]{2,1,0:T(8,128)S(1)}, f32[16,8,128]{2,1,0:T(8,128)S(1)}, u32[]{:S(2)}, u32[]{:S(2)}) collective-permute-start(f32[16,8,128]{2,1,0:T(8,128)S(1)} %get-tuple-element.21), channel_id=1, source_target_pairs={{64,32},{65,33},{66,34},{67,35},{68,36},{69,37},{70,38},{71,39},{7... | collective-permute-start | bytes 196616 | tf_op jit(solution)/shard_map/ppermute | solution.py:568
  55.2 26.4 %collective-permute-start.7 = (f32[16,8,128]{2,1,0:T(8,128)S(1)}, f32[16,8,128]{2,1,0:T(8,128)S(1)}, u32[]{:S(2)}, u32[]{:S(2)}) collective-permute-start(f32[16,8,128]{2,1,0:T(8,128)S(1)} %get-tuple-element.21), channel_id=1, source_target_pairs={{96,32},{97,33},{98,34},{99,35},{100,36},{101,37},{102,38},{103,39... | collective-permute-start | bytes 196616 | tf_op jit(solution)/shard_map/ppermute | solution.py:567
  82.3 12.3 %all-to-all-start.1 = ((f32[32,8,128]{2,1,0:T(8,128)}), f32[32,8,128]{2,1,0:T(8,128)S(1)}, u32[]{:S(2)}, u32[]{:S(2)}) async-start(f32[32,8,128]{2,1,0:T(8,128)} %fusion), calls=%async_computation.1 | async-start | bytes 262144 | tf_op jit(solution)/shard_map/all_to_all | solution.py:571

commit v3 on v2

--- a/solution.py
+++ b/solution.py
@@ -12,17 +12,21 @@
 FIELDS, LEVELS, GPOINTS, BANDS, NODES = 3, 32, 112, 14, 32
 ROWS = FIELDS * LEVELS
 CELLS, COARSE = 2048, 512
+LANES = 128
 BLOCKS, BLOCK_COLS, MOST = 32, 16, 2
 DOMAINS, SLOTS = 32, 4
 SLOT_COLS = BLOCK_COLS * MOST
-LANES = 128
+SPAN = ROWS // (LANES // SLOT_COLS)
+LINES = SPAN + 1
 PER_TILE = LANES // SLOT_COLS
 TILES = CELLS // LANES
 UNIT = 256
 UNIT_SENDERS = UNIT // SLOT_COLS
-STAY = 16
+STAY = 24
 MOVED = DOMAINS - STAY
 LEVEL_BLOCK = 8
+AERO = 2 * BANDS + 2
+PITCH = LEVELS + 8
 LOG2E = 1.4426950408889634
 VMEM_LIMIT = 28 * 1024 * 1024
 
@@ -73,58 +77,52 @@
 
 def aerosol_copies(depth, ssa, albedo, target, begin, count, sems):
     lanes = pl.ds(begin, count)
-    height = BANDS * LEVELS
+    levels = pl.ds(0, LEVELS)
     return [
-        pltpu.make_async_copy(depth.at[:, lanes], target.at[pl.ds(0, height)], sems.at[0]),
-        pltpu.make_async_copy(ssa.at[:, lanes], target.at[pl.ds(height, height)], sems.at[1]),
-        pltpu.make_async_copy(albedo.at[:, lanes], target.at[pl.ds(2 * height, 1)], sems.at[2]),
+        pltpu.make_async_copy(
+            depth.at[:, :, lanes], target.at[pl.ds(0, BANDS), levels], sems.at[0]
+        ),
+        pltpu.make_async_copy(
+            ssa.at[:, :, lanes], target.at[pl.ds(BANDS, BANDS), levels], sems.at[1]
+        ),
+        pltpu.make_async_copy(
+            albedo.at[:, lanes], target.at[2 * BANDS, pl.ds(0, 1)], sems.at[2]
+        ),
     ]
 
 
-def edge_kernel(role, low_state, low_kappa, low_near, high_state, high_kappa, high_near, low, high):
-    @pl.when(role[0] != SLOTS - 1)
-    def _():
-        for state, kappa, near, edge in (
-            (low_state, low_kappa, low_near, low), (high_state, high_kappa, high_near, high)
-        ):
-            edge[0:ROWS, :] = state[...]
-            others = [near[n].astype(F32) for n in range(3)]
-            edge[ROWS : ROWS + 8, :] = jnp.concatenate(
-                [kappa[...]] + others + [jnp.zeros((4, LANES), F32)], axis=0
-            )
-
-
-def stage_kernel(
-    role, gas, ext, ssa, ray, solar, aero_depth, aero_ssa, albedo,
-    weights, solar_out, aero_two, staged, sems,
+def first_kernel(
+    role, routes, state, parent, sun, kappa, near, gas, ext, ssa, ray, solar,
+    aero_depth, aero_ssa, albedo,
+    message, slots_out, edge_low, edge_high, weights, solar_out, aero_two, sems,
 ):
     is_last = role[0] == SLOTS - 1
-    tail = (DOMAINS + MOVED) * SLOT_COLS
-    total = (SLOTS - 1) * DOMAINS * SLOT_COLS
-    copies = aerosol_copies(aero_depth, aero_ssa, albedo, staged, total - tail, tail, sems)
-    onward = pltpu.make_async_copy(staged, aero_two, sems.at[3])
+
+    @pl.when(jnp.logical_not(is_last))
+    def _():
+        for edge, start in ((edge_high, CELLS - LANES), (edge_low, 0)):
+            here = slice(start, start + LANES)
+            edge[0:ROWS, :] = state[:, here]
+            others = [near[n, :, here].astype(F32) for n in range(3)]
+            edge[ROWS : ROWS + 8, :] = jnp.concatenate(
+                [kappa[:, here]] + others + [jnp.zeros((4, LANES), F32)], axis=0
+            )
+        pack_columns(routes, state, parent, sun, message, slots_out)
+
+    @pl.when(role[0] == SLOTS - 2)
+    def _():
+        radiation_weights(gas, ext, ssa, ray, solar, weights, solar_out)
 
     @pl.when(is_last)
     def _():
+        tail = (DOMAINS + MOVED) * SLOT_COLS
+        total = (SLOTS - 1) * DOMAINS * SLOT_COLS
+        copies = aerosol_copies(aero_depth, aero_ssa, albedo, aero_two, total - tail, tail, sems)
         for copy in copies:
             copy.start()
-
-    @pl.when(role[0] >= SLOTS - 2)
-    def _():
         radiation_weights(gas, ext, ssa, ray, solar, weights, solar_out)
-
-    @pl.when(is_last)
-    def _():
         for copy in copies:
             copy.wait()
-        onward.start()
-        onward.wait()
-
-
-def coarsen_kernel(role, routes, state, parent, sun, _, message, slots_out):
-    @pl.when(role[0] != SLOTS - 1)
-    def _():
-        pack_columns(routes, state, parent, sun, message, slots_out)
 
 
 def pack_columns(routes, state, parent, sun, message, slots_out):
@@ -145,14 +143,14 @@
     columns = jnp.concatenate([coarse, sun_rows], axis=0)
     placed = ones_where(iota((DOMAINS * SLOT_COLS, COARSE), 0) == place)
     packed = exact_dot(columns, placed, 1)
-    span = ROWS // PER_TILE
     for tile in range(DOMAINS // PER_TILE):
         part = packed[:, tile * LANES : (tile + 1) * LANES]
         for e in range(PER_TILE):
-            pieces = [part[a * span : (a + 1) * span] for a in range(PER_TILE)]
-            message[tile * PER_TILE + e, 0:span, :] = regroup(pieces, lambda a: a - e)
+            first = (tile * PER_TILE + e) * LINES
+            pieces = [part[a * SPAN : (a + 1) * SPAN] for a in range(PER_TILE)]
+            message[first : first + SPAN, :] = regroup(pieces, lambda a: a - e)
             moved = pltpu.roll(part[ROWS:], ((-e) % PER_TILE) * SLOT_COLS, 1) if e else part[ROWS:]
-            message[tile * PER_TILE + e, span : span + 8, :] = moved
+            message[first + SPAN : first + LINES, :] = moved[0:1]
 
 
 def radiation_weights(gas, ext, ssa, ray, solar, weights, solar_out):
@@ -173,7 +171,9 @@
     solar_out[...] = jnp.broadcast_to(column(solar[...]), (GPOINTS, LANES))
 
 
-def diffuse_kernel(role, state, kappa, near, left, right, _, out, fields, rates, goal, chosen):
+def diffuse_kernel(
+    role, state, kappa, near, left, right, _, out, fields, rates, goal, chosen,
+):
     @pl.when(role[0] == SLOTS - 1)
     def _():
         out[...] = jnp.zeros_like(out)
@@ -229,7 +229,7 @@
     steps = pl.num_programs(0)
     is_third, is_last = role[0] == SLOTS - 2, role[0] == SLOTS - 1
     ahead = DOMAINS // UNIT_SENDERS
-    active = is_third | is_last
+    active = is_last | (is_third & (step < ahead + MOVED // UNIT_SENDERS))
 
     def copies(unit, slot):
         two = jnp.where(unit < ahead, unit + MOVED // UNIT_SENDERS, unit - ahead) * UNIT
@@ -238,8 +238,8 @@
             lanes = pl.ds(pl.multiple_of(two + tile * LANES, LANES), LANES)
             third.append(
                 pltpu.make_async_copy(
-                    aero_two.at[:, lanes],
-                    aero.at[slot, tile, pl.ds(0, 2 * BANDS * LEVELS + 8)],
+                    aero_two.at[:, :, lanes],
+                    aero.at[slot, tile, pl.ds(0, 2 * BANDS + 1), pl.ds(0, LEVELS)],
                     sems.at[slot, tile, 0],
                 )
             )
@@ -251,7 +251,7 @@
 
     def begin(unit, slot):
         for chosen, descriptors in copies(unit, slot):
-            @pl.when(chosen)
+            @pl.when(chosen & (is_last | (unit < ahead + MOVED // UNIT_SENDERS)))
             def _():
                 for descriptor in descriptors:
                     descriptor.start()
@@ -270,23 +270,23 @@
         (is_third & (step < ahead), received, 0),
         (is_last & (step < ahead), from_first, 0),
         (is_last & (step >= ahead), from_second, ahead),
-        (is_third & (step >= ahead), from_moved, ahead),
+        (active & is_third & (step >= ahead), from_moved, ahead),
     ):
         @pl.when(chosen)
         def _():
-            profile[...] = ref[pl.ds((step - first) * UNIT_SENDERS, UNIT_SENDERS)]
+            height = UNIT_SENDERS * LINES
+            profile[...] = ref[pl.ds(pl.multiple_of((step - first) * height, 8), height), :]
 
     @pl.when(active)
     def _():
-        span = ROWS // PER_TILE
         for tile in range(UNIT // LANES):
             lanes = slice(tile * LANES, (tile + 1) * LANES)
-            parts = [profile[tile * PER_TILE + e] for e in range(PER_TILE)]
+            starts = [(tile * PER_TILE + e) * LINES for e in range(PER_TILE)]
+            parts = [profile[start : start + SPAN, :] for start in starts]
             for a in range(PER_TILE):
-                pieces = [part[0:span] for part in parts]
-                columns[a * span : (a + 1) * span, lanes] = regroup(pieces, lambda e: e - a)
-            pieces = [part[span : span + 8] for part in parts]
-            columns[ROWS : ROWS + 8, lanes] = regroup(pieces, lambda e: e)
+                columns[a * SPAN : (a + 1) * SPAN, lanes] = regroup(parts, lambda e: e - a)
+            suns = [profile[start + SPAN : start + LINES, :] for start in starts]
+            columns[ROWS : ROWS + 1, lanes] = regroup(suns, lambda e: e)
         for chosen, descriptors in copies(step, slot):
             @pl.when(chosen)
             def _():
@@ -312,6 +312,10 @@
                 late[e] = message
 
 
+def over_groups(x):
+    return x.reshape(x.shape[0] // 8, 8, LANES).sum(axis=0)
+
+
 def radiate(weights, solar, columns, aero, slot, optics, scatter_q, decay, beam, glow, net):
     cosine = columns[ROWS : ROWS + 1, :]
     path = jnp.maximum(cosine, 0.1)
@@ -322,10 +326,10 @@
     spot = iota((16, UNIT), 0)
     half = GPOINTS // 2
 
-    def bands_of(first):
-        tiles = range(UNIT // LANES)
-        rows = pl.ds(first, 16, stride=LEVELS)
-        return jnp.concatenate([aero[slot, tile, rows, :] for tile in tiles], axis=1)
+    def bands_of(band, level):
+        rows = pl.ds(band * PITCH + level, 16, stride=PITCH)
+        tiles = [aero.at[slot, tile].reshape(AERO * PITCH, LANES) for tile in range(UNIT // LANES)]
+        return jnp.concatenate([tile[rows, :] for tile in tiles], axis=1)
 
     def down(block, _):
         first = block * LEVEL_BLOCK
@@ -335,8 +339,8 @@
             vapour = columns[pl.ds(level + LEVELS, 1), :] * scale
             cloud = columns[pl.ds(level + 2 * LEVELS, 1), :] * scale
             hat = jnp.maximum(0.0, 1.0 - jnp.abs(warmth - node)) * vapour
-            depth = bands_of(level) * scale
-            share = depth * bands_of(level + BANDS * LEVELS)
+            depth = bands_of(0, level) * scale
+            share = depth * bands_of(BANDS, level)
             hat_hi, hat_lo = halves(hat)
             opt_hi, opt_lo = halves(
                 jnp.where(spot < BANDS, depth, jnp.where(spot == BANDS, scale, cloud))
@@ -354,6 +358,11 @@
                 straight = beam[rows, lanes]
                 spread = glow[rows, lanes]
                 for j in range(LEVEL_BLOCK):
+                    total = 2.0 * over_groups(straight) + over_groups(spread)
+                    if row == 0:
+                        net[first + j, :, lanes] = total
+                    else:
+                        net[first + j, :, lanes] += total
                     loss = optics[j, rows, lanes]
                     part = optics[j, GPOINTS + row : GPOINTS + row + half, lanes]
                     through = straight * jnp.exp2(loss)
@@ -361,11 +370,6 @@
                     source = (through - straight) * (part * pl.reciprocal(loss, approx=True))
                     scatter_q[first + j, rows, lanes] = source
                     decay[first + j, rows, lanes] = kept
-                    total = (straight + straight + spread).reshape(half // 8, 8, LANES).sum(axis=0)
-                    if row == 0:
-                        net[first + j, :, lanes] = total
-                    else:
-                        net[first + j, :, lanes] += total
                     spread = spread * kept + source
                     straight = through
                 beam[rows, lanes] = straight
@@ -376,24 +380,23 @@
     for lane in range(0, UNIT, LANES):
         lanes = slice(lane, lane + LANES)
         floor = 2.0 * beam[:, lanes] + glow[:, lanes]
-        ground = 2 * BANDS * LEVELS
-        rising = aero[slot, lane // LANES, ground : ground + 1, :] * floor
-        net[LEVELS, :, lanes] = (floor - rising).reshape(GPOINTS // 8, 8, LANES).sum(axis=0)
+        rising = aero[slot, lane // LANES, 2 * BANDS, 0:1, :] * floor
+        net[LEVELS, :, lanes] = over_groups(floor - rising)
 
         def up(i, rising):
-            for k in range(4):
-                level = LEVELS - 1 - (i * 4 + k)
+            for k in range(8):
+                level = LEVELS - 1 - (i * 8 + k)
                 rising = rising * decay[level, :, lanes] + scatter_q[level, :, lanes]
-                net[level, :, lanes] -= rising.reshape(GPOINTS // 8, 8, LANES).sum(axis=0)
+                net[level, :, lanes] -= over_groups(rising)
             return rising
 
-        lax.fori_loop(0, LEVELS // 4, up, rising)
+        lax.fori_loop(0, LEVELS // 8, up, rising)
 
 
 def rad_scratch():
     return [
         pltpu.VMEM((ROWS + 8, UNIT), F32),
-        pltpu.VMEM((2, UNIT // LANES, (2 * BANDS + 2) * LEVELS, LANES), F32),
+        pltpu.VMEM((2, UNIT // LANES, AERO, PITCH, LANES), F32),
         pltpu.VMEM((LEVEL_BLOCK, 2 * GPOINTS, UNIT), F32),
         pltpu.VMEM((LEVELS, GPOINTS, UNIT), F32),
         pltpu.VMEM((LEVELS, GPOINTS, UNIT), F32),
@@ -444,26 +447,32 @@
     near = jnp.transpose(neighbours, (1, 0, 2))
     slot = lax.axis_index("grp").astype(I32).reshape(1)
     last = SLOTS - 1
-    depth = jnp.transpose(aerosol_depth[0], (1, 0, 2)).reshape(BANDS * LEVELS, -1)
-    ssa = jnp.transpose(aerosol_ssa[0], (1, 0, 2)).reshape(BANDS * LEVELS, -1)
-    aero_rows = 2 * BANDS * LEVELS + 8
-
-    def edges(tile):
-        return [
-            pl.BlockSpec((ROWS, LANES), lambda i: (0, tile)),
-            pl.BlockSpec((1, LANES), lambda i: (0, tile)),
-            pl.BlockSpec((3, 1, LANES), lambda i: (0, 0, tile)),
-        ]
-
-    edge_low, edge_high = pl.pallas_call(
-        edge_kernel,
-        grid=(1,),
-        in_specs=[SMEM] + edges(0) + edges(TILES - 1),
-        out_specs=[pl.BlockSpec((ROWS + 8, LANES), lambda i: (0, 0))] * 2,
-        out_shape=[jax.ShapeDtypeStruct((ROWS + 8, LANES), F32)] * 2,
+    depth = jnp.transpose(aerosol_depth[0], (1, 0, 2))
+    ssa = jnp.transpose(aerosol_ssa[0], (1, 0, 2))
+
+    message, places, edge_low, edge_high, weights, solar, aero_two = pl.pallas_call(
+        first_kernel,
+        in_specs=[SMEM, SMEM] + [VMEM] * 10 + [HBM] * 3,
+        out_specs=[VMEM] * 7,
+        out_shape=[
+            jax.ShapeDtypeStruct((DOMAINS * LINES, LANES), F32),
+            jax.ShapeDtypeStruct((1, COARSE), I32),
+            jax.ShapeDtypeStruct((ROWS + 8, LANES), F32),
+            jax.ShapeDtypeStruct((ROWS + 8, LANES), F32),
+            jax.ShapeDtypeStruct((2 * GPOINTS, 176), BF16),
+            jax.ShapeDtypeStruct((GPOINTS, LANES), F32),
+            pltpu.VMEM((2 * BANDS + 1, LEVELS, (DOMAINS + MOVED) * SLOT_COLS), F32),
+        ],
+        scratch_shapes=[pltpu.SemaphoreType.DMA((3,))],
         compiler_params=params(),
-        name="edge",
-    )(slot, far(fields), far(kappa), far(near), far(fields), far(kappa), far(near))
+        name="first",
+    )(
+        slot, far(jnp.transpose(routes, (0, 2, 1))), far(fields), far(parent), far(cos_zenith),
+        far(kappa), far(near), far(gas_table.T), far(cloud_ext[None]), far(cloud_ssa[None]),
+        far(rayleigh[None]), far(solar_weight[None]), far(depth), far(ssa), far(rad_albedo),
+    )
+    aero_two = lax.ppermute(aero_two, "grp", [(last, last - 1)])
+
     forward = [
         (s * DOMAINS + i, s * DOMAINS + (i + 1) % DOMAINS) for s in range(last) for i in range(DOMAINS)
     ]
@@ -471,42 +480,12 @@
     left = lax.ppermute(edge_high, ("grp", "dom"), forward)
     right = lax.ppermute(edge_low, ("grp", "dom"), backward)
 
-    weights, solar, aero_two = pl.pallas_call(
-        stage_kernel,
-        in_specs=[SMEM] + [VMEM] * 5 + [HBM] * 3,
-        out_specs=[VMEM] * 2 + [HBM],
-        out_shape=[
-            jax.ShapeDtypeStruct((2 * GPOINTS, 176), BF16),
-            jax.ShapeDtypeStruct((GPOINTS, LANES), F32),
-            jax.ShapeDtypeStruct((aero_rows, (DOMAINS + MOVED) * SLOT_COLS), F32),
-        ],
-        scratch_shapes=[
-            pltpu.VMEM((aero_rows, (DOMAINS + MOVED) * SLOT_COLS), F32),
-            pltpu.SemaphoreType.DMA((4,)),
-        ],
-        compiler_params=params(),
-        name="stage",
-    )(
-        slot, far(gas_table.T), far(cloud_ext[None]), far(cloud_ssa[None]), far(rayleigh[None]),
-        far(solar_weight[None]), far(depth), far(ssa), far(rad_albedo),
-    )
-    aero_two = lax.ppermute(aero_two, "grp", [(last, last - 1)])
-
-    message, places = pl.pallas_call(
-        coarsen_kernel,
-        in_specs=[SMEM, SMEM] + [VMEM] * 3 + [HBM],
-        out_specs=[VMEM] * 2,
-        out_shape=[
-            jax.ShapeDtypeStruct((DOMAINS, 32, LANES), F32),
-            jax.ShapeDtypeStruct((1, COARSE), I32),
-        ],
-        compiler_params=params(),
-        name="coarsen",
-    )(slot, far(jnp.transpose(routes, (0, 2, 1))), far(fields), far(parent), far(cos_zenith), weights)
-    received = lax.all_to_all(message, "dom", 0, 0, tiled=True)
+    received = lax.all_to_all(
+        message.reshape(DOMAINS, 1, LINES * LANES), "dom", 0, 0, tiled=True
+    ).reshape(DOMAINS * LINES, LANES)
     from_first = lax.ppermute(received, "grp", [(0, last)])
-    from_second = lax.ppermute(received[:STAY], "grp", [(1, last)])
-    from_moved = lax.ppermute(received[STAY:], "grp", [(1, 2)])
+    from_second = lax.ppermute(received[: STAY * LINES], "grp", [(1, last)])
+    from_moved = lax.ppermute(received[STAY * LINES :], "grp", [(1, 2)])
 
     ahead = DOMAINS // UNIT_SENDERS
     units = ahead + STAY // UNIT_SENDERS
@@ -530,7 +509,7 @@
                 ),
             ],
             scratch_shapes=[
-                pltpu.VMEM((UNIT_SENDERS, 32, LANES), F32),
+                pltpu.VMEM((UNIT_SENDERS * LINES, LANES), F32),
                 *rad_scratch(),
                 pltpu.SemaphoreType.DMA((2, UNIT // LANES, 3)),
             ],
@@ -566,7 +545,7 @@
     to_first = lax.ppermute(early, "grp", [(last, 0)])
     to_second = lax.ppermute(late, "grp", [(last, 1)])
     moved_back = lax.ppermute(late, "grp", [(2, 1)])
-    away = to_first + jnp.concatenate([to_second, moved_back], axis=0)
+    away = to_first + jnp.concatenate([to_second, moved_back[:MOVED]], axis=0)
     returning = jnp.where(slot[0] == last - 1, early, away)
     mine = lax.all_to_all(returning, "dom", 0, 0, tiled=True)
 

time: 97.8 us -> 92.2 us (0.943)
  starting transfers between devices: 27.3 us -> 24.7 us
  Pallas kernels: 12.5 us -> 11.1 us
    ppermute x1, waiting for transfers between devices: 0.01 us -> 5.55 us  [per_device(): to_second = lax.ppermute(late, 'grp', [(last, 1)])]
    ppermute x1, waiting for transfers between devices: 25.1 us -> 19.8 us  [per_device(): moved_back = lax.ppermute(late, 'grp', [(2, 1)])]
    pallas_call x3 -> x1, Pallas kernels: 4.4 us -> 2.84 us  [per_device(): pl.pallas_call(first_kernel, in_specs=[SMEM, SMEM] + [VMEM] * 10 + [HBM]...]
    ppermute x1, waiting for transfers between devices: 7.97 us -> 6.46 us  [per_device(): left = lax.ppermute(edge_high, ('grp', 'dom'), forward)]
    ppermute x1, starting transfers between devices: 4.64 us -> 3.22 us  [per_device(): right = lax.ppermute(edge_low, ('grp', 'dom'), backward)]
  transfers between devices with their start and end apart: 10 -> 10, of which waited for: 4 -> 5; matrix products, arithmetic and copies ran while one was open for 0% -> 0% of each run, Pallas kernels for 9% -> 5%
where the time goes in v3:
time: 92.2 us; the launch traced here: 91.8 us
  waiting for transfers between devices  36.4 us (39%)
  starting transfers between devices  24.7 us (27%)
  blocking collectives  18.8 us (20%)
  Pallas kernels  11.1 us (12%)
    ppermute x1, waiting for transfers between devices, per_device(): moved_back = lax.ppermute(late, 'grp', [(2, 1)])  19.8 us
    all_to_all x1, blocking collectives, per_device(): lax.all_to_all(message.reshape(DOMAINS, 1, LINES * LANES), 'dom', 0, 0, t...  18.8 us
    ppermute x1, starting transfers between devices, per_device(): from_second = lax.ppermute(received[:STAY * LINES], 'grp', [(1, last)])  9.19 us
    ppermute x1, waiting for transfers between devices, per_device(): left = lax.ppermute(edge_high, ('grp', 'dom'), forward)  6.46 us
    ppermute x1, waiting for transfers between devices, per_device(): to_second = lax.ppermute(late, 'grp', [(last, 1)])  5.55 us
    pallas_call x1, Pallas kernels, per_device(): pl.pallas_call(diffuse_kernel, in_specs=[SMEM] + [VMEM] * 5 + [HBM], out_...  4.93 us
    all_to_all x1, starting transfers between devices, per_device(): mine = lax.all_to_all(returning, 'dom', 0, 0, tiled=True)  4.16 us
    ppermute x1, starting transfers between devices, per_device(): right = lax.ppermute(edge_low, ('grp', 'dom'), backward)  3.22 us
  transfers between devices with their start and end apart: 10, of which 5 were waited for; matrix products, arithmetic and copies ran while one was open for 0% of the time, Pallas kernels for 5%

profile of v3, /device:TPU:1, one launch (start us, length us, event | category | flops | bytes accessed | tf_op | source)
XLA Modules:
  0.0 91.8 jit_solution(9065852363307218530)
XLA Ops:
  0.0 2.8 %first.1 = (f32[800,128]{1,0:T(8,128)S(1)}, s32[1,512]{1,0:T(1,128)S(1)}, f32[104,128]{1,0:T(8,128)S(1)}, f32[104,128]{1,0:T(8,128)S(1)}, bf16[224,176]{1,0:T(8,...) custom-call(s32[1]{0:T(128)} %bitcast.role, s32[1,1,32]{2,1,0:T(1,128)} %bitcast.34, ...), custom_call_target="tpu_custom_call" | custom-call | tf_op jit(solution)/shard_map/first/pallas_call | solution.py:453
  2.8 1.0 %collective-permute-start.5 = (f32[29,32,1280]{2,1,0:T(8,128)S(1)}, f32[29,32,1280]{2,1,0:T(8,128)S(1)}, u32[]{:S(2)}, u32[]{:S(2)}) collective-permute-start(f32[29,32,1280]{2,1,0:T(8,128)S(1)} %get-tuple-element.19), channel_id=1, source_target_pairs={{96,64},{97,65},{98,66},{99,67},{100,68},{101,69},{102,70},{103,71... | collective-permute-start | bytes 14254088 | tf_op jit(solution)/shard_map/ppermute | solution.py:474
  3.8 18.8 %all_to_all.10 = f32[32,1,3200]{2,1,0:T(1,128)S(1)} all-to-all(f32[32,1,3200]{2,1,0:T(1,128)S(1)} %bitcast.22), channel_id=1, replica_groups=mesh['grp'=4,'dom'=32] {'dom'}, dimensions={0} | all-to-all | bytes 819200 | tf_op jit(solution)/shard_map/all_to_all | solution.py:483
  22.6 0.7 collective-permute-start
  23.3 9.2 %collective-permute-start.1 = (f32[600,128]{1,0:T(8,128)S(1)}, f32[600,128]{1,0:T(8,128)S(1)}, u32[]{:S(2)}, u32[]{:S(2)}) collective-permute-start(f32[600,128]{1,0:T(8,128)S(1)} %bitcast.29), channel_id=1, source_target_pairs={{32,96},{33,97},{34,98},{35,99},{36,100},{37,101},{38,102},{39,103... | collective-permute-start | bytes 921608 | tf_op jit(solution)/shard_map/ppermute | solution.py:487
  32.5 1.9 %collective-permute-start.3 = (f32[104,128]{1,0:T(8,128)S(1)}, f32[104,128]{1,0:T(8,128)S(1)}, u32[]{:S(2)}, u32[]{:S(2)}) collective-permute-start(f32[104,128]{1,0:T(8,128)S(1)} %get-tuple-element.17), channel_id=1, source_target_pairs={{0,1},{1,2},{2,3},{3,4},{4,5},{5,6},{6,7},{7,8},{8,9},{9,10},{10,1... | collective-permute-start | bytes 159752 | tf_op jit(solution)/shard_map/ppermute | solution.py:480
  34.5 1.3 %collective-permute-start.2 = (f32[200,128]{1,0:T(8,128)S(1)}, f32[200,128]{1,0:T(8,128)S(1)}, u32[]{:S(2)}, u32[]{:S(2)}) collective-permute-start(f32[200,128]{1,0:T(8,128)S(1)} %bitcast.30), channel_id=1, source_target_pairs={{32,64},{33,65},{34,66},{35,67},{36,68},{37,69},{38,70},{39,71},{4... | collective-permute-start | bytes 307208 | tf_op jit(solution)/shard_map/ppermute | solution.py:488
  35.8 6.5 %collective-permute-done.3._left.left = f32[104,128]{1,0:T(8,128)S(1)} collective-permute-done((f32[104,128]{1,0:T(8,128)S(1)}, f32[104,128]{1,0:T(8,128)S(1)}, u32[]{:S(2)}, u32[]{:S(2)}) %collective-permute-start.3) | collective-permute-done | bytes 53280 | tf_op jit(solution)/shard_map/ppermute | solution.py:480
  42.2 3.2 %collective-permute-start.4 = (f32[104,128]{1,0:T(8,128)S(1)}, f32[104,128]{1,0:T(8,128)S(1)}, u32[]{:S(2)}, u32[]{:S(2)}) collective-permute-start(f32[104,128]{1,0:T(8,128)S(1)} %get-tuple-element.18), channel_id=1, source_target_pairs={{1,0},{2,1},{3,2},{4,3},{5,4},{6,5},{7,6},{8,7},{9,8},{10,9},{11,1... | collective-permute-start | bytes 159752 | tf_op jit(solution)/shard_map/ppermute | solution.py:481
  45.5 1.6 %collective-permute-done.4._right.right = f32[104,128]{1,0:T(8,128)S(1)} collective-permute-done((f32[104,128]{1,0:T(8,128)S(1)}, f32[104,128]{1,0:T(8,128)S(1)}, u32[]{:S(2)}, u32[]{:S(2)}) %collective-permute-start.4) | collective-permute-done | bytes 53280 | tf_op jit(solution)/shard_map/ppermute | solution.py:481
  47.1 0.0 collective-permute-done.2.from_moved
  47.1 0.0 collective-permute-done.1.from_second
  47.1 0.0 collective-permute-done.from_first
  47.1 0.0 collective-permute-done.5.aero_two
  47.1 0.7 radiation.1
  47.8 0.7 collective-permute-start.6
  48.5 1.3 %collective-permute-start.8 = (f32[24,8,128]{2,1,0:T(8,128)S(1)}, f32[24,8,128]{2,1,0:T(8,128)S(1)}, u32[]{:S(2)}, u32[]{:S(2)}) collective-permute-start(f32[24,8,128]{2,1,0:T(8,128)S(1)} %get-tuple-element.21), channel_id=1, source_target_pairs={{64,32},{65,33},{66,34},{67,35},{68,36},{69,37},{70,38},{71,39},{7... | collective-permute-start | bytes 294920 | tf_op jit(solution)/shard_map/ppermute | solution.py:547
  49.8 1.3 %collective-permute-start.7 = (f32[24,8,128]{2,1,0:T(8,128)S(1)}, f32[24,8,128]{2,1,0:T(8,128)S(1)}, u32[]{:S(2)}, u32[]{:S(2)}) collective-permute-start(f32[24,8,128]{2,1,0:T(8,128)S(1)} %get-tuple-element.21), channel_id=1, source_target_pairs={{96,32},{97,33},{98,34},{99,35},{100,36},{101,37},{102,38},{103,39... | collective-permute-start | bytes 294920 | tf_op jit(solution)/shard_map/ppermute | solution.py:546
  51.1 19.8 %collective-permute-done.8 = f32[24,8,128]{2,1,0:T(8,128)S(1)} collective-permute-done((f32[24,8,128]{2,1,0:T(8,128)S(1)}, f32[24,8,128]{2,1,0:T(8,128)S(1)}, u32[]{:S(2)}, u32[]{:S(2)}) %collective-permute-start.8) | collective-permute-done | bytes 98336 | tf_op jit(solution)/shard_map/ppermute | solution.py:547
  70.9 5.5 %collective-permute-done.7 = f32[24,8,128]{2,1,0:T(8,128)S(1)} collective-permute-done((f32[24,8,128]{2,1,0:T(8,128)S(1)}, f32[24,8,128]{2,1,0:T(8,128)S(1)}, u32[]{:S(2)}, u32[]{:S(2)}) %collective-permute-start.7) | collective-permute-done | bytes 98336 | tf_op jit(solution)/shard_map/ppermute | solution.py:546
  76.5 0.0 collective-permute-done.6
  76.5 0.7 fusion
  77.2 4.2 %all-to-all-start.1 = ((f32[32,8,128]{2,1,0:T(8,128)}), f32[32,8,128]{2,1,0:T(8,128)S(1)}, u32[]{:S(2)}, u32[]{:S(2)}) async-start(f32[32,8,128]{2,1,0:T(8,128)} %fusion), calls=%async_computation.1 | async-start | bytes 262144 | tf_op jit(solution)/shard_map/all_to_all | solution.py:550
  81.3 4.9 %diffuse.1.stepped = f32[96,2048]{1,0:T(8,128)} custom-call(s32[1]{0:T(128)} %bitcast.role, f32[96,2048]{1,0:T(8,128)} %bitcast.28, f32[1,2048]{1,0:T(1,128)} %kappa.3, s32[3,1,2048]{2,1,0:T(1,128)} %bitcast.32, f32[104,128]{1,0:T(8,128)S(1)} %collective-permute-done.3._left.left, f32[104,128]{1,0:T(8,128)S(1)} %collective-permute-done.4._right.right, ...), custom_call_target="tpu_custom_call" | custom-call | tf_op jit(solution)/shard_map/diffuse/pallas_call | solution.py:530
  86.3 3.0 %all-to-all-done.1.mine = f32[32,8,128]{2,1,0:T(8,128)S(1)} async-done(((f32[32,8,128]{2,1,0:T(8,128)}), f32[32,8,128]{2,1,0:T(8,128)S(1)}, u32[]{:S(2)}, u32[]{:S(2)}) %all-to-all-start.1) | async-done | bytes 131104 | tf_op jit(solution)/shard_map/all_to_all | solution.py:550
  89.2 2.6 %warm.1 = f32[96,2048]{1,0:T(8,128)} custom-call(s32[1]{0:T(128)} %bitcast.role, f32[32,8,128]{2,1,0:T(8,128)S(1)} %all-to-all-done.1.mine, s32[1,2048]{1,0:T(1,128)} %parent.3, s32[1,512]{1,0:T(1,128)S(1)} %get-tuple-element.22.slots_in, f32[96,2048]{1,0:T(8,128)} %diffuse.1.stepped), custom_call_target="tpu_custom_call", output_to_operand_aliasing={{}: (4, {})} | custom-call | tf_op jit(solution)/shard_map/warm/pallas_call | solution.py:552
  (3 shorter events, 0.0 us)
Async XLA Ops:
  2.8 44.3 %collective-permute-start.5 = (f32[29,32,1280]{2,1,0:T(8,128)S(1)}, f32[29,32,1280]{2,1,0:T(8,128)S(1)}, u32[]{:S(2)}, u32[]{:S(2)}) collective-permute-start(f32[29,32,1280]{2,1,0:T(8,128)S(1)} %get-tuple-element.19), channel_id=1, source_target_pairs={{96,64},{97,65},{98,66},{99,67},{100,68},{101,69},{102,70},{103,71... | collective-permute-start | bytes 14254088 | tf_op jit(solution)/shard_map/ppermute | solution.py:474
  22.6 24.5 %collective-permute-start = (f32[800,128]{1,0:T(8,128)S(1)}, f32[800,128]{1,0:T(8,128)S(1)}, u32[]{:S(2)}, u32[]{:S(2)}) collective-permute-start(f32[800,128]{1,0:T(8,128)S(1)} %bitcast.20), channel_id=1, source_target_pairs={{0,96},{1,97},{2,98},{3,99},{4,100},{5,101},{6,102},{7,103},{8,104... | collective-permute-start | bytes 1228808 | tf_op jit(solution)/shard_map/ppermute | solution.py:486
  23.3 23.8 %collective-permute-start.1 = (f32[600,128]{1,0:T(8,128)S(1)}, f32[600,128]{1,0:T(8,128)S(1)}, u32[]{:S(2)}, u32[]{:S(2)}) collective-permute-start(f32[600,128]{1,0:T(8,128)S(1)} %bitcast.29), channel_id=1, source_target_pairs={{32,96},{33,97},{34,98},{35,99},{36,100},{37,101},{38,102},{39,103... | collective-permute-start | bytes 921608 | tf_op jit(solution)/shard_map/ppermute | solution.py:487
  32.5 9.7 %collective-permute-start.3 = (f32[104,128]{1,0:T(8,128)S(1)}, f32[104,128]{1,0:T(8,128)S(1)}, u32[]{:S(2)}, u32[]{:S(2)}) collective-permute-start(f32[104,128]{1,0:T(8,128)S(1)} %get-tuple-element.17), channel_id=1, source_target_pairs={{0,1},{1,2},{2,3},{3,4},{4,5},{5,6},{6,7},{7,8},{8,9},{9,10},{10,1... | collective-permute-start | bytes 159752 | tf_op jit(solution)/shard_map/ppermute | solution.py:480
  34.5 12.6 %collective-permute-start.2 = (f32[200,128]{1,0:T(8,128)S(1)}, f32[200,128]{1,0:T(8,128)S(1)}, u32[]{:S(2)}, u32[]{:S(2)}) collective-permute-start(f32[200,128]{1,0:T(8,128)S(1)} %bitcast.30), channel_id=1, source_target_pairs={{32,64},{33,65},{34,66},{35,67},{36,68},{37,69},{38,70},{39,71},{4... | collective-permute-start | bytes 307208 | tf_op jit(solution)/shard_map/ppermute | solution.py:488
  42.2 4.9 %collective-permute-start.4 = (f32[104,128]{1,0:T(8,128)S(1)}, f32[104,128]{1,0:T(8,128)S(1)}, u32[]{:S(2)}, u32[]{:S(2)}) collective-permute-start(f32[104,128]{1,0:T(8,128)S(1)} %get-tuple-element.18), channel_id=1, source_target_pairs={{1,0},{2,1},{3,2},{4,3},{5,4},{6,5},{7,6},{8,7},{9,8},{10,9},{11,1... | collective-permute-start | bytes 159752 | tf_op jit(solution)/shard_map/ppermute | solution.py:481
  47.8 28.7 %collective-permute-start.6 = (f32[32,8,128]{2,1,0:T(8,128)S(1)}, f32[32,8,128]{2,1,0:T(8,128)S(1)}, u32[]{:S(2)}, u32[]{:S(2)}) collective-permute-start(f32[32,8,128]{2,1,0:T(8,128)S(1)} %get-tuple-element.20._), channel_id=1, source_target_pairs={{96,0},{97,1},{98,2},{99,3},{100,4},{101,5},{102,6},{103,7},{104,8... | collective-permute-start | bytes 393224 | tf_op jit(solution)/shard_map/ppermute | solution.py:545
  48.5 22.4 %collective-permute-start.8 = (f32[24,8,128]{2,1,0:T(8,128)S(1)}, f32[24,8,128]{2,1,0:T(8,128)S(1)}, u32[]{:S(2)}, u32[]{:S(2)}) collective-permute-start(f32[24,8,128]{2,1,0:T(8,128)S(1)} %get-tuple-element.21), channel_id=1, source_target_pairs={{64,32},{65,33},{66,34},{67,35},{68,36},{69,37},{70,38},{71,39},{7... | collective-permute-start | bytes 294920 | tf_op jit(solution)/shard_map/ppermute | solution.py:547
  49.8 26.7 %collective-permute-start.7 = (f32[24,8,128]{2,1,0:T(8,128)S(1)}, f32[24,8,128]{2,1,0:T(8,128)S(1)}, u32[]{:S(2)}, u32[]{:S(2)}) collective-permute-start(f32[24,8,128]{2,1,0:T(8,128)S(1)} %get-tuple-element.21), channel_id=1, source_target_pairs={{96,32},{97,33},{98,34},{99,35},{100,36},{101,37},{102,38},{103,39... | collective-permute-start | bytes 294920 | tf_op jit(solution)/shard_map/ppermute | solution.py:546
  77.2 12.1 %all-to-all-start.1 = ((f32[32,8,128]{2,1,0:T(8,128)}), f32[32,8,128]{2,1,0:T(8,128)S(1)}, u32[]{:S(2)}, u32[]{:S(2)}) async-start(f32[32,8,128]{2,1,0:T(8,128)} %fusion), calls=%async_computation.1 | async-start | bytes 262144 | tf_op jit(solution)/shard_map/all_to_all | solution.py:550

commit v4 on v3

--- a/solution.py
+++ b/solution.py
@@ -22,8 +22,10 @@
 TILES = CELLS // LANES
 UNIT = 256
 UNIT_SENDERS = UNIT // SLOT_COLS
-STAY = 24
+STAY = 16
 MOVED = DOMAINS - STAY
+SOON = max(STAY, MOVED) // UNIT_SENDERS
+LATER = DOMAINS // UNIT_SENDERS
 LEVEL_BLOCK = 8
 AERO = 2 * BANDS + 2
 PITCH = LEVELS + 8
@@ -94,19 +96,23 @@
 def first_kernel(
     role, routes, state, parent, sun, kappa, near, gas, ext, ssa, ray, solar,
     aero_depth, aero_ssa, albedo,
-    message, slots_out, edge_low, edge_high, weights, solar_out, aero_two, sems,
+    message, slots_out, edge_pair, edge_next, weights, solar_out, aero_two, sems,
 ):
     is_last = role[0] == SLOTS - 1
 
     @pl.when(jnp.logical_not(is_last))
     def _():
-        for edge, start in ((edge_high, CELLS - LANES), (edge_low, 0)):
-            here = slice(start, start + LANES)
-            edge[0:ROWS, :] = state[:, here]
-            others = [near[n, :, here].astype(F32) for n in range(3)]
-            edge[ROWS : ROWS + 8, :] = jnp.concatenate(
-                [kappa[:, here]] + others + [jnp.zeros((4, LANES), F32)], axis=0
-            )
+        for parity, above, below in ((0, edge_pair, edge_next), (1, edge_next, edge_pair)):
+            @pl.when(role[1] == parity)
+            def _():
+                for edge, start in ((above, CELLS - LANES), (below, 0)):
+                    here = slice(start, start + LANES)
+                    edge[0:ROWS, :] = state[:, here]
+                    others = [near[n, :, here].astype(F32) for n in range(3)]
+                    edge[ROWS : ROWS + 8, :] = jnp.concatenate(
+                        [kappa[:, here]] + others + [jnp.zeros((4, LANES), F32)], axis=0
+                    )
+
         pack_columns(routes, state, parent, sun, message, slots_out)
 
     @pl.when(role[0] == SLOTS - 2)
@@ -115,9 +121,8 @@
 
     @pl.when(is_last)
     def _():
-        tail = (DOMAINS + MOVED) * SLOT_COLS
-        total = (SLOTS - 1) * DOMAINS * SLOT_COLS
-        copies = aerosol_copies(aero_depth, aero_ssa, albedo, aero_two, total - tail, tail, sems)
+        start, count = DOMAINS * SLOT_COLS, (DOMAINS + STAY) * SLOT_COLS
+        copies = aerosol_copies(aero_depth, aero_ssa, albedo, aero_two, start, count, sems)
         for copy in copies:
             copy.start()
         radiation_weights(gas, ext, ssa, ray, solar, weights, solar_out)
@@ -172,7 +177,7 @@
 
 
 def diffuse_kernel(
-    role, state, kappa, near, left, right, _, out, fields, rates, goal, chosen,
+    role, state, kappa, near, of_pair, of_next, _, out, fields, rates, goal, chosen,
 ):
     @pl.when(role[0] == SLOTS - 1)
     def _():
@@ -180,13 +185,15 @@
 
     @pl.when(role[0] != SLOTS - 1)
     def _():
-        for ref, start, width, shift in (
-            (left, 0, LANES, LANES - HALO - CELLS),
-            (right, LANES + CELLS, LANES, LANES - HALO + CELLS),
+        even = role[1] == 0
+        for edge, start, shift in (
+            (jnp.where(even, of_next[...], of_pair[...]), 0, LANES - HALO - CELLS),
+            (jnp.where(even, of_pair[...], of_next[...]), LANES + CELLS, LANES - HALO + CELLS),
         ):
-            fields[:, start : start + width] = ref[0:ROWS, :]
-            rates[:, start : start + width] = ref[ROWS : ROWS + 1, :]
-            goal[0:3, start : start + width] = ref[ROWS + 1 : ROWS + 4, :].astype(I32) + shift
+            here = slice(start, start + LANES)
+            fields[:, here] = edge[0:ROWS]
+            rates[:, here] = edge[ROWS : ROWS + 1]
+            goal[0:3, here] = edge[ROWS + 1 : ROWS + 4].astype(I32) + shift
         fields[:, LANES : LANES + CELLS] = state[...]
         rates[:, LANES : LANES + CELLS] = kappa[...]
         for n in range(3):
@@ -220,38 +227,62 @@
             out[:, (tile - 1) * LANES : tile * LANES] = value
 
 
-def radiation_kernel(
-    role, weights, solar, received, from_first, from_second, from_moved, _left, _right, depth, ssa, albedo,
-    aero_two, early, late,
+def soon_kernel(
+    role, weights, solar, received, from_third, depth, ssa, albedo, aero_two, out, *scratch
+):
+    is_third, is_last = role[0] == SLOTS - 2, role[0] == SLOTS - 1
+    radiate_unit(
+        (is_third, received, STAY // UNIT_SENDERS, DOMAINS // UNIT_SENDERS),
+        (is_last, from_third, MOVED // UNIT_SENDERS, (2 * DOMAINS + STAY) // UNIT_SENDERS),
+        weights, solar, depth, ssa, albedo, aero_two, out, *scratch,
+    )
+
+
+def later_kernel(
+    role, weights, solar, arrived, _pair, _next, _soon, depth, ssa, albedo, aero_two, out, *scratch
+):
+    is_third, is_last = role[0] == SLOTS - 2, role[0] == SLOTS - 1
+    radiate_unit(
+        (is_third, arrived, LATER, 0), (is_last, arrived, LATER, 0),
+        weights, solar, depth, ssa, albedo, aero_two, out, *scratch,
+    )
+
+
+def radiate_unit(
+    third, last, weights, solar, depth, ssa, albedo, aero_two, out,
     profile, columns, aero, optics, scatter_q, decay, beam, glow, net, sems,
 ):
     step = pl.program_id(0)
     steps = pl.num_programs(0)
-    is_third, is_last = role[0] == SLOTS - 2, role[0] == SLOTS - 1
-    ahead = DOMAINS // UNIT_SENDERS
-    active = is_last | (is_third & (step < ahead + MOVED // UNIT_SENDERS))
+    is_third, third_profiles, third_units, third_first = third
+    is_last, last_profiles, last_units, last_first = last
+
+    def taken(unit):
+        return (is_third & (unit < third_units)) | (is_last & (unit < last_units))
+
+    active = taken(step)
 
     def copies(unit, slot):
-        two = jnp.where(unit < ahead, unit + MOVED // UNIT_SENDERS, unit - ahead) * UNIT
-        third, fourth = [], []
+        here, there = [], []
         for tile in range(UNIT // LANES):
-            lanes = pl.ds(pl.multiple_of(two + tile * LANES, LANES), LANES)
-            third.append(
+            offset = tile * LANES
+            lanes = pl.ds(pl.multiple_of((third_first + unit) * UNIT + offset, LANES), LANES)
+            here.append(
                 pltpu.make_async_copy(
                     aero_two.at[:, :, lanes],
                     aero.at[slot, tile, pl.ds(0, 2 * BANDS + 1), pl.ds(0, LEVELS)],
                     sems.at[slot, tile, 0],
                 )
             )
-            fourth += aerosol_copies(
+            there += aerosol_copies(
                 depth, ssa, albedo, aero.at[slot, tile],
-                pl.multiple_of(unit * UNIT + tile * LANES, LANES), LANES, sems.at[slot, tile],
+                pl.multiple_of((last_first + unit) * UNIT + offset, LANES), LANES, sems.at[slot, tile],
             )
-        return (is_third, third), (is_last, fourth)
+        return (is_third, here), (is_last, there)
 
     def begin(unit, slot):
         for chosen, descriptors in copies(unit, slot):
-            @pl.when(chosen & (is_last | (unit < ahead + MOVED // UNIT_SENDERS)))
+            @pl.when(chosen & taken(unit))
             def _():
                 for descriptor in descriptors:
                     descriptor.start()
@@ -266,16 +297,11 @@
     def _():
         begin(step + 1, 1 - slot)
 
-    for chosen, ref, first in (
-        (is_third & (step < ahead), received, 0),
-        (is_last & (step < ahead), from_first, 0),
-        (is_last & (step >= ahead), from_second, ahead),
-        (active & is_third & (step >= ahead), from_moved, ahead),
-    ):
-        @pl.when(chosen)
+    for chosen, ref in ((is_third, third_profiles), (is_last, last_profiles)):
+        @pl.when(chosen & active)
         def _():
             height = UNIT_SENDERS * LINES
-            profile[...] = ref[pl.ds(pl.multiple_of((step - first) * height, 8), height), :]
+            profile[...] = ref[pl.ds(pl.multiple_of(step * height, 8), height), :]
 
     @pl.when(active)
     def _():
@@ -301,15 +327,8 @@
             pieces = [part[a * span : (a + 1) * span] for a in range(PER_TILE)]
             messages += [regroup(pieces, lambda a: a - e) for e in range(PER_TILE)]
 
-        @pl.when(step < ahead)
-        def _():
-            for e, message in enumerate(messages):
-                early[e] = message
-
-        @pl.when(step >= ahead)
-        def _():
-            for e, message in enumerate(messages):
-                late[e] = message
+        for e, message in enumerate(messages):
+            out[e] = message
 
 
 def over_groups(x):
@@ -445,12 +464,12 @@
 ):
     fields = state.reshape(ROWS, CELLS)
     near = jnp.transpose(neighbours, (1, 0, 2))
-    slot = lax.axis_index("grp").astype(I32).reshape(1)
+    slot = jnp.stack([lax.axis_index("grp"), lax.axis_index("dom") % 2]).astype(I32)
     last = SLOTS - 1
     depth = jnp.transpose(aerosol_depth[0], (1, 0, 2))
     ssa = jnp.transpose(aerosol_ssa[0], (1, 0, 2))
 
-    message, places, edge_low, edge_high, weights, solar, aero_two = pl.pallas_call(
+    message, places, edge_pair, edge_next, weights, solar, aero_two = pl.pallas_call(
         first_kernel,
         in_specs=[SMEM, SMEM] + [VMEM] * 10 + [HBM] * 3,
         out_specs=[VMEM] * 7,
@@ -461,7 +480,7 @@
             jax.ShapeDtypeStruct((ROWS + 8, LANES), F32),
             jax.ShapeDtypeStruct((2 * GPOINTS, 176), BF16),
             jax.ShapeDtypeStruct((GPOINTS, LANES), F32),
-            pltpu.VMEM((2 * BANDS + 1, LEVELS, (DOMAINS + MOVED) * SLOT_COLS), F32),
+            pltpu.VMEM((2 * BANDS + 1, LEVELS, (DOMAINS + STAY) * SLOT_COLS), F32),
         ],
         scratch_shapes=[pltpu.SemaphoreType.DMA((3,))],
         compiler_params=params(),
@@ -473,57 +492,52 @@
     )
     aero_two = lax.ppermute(aero_two, "grp", [(last, last - 1)])
 
-    forward = [
-        (s * DOMAINS + i, s * DOMAINS + (i + 1) % DOMAINS) for s in range(last) for i in range(DOMAINS)
-    ]
-    backward = [(target, source) for source, target in forward]
-    left = lax.ppermute(edge_high, ("grp", "dom"), forward)
-    right = lax.ppermute(edge_low, ("grp", "dom"), backward)
-
     received = lax.all_to_all(
         message.reshape(DOMAINS, 1, LINES * LANES), "dom", 0, 0, tiled=True
     ).reshape(DOMAINS * LINES, LANES)
-    from_first = lax.ppermute(received, "grp", [(0, last)])
-    from_second = lax.ppermute(received[: STAY * LINES], "grp", [(1, last)])
-    from_moved = lax.ppermute(received[STAY * LINES :], "grp", [(1, 2)])
-
-    ahead = DOMAINS // UNIT_SENDERS
-    units = ahead + STAY // UNIT_SENDERS
-
-    early, late = pl.pallas_call(
-        radiation_kernel,
-        grid_spec=pltpu.PrefetchScalarGridSpec(
-            num_scalar_prefetch=1,
-            grid=(units,),
-            in_specs=[
-                pl.BlockSpec((2 * GPOINTS, 176), lambda i, role: (0, 0)),
-                pl.BlockSpec((GPOINTS, LANES), lambda i, role: (0, 0)),
-                VMEM, VMEM, VMEM, VMEM, VMEM, VMEM, HBM, HBM, HBM, VMEM,
-            ],
-            out_specs=[
-                pl.BlockSpec(
-                    (UNIT_SENDERS, 8, LANES), lambda i, role: (jnp.minimum(i, ahead - 1), 0, 0)
-                ),
-                pl.BlockSpec(
-                    (UNIT_SENDERS, 8, LANES), lambda i, role: (jnp.maximum(i - ahead, 0), 0, 0)
-                ),
-            ],
-            scratch_shapes=[
-                pltpu.VMEM((UNIT_SENDERS * LINES, LANES), F32),
-                *rad_scratch(),
-                pltpu.SemaphoreType.DMA((2, UNIT // LANES, 3)),
-            ],
-        ),
-        out_shape=[
-            jax.ShapeDtypeStruct((ahead * UNIT_SENDERS, 8, LANES), F32),
-            jax.ShapeDtypeStruct(((units - ahead) * UNIT_SENDERS, 8, LANES), F32),
-        ],
-        compiler_params=params(),
-        name="radiation",
-    )(
-        slot, weights, solar, near_core(received), near_core(from_first), near_core(from_second),
-        near_core(from_moved), near_core(left), near_core(right), far(depth), far(ssa), far(rad_albedo),
-        near_core(aero_two),
+    from_third = lax.ppermute(received[STAY * LINES :], "grp", [(last - 1, last)])
+    arrived = lax.ppermute(received, "grp", [(0, last), (1, last - 1)])
+
+    heat_block = (UNIT_SENDERS, 8, LANES)
+    fixed = [
+        pl.BlockSpec((2 * GPOINTS, 176), lambda i, role: (0, 0)),
+        pl.BlockSpec((GPOINTS, LANES), lambda i, role: (0, 0)),
+    ]
+    common = (far(depth), far(ssa), far(rad_albedo), near_core(aero_two))
+    scratch = [
+        pltpu.VMEM((UNIT_SENDERS * LINES, LANES), F32),
+        *rad_scratch(),
+        pltpu.SemaphoreType.DMA((2, UNIT // LANES, 3)),
+    ]
+    def swap(edge, offset):
+        pairs = [
+            (s * DOMAINS + (i + offset) % DOMAINS, s * DOMAINS + (i + 1 + offset) % DOMAINS)
+            for s in range(last)
+            for i in range(0, DOMAINS, 2)
+        ]
+        return lax.ppermute(edge, ("grp", "dom"), pairs + [(b, a) for a, b in pairs])
+
+    of_pair = swap(edge_pair, 0)
+    of_next = swap(edge_next, 1)
+
+    def radiation(kernel, name, units, extra, *operands):
+        return pl.pallas_call(
+            kernel,
+            grid_spec=pltpu.PrefetchScalarGridSpec(
+                num_scalar_prefetch=1,
+                grid=(units,),
+                in_specs=fixed + [VMEM] * (len(operands) - extra) + [HBM] * (extra + 3) + [VMEM],
+                out_specs=pl.BlockSpec(heat_block, lambda i, role: (i, 0, 0)),
+                scratch_shapes=scratch,
+            ),
+            out_shape=jax.ShapeDtypeStruct((units * UNIT_SENDERS, 8, LANES), F32),
+            compiler_params=params(),
+            name=name,
+        )(slot, weights, solar, *operands, *common)
+
+    soon = radiation(soon_kernel, "soon", SOON, 0, near_core(received), near_core(from_third))
+    later = radiation(
+        later_kernel, "later", LATER, 1, near_core(arrived), near_core(of_pair), near_core(of_next), soon
     )
 
     extended = CELLS + 2 * LANES
@@ -540,13 +554,12 @@
         ],
         compiler_params=params(),
         name="diffuse",
-    )(slot, far(fields), far(kappa), far(near), near_core(left), near_core(right), early)
-
-    to_first = lax.ppermute(early, "grp", [(last, 0)])
-    to_second = lax.ppermute(late, "grp", [(last, 1)])
-    moved_back = lax.ppermute(late, "grp", [(2, 1)])
-    away = to_first + jnp.concatenate([to_second, moved_back[:MOVED]], axis=0)
-    returning = jnp.where(slot[0] == last - 1, early, away)
+    )(slot, far(fields), far(kappa), far(near), near_core(of_pair), near_core(of_next), later)
+
+    third_back = lax.ppermute(soon, "grp", [(last, last - 1)])
+    back = lax.ppermute(later, "grp", [(last, 0), (last - 1, 1)])
+    own = jnp.concatenate([soon[:STAY], third_back[:MOVED]], axis=0)
+    returning = jnp.where(slot[0] == last - 1, own, back)
     mine = lax.all_to_all(returning, "dom", 0, 0, tiled=True)
 
     warmed = pl.pallas_call(

time: 92.2 us -> 84.1 us (0.912)
  waiting for transfers between devices: 36.4 us -> 28.4 us
  starting transfers between devices: 24.7 us -> 23.4 us
  Pallas kernels: 11.1 us -> 12.2 us
    ppermute x8 -> x6, waiting for transfers between devices: 33.5 us -> 26.1 us  [the longest x1 22 us: per_device(): back = lax.ppermute(later, 'grp', [(last, 0), (last - 1, 1)])]
    ppermute x8 -> x6, starting transfers between devices: 19.6 us -> 17.4 us  [the longest x1 8.63 us: per_device(): arrived = lax.ppermute(received, 'grp', [(0, last), (1, last - 1)])]
    pallas_call x1 -> x2, Pallas kernels: 0.7 us -> 1.76 us  [radiation(): pl.pallas_call(kernel, grid_spec=pltpu.PrefetchScalarGridSpec(num_scalar_...]
  transfers between devices with their start and end apart: 10 -> 8, of which waited for: 5 -> 4; matrix products, arithmetic and copies ran while one was open for 0% -> 0% of each run, Pallas kernels for 5% -> 7%
where the time goes in v4:
time: 84.1 us; the launch traced here: 83.7 us
  waiting for transfers between devices  28.4 us (34%)
  starting transfers between devices  23.4 us (28%)
  blocking collectives  18.8 us (22%)
  Pallas kernels  12.2 us (15%)
    ppermute x1, waiting for transfers between devices, per_device(): back = lax.ppermute(later, 'grp', [(last, 0), (last - 1, 1)])  22 us
    all_to_all x1, blocking collectives, per_device(): lax.all_to_all(message.reshape(DOMAINS, 1, LINES * LANES), 'dom', 0, 0, t...  18.8 us
    ppermute x1, starting transfers between devices, per_device(): arrived = lax.ppermute(received, 'grp', [(0, last), (1, last - 1)])  8.63 us
    ppermute x2, starting transfers between devices, swap(): lax.ppermute(edge, ('grp', 'dom'), pairs + [(b, a) for a, b in pairs])  6.15 us
    all_to_all x1, starting transfers between devices, per_device(): mine = lax.all_to_all(returning, 'dom', 0, 0, tiled=True)  4.96 us
    pallas_call x1, Pallas kernels, per_device(): pl.pallas_call(diffuse_kernel, in_specs=[SMEM] + [VMEM] * 5 + [HBM], out_...  4.96 us
    ppermute x2, waiting for transfers between devices, swap(): lax.ppermute(edge, ('grp', 'dom'), pairs + [(b, a) for a, b in pairs])  4.01 us
    pallas_call x1, Pallas kernels, per_device(): pl.pallas_call(first_kernel, in_specs=[SMEM, SMEM] + [VMEM] * 10 + [HBM]...  2.88 us
  transfers between devices with their start and end apart: 8, of which 4 were waited for; matrix products, arithmetic and copies ran while one was open for 0% of the time, Pallas kernels for 7%

profile of v4, /device:TPU:1, one launch (start us, length us, event | category | flops | bytes accessed | tf_op | source)
XLA Modules:
  0.0 83.7 jit_solution(16082138331672070868)
XLA Ops:
  0.0 0.1 pad_add_fusion.role
  0.1 2.9 %first.1 = (f32[800,128]{1,0:T(8,128)S(1)}, s32[1,512]{1,0:T(1,128)S(1)}, f32[104,128]{1,0:T(8,128)S(1)}, f32[104,128]{1,0:T(8,128)S(1)}, bf16[224,176]{1,0:T(8,...) custom-call(s32[2]{0:T(128)S(1)} %pad_add_fusion.role, s32[1,1,32]{2,1,0:T(1,128)} %bitcast.35, ...), custom_call_target="tpu_custom_call" | custom-call | tf_op jit(solution)/shard_map/first/pallas_call | solution.py:472
  3.0 1.0 %collective-permute-start.1 = (f32[29,32,1536]{2,1,0:T(8,128)S(1)}, f32[29,32,1536]{2,1,0:T(8,128)S(1)}, u32[]{:S(2)}, u32[]{:S(2)}) collective-permute-start(f32[29,32,1536]{2,1,0:T(8,128)S(1)} %get-tuple-element.15), channel_id=1, source_target_pairs={{96,64},{97,65},{98,66},{99,67},{100,68},{101,69},{102,70},{103,71... | collective-permute-start | bytes 17104904 | tf_op jit(solution)/shard_map/ppermute | solution.py:493
  4.0 18.8 %all_to_all.10 = f32[32,1,3200]{2,1,0:T(1,128)S(1)} all-to-all(f32[32,1,3200]{2,1,0:T(1,128)S(1)} %bitcast.22), channel_id=1, replica_groups=mesh['grp'=4,'dom'=32] {'dom'}, dimensions={0} | all-to-all | bytes 819200 | tf_op jit(solution)/shard_map/all_to_all | solution.py:495
  22.8 8.6 %collective-permute-start.3 = (f32[800,128]{1,0:T(8,128)S(1)}, f32[800,128]{1,0:T(8,128)S(1)}, u32[]{:S(2)}, u32[]{:S(2)}) collective-permute-start(f32[800,128]{1,0:T(8,128)S(1)} %bitcast.20), channel_id=1, source_target_pairs={{0,96},{32,64},{1,97},{33,65},{2,98},{34,66},{3,99},{35,67},{4,100... | collective-permute-start | bytes 1228808 | tf_op jit(solution)/shard_map/ppermute | solution.py:499
  31.4 0.7 collective-permute-start
  32.1 1.9 %collective-permute-start.4 = (f32[104,128]{1,0:T(8,128)S(1)}, f32[104,128]{1,0:T(8,128)S(1)}, u32[]{:S(2)}, u32[]{:S(2)}) collective-permute-start(f32[104,128]{1,0:T(8,128)S(1)} %get-tuple-element.16), channel_id=1, source_target_pairs={{0,1},{2,3},{4,5},{6,7},{8,9},{10,11},{12,13},{14,15},{16,17},{18,... | collective-permute-start | bytes 159752 | tf_op jit(solution)/shard_map/ppermute | solution.py:518
  34.0 4.2 %collective-permute-start.5 = (f32[104,128]{1,0:T(8,128)S(1)}, f32[104,128]{1,0:T(8,128)S(1)}, u32[]{:S(2)}, u32[]{:S(2)}) collective-permute-start(f32[104,128]{1,0:T(8,128)S(1)} %get-tuple-element.17), channel_id=1, source_target_pairs={{1,2},{3,4},{5,6},{7,8},{9,10},{11,12},{13,14},{15,16},{17,18},{19... | collective-permute-start | bytes 159752 | tf_op jit(solution)/shard_map/ppermute | solution.py:518
  38.3 0.0 collective-permute-done.from_third
  38.3 0.0 collective-permute-done.1.aero_two
  38.3 0.8 soon.1._soon
  39.1 3.5 %collective-permute-done.4._pair.of_pair = f32[104,128]{1,0:T(8,128)S(1)} collective-permute-done((f32[104,128]{1,0:T(8,128)S(1)}, f32[104,128]{1,0:T(8,128)S(1)}, u32[]{:S(2)}, u32[]{:S(2)}) %collective-permute-start.4) | collective-permute-done | bytes 53280 | tf_op jit(solution)/shard_map/ppermute | solution.py:518
  42.6 0.5 collective-permute-done.5._next.of_next
  43.1 0.0 collective-permute-done.3.arrived
  43.1 0.9 %later.1._ = f32[32,8,128]{2,1,0:T(8,128)S(1)} custom-call(s32[2]{0:T(128)S(1)} %pad_add_fusion.role, bf16[224,176]{1,0:T(8,128)(2,1)S(1)} %get-tuple-element.12.weights, f32[112,128]{1,0:T(8,128)S(1)} %get-tuple-element.13.solar, f32[800,128]{1,0:T(8,128)S(1)} %collective-permute-done.3.arrived, f32[104,128]{1,0:T(8,128)S(1)} %collective-permute-done.4._pair.of_pair, ...), custom_call_target="tpu_custom_call" | custom-call | tf_op jit(solution)/shard_map/later/pallas_call | solution.py:524
  44.1 1.3 %collective-permute-start.6 = (f32[32,8,128]{2,1,0:T(8,128)S(1)}, f32[32,8,128]{2,1,0:T(8,128)S(1)}, u32[]{:S(2)}, u32[]{:S(2)}) collective-permute-start(f32[32,8,128]{2,1,0:T(8,128)S(1)} %later.1._), channel_id=1, source_target_pairs={{96,0},{64,32},{97,1},{65,33},{98,2},{66,34},{99,3},{67,35},{100,4... | collective-permute-start | bytes 393224 | tf_op jit(solution)/shard_map/ppermute | solution.py:560
  45.4 0.7 collective-permute-start.2
  46.1 0.0 collective-permute-done.2
  46.1 22.0 %collective-permute-done.6 = f32[32,8,128]{2,1,0:T(8,128)S(1)} collective-permute-done((f32[32,8,128]{2,1,0:T(8,128)S(1)}, f32[32,8,128]{2,1,0:T(8,128)S(1)}, u32[]{:S(2)}, u32[]{:S(2)}) %collective-permute-start.6) | collective-permute-done | bytes 131104 | tf_op jit(solution)/shard_map/ppermute | solution.py:560
  68.1 0.7 maximum_select_fusion
  68.8 5.0 %all-to-all-start.1 = ((f32[32,8,128]{2,1,0:T(8,128)}), f32[32,8,128]{2,1,0:T(8,128)S(1)}, u32[]{:S(2)}, u32[]{:S(2)}) async-start(f32[32,8,128]{2,1,0:T(8,128)} %maximum_select_fusion), calls=%async_computation.1 | async-start | bytes 262144 | tf_op jit(solution)/shard_map/all_to_all | solution.py:563
  73.8 5.0 %diffuse.1.stepped = f32[96,2048]{1,0:T(8,128)} custom-call(s32[2]{0:T(128)S(1)} %pad_add_fusion.role, f32[96,2048]{1,0:T(8,128)} %bitcast.30, f32[1,2048]{1,0:T(1,128)} %kappa.3, s32[3,1,2048]{2,1,0:T(1,128)} %bitcast.33, f32[104,128]{1,0:T(8,128)S(1)} %collective-permute-done.4._pair.of_pair, f32[104,128]{1,0:T(8,128)S(1)} %collective-permute-done.5._next.of_next, ...), custom_call_target="tpu_custom_call" | custom-call | tf_op jit(solution)/shard_map/diffuse/pallas_call | solution.py:544
  78.7 2.4 %all-to-all-done.1.mine = f32[32,8,128]{2,1,0:T(8,128)S(1)} async-done(((f32[32,8,128]{2,1,0:T(8,128)}), f32[32,8,128]{2,1,0:T(8,128)S(1)}, u32[]{:S(2)}, u32[]{:S(2)}) %all-to-all-start.1) | async-done | bytes 131104 | tf_op jit(solution)/shard_map/all_to_all | solution.py:563
  81.1 2.6 %warm.1 = f32[96,2048]{1,0:T(8,128)} custom-call(s32[2]{0:T(128)S(1)} %pad_add_fusion.role, f32[32,8,128]{2,1,0:T(8,128)S(1)} %all-to-all-done.1.mine, s32[1,2048]{1,0:T(1,128)} %parent.3, s32[1,512]{1,0:T(1,128)S(1)} %get-tuple-element.18.slots_in, f32[96,2048]{1,0:T(8,128)} %diffuse.1.stepped), custom_call_target="tpu_custom_call", output_to_operand_aliasing={{}: (4, {})} | custom-call | tf_op jit(solution)/shard_map/warm/pallas_call | solution.py:565
  (1 shorter events, 0.0 us)
Async XLA Ops:
  3.0 35.3 %collective-permute-start.1 = (f32[29,32,1536]{2,1,0:T(8,128)S(1)}, f32[29,32,1536]{2,1,0:T(8,128)S(1)}, u32[]{:S(2)}, u32[]{:S(2)}) collective-permute-start(f32[29,32,1536]{2,1,0:T(8,128)S(1)} %get-tuple-element.15), channel_id=1, source_target_pairs={{96,64},{97,65},{98,66},{99,67},{100,68},{101,69},{102,70},{103,71... | collective-permute-start | bytes 17104904 | tf_op jit(solution)/shard_map/ppermute | solution.py:493
  22.8 20.4 %collective-permute-start.3 = (f32[800,128]{1,0:T(8,128)S(1)}, f32[800,128]{1,0:T(8,128)S(1)}, u32[]{:S(2)}, u32[]{:S(2)}) collective-permute-start(f32[800,128]{1,0:T(8,128)S(1)} %bitcast.20), channel_id=1, source_target_pairs={{0,96},{32,64},{1,97},{33,65},{2,98},{34,66},{3,99},{35,67},{4,100... | collective-permute-start | bytes 1228808 | tf_op jit(solution)/shard_map/ppermute | solution.py:499
  31.4 6.9 %collective-permute-start = (f32[400,128]{1,0:T(8,128)S(1)}, f32[400,128]{1,0:T(8,128)S(1)}, u32[]{:S(2)}, u32[]{:S(2)}) collective-permute-start(f32[400,128]{1,0:T(8,128)S(1)} %bitcast.31), channel_id=1, source_target_pairs={{64,96},{65,97},{66,98},{67,99},{68,100},{69,101},{70,102},{71,103... | collective-permute-start | bytes 614408 | tf_op jit(solution)/shard_map/ppermute | solution.py:498
  32.1 10.5 %collective-permute-start.4 = (f32[104,128]{1,0:T(8,128)S(1)}, f32[104,128]{1,0:T(8,128)S(1)}, u32[]{:S(2)}, u32[]{:S(2)}) collective-permute-start(f32[104,128]{1,0:T(8,128)S(1)} %get-tuple-element.16), channel_id=1, source_target_pairs={{0,1},{2,3},{4,5},{6,7},{8,9},{10,11},{12,13},{14,15},{16,17},{18,... | collective-permute-start | bytes 159752 | tf_op jit(solution)/shard_map/ppermute | solution.py:518
  34.0 9.1 %collective-permute-start.5 = (f32[104,128]{1,0:T(8,128)S(1)}, f32[104,128]{1,0:T(8,128)S(1)}, u32[]{:S(2)}, u32[]{:S(2)}) collective-permute-start(f32[104,128]{1,0:T(8,128)S(1)} %get-tuple-element.17), channel_id=1, source_target_pairs={{1,2},{3,4},{5,6},{7,8},{9,10},{11,12},{13,14},{15,16},{17,18},{19... | collective-permute-start | bytes 159752 | tf_op jit(solution)/shard_map/ppermute | solution.py:518
  44.1 24.0 %collective-permute-start.6 = (f32[32,8,128]{2,1,0:T(8,128)S(1)}, f32[32,8,128]{2,1,0:T(8,128)S(1)}, u32[]{:S(2)}, u32[]{:S(2)}) collective-permute-start(f32[32,8,128]{2,1,0:T(8,128)S(1)} %later.1._), channel_id=1, source_target_pairs={{96,0},{64,32},{97,1},{65,33},{98,2},{66,34},{99,3},{67,35},{100,4... | collective-permute-start | bytes 393224 | tf_op jit(solution)/shard_map/ppermute | solution.py:560
  45.4 0.7 collective-permute-start.2
  68.8 12.3 %all-to-all-start.1 = ((f32[32,8,128]{2,1,0:T(8,128)}), f32[32,8,128]{2,1,0:T(8,128)S(1)}, u32[]{:S(2)}, u32[]{:S(2)}) async-start(f32[32,8,128]{2,1,0:T(8,128)} %maximum_select_fusion), calls=%async_computation.1 | async-start | bytes 262144 | tf_op jit(solution)/shard_map/all_to_all | solution.py:563

commit v5 on v4

--- a/solution.py
+++ b/solution.py
@@ -425,6 +425,21 @@
     ]
 
 
+def columns_at(table, index):
+    shape = (table.shape[0], LANES)
+    tiles = []
+    for start in range(0, index.shape[1], LANES):
+        here = jnp.broadcast_to(index[:, start : start + LANES], shape)
+        source, lane = here // LANES, here % LANES
+        result = None
+        for k in range(table.shape[1] // LANES):
+            part = table[:, k * LANES : (k + 1) * LANES]
+            found = jnp.take_along_axis(part, lane, axis=1, mode="promise_in_bounds")
+            result = found if result is None else jnp.where(source == k, found, result)
+        tiles.append(result)
+    return jnp.concatenate(tiles, axis=1)
+
+
 def warm_kernel(role, mine, parent, slots_in, stepped, out):
     span = LEVELS // PER_TILE
     tiles = []
@@ -434,10 +449,8 @@
             jnp.concatenate([regroup(parts, lambda e: e - a) for a in range(PER_TILE)], axis=0)
         )
     heat = jnp.concatenate(tiles, axis=1)
-    placed = ones_where(iota((DOMAINS * SLOT_COLS, COARSE), 0) == slots_in[...])
-    coarse = exact_dot(heat, placed, 0)
-    lineage = ones_where(iota((COARSE, CELLS), 0) == parent[...])
-    fine = exact_dot(coarse, lineage, 0)
+    coarse = columns_at(heat, slots_in[...])
+    fine = columns_at(coarse, parent[...])
     out[...] = jnp.where(role[0] != SLOTS - 1, stepped[...] + 0.5 * fine, 0.0)
 
 
@@ -474,10 +487,10 @@
         in_specs=[SMEM, SMEM] + [VMEM] * 10 + [HBM] * 3,
         out_specs=[VMEM] * 7,
         out_shape=[
-            jax.ShapeDtypeStruct((DOMAINS * LINES, LANES), F32),
+            pltpu.VMEM((DOMAINS * LINES, LANES), F32),
             jax.ShapeDtypeStruct((1, COARSE), I32),
-            jax.ShapeDtypeStruct((ROWS + 8, LANES), F32),
-            jax.ShapeDtypeStruct((ROWS + 8, LANES), F32),
+            pltpu.VMEM((ROWS + 8, LANES), F32),
+            pltpu.VMEM((ROWS + 8, LANES), F32),
             jax.ShapeDtypeStruct((2 * GPOINTS, 176), BF16),
             jax.ShapeDtypeStruct((GPOINTS, LANES), F32),
             pltpu.VMEM((2 * BANDS + 1, LEVELS, (DOMAINS + STAY) * SLOT_COLS), F32),

time: 84.1 us -> 83.9 us (level)
  no operation moved by 1% of the time
where the time goes in v5:
time: 83.9 us; the launch traced here: 83.5 us
  waiting for transfers between devices  28.4 us (34%)
  starting transfers between devices  23.4 us (28%)
  blocking collectives  18.8 us (22%)
  Pallas kernels  12 us (14%)
    ppermute x1, waiting for transfers between devices, per_device(): back = lax.ppermute(later, 'grp', [(last, 0), (last - 1, 1)])  22 us
    all_to_all x1, blocking collectives, per_device(): lax.all_to_all(message.reshape(DOMAINS, 1, LINES * LANES), 'dom', 0, 0, t...  18.8 us
    ppermute x1, starting transfers between devices, per_device(): arrived = lax.ppermute(received, 'grp', [(0, last), (1, last - 1)])  8.63 us
    ppermute x2, starting transfers between devices, swap(): lax.ppermute(edge, ('grp', 'dom'), pairs + [(b, a) for a, b in pairs])  6.15 us
    all_to_all x1, starting transfers between devices, per_device(): mine = lax.all_to_all(returning, 'dom', 0, 0, tiled=True)  4.96 us
    pallas_call x1, Pallas kernels, per_device(): pl.pallas_call(diffuse_kernel, in_specs=[SMEM] + [VMEM] * 5 + [HBM], out_...  4.96 us
    ppermute x2, waiting for transfers between devices, swap(): lax.ppermute(edge, ('grp', 'dom'), pairs + [(b, a) for a, b in pairs])  4.01 us
    pallas_call x1, Pallas kernels, per_device(): pl.pallas_call(first_kernel, in_specs=[SMEM, SMEM] + [VMEM] * 10 + [HBM]...  2.88 us
  transfers between devices with their start and end apart: 8, of which 4 were waited for; matrix products, arithmetic and copies ran while one was open for 0% of the time, Pallas kernels for 7%

profile of v5, /device:TPU:1, one launch (start us, length us, event | category | flops | bytes accessed | tf_op | source)
XLA Modules:
  0.0 83.5 jit_solution(9797297310745707985)
XLA Ops:
  0.0 0.1 pad_add_fusion.role
  0.1 2.9 %first.1 = (f32[800,128]{1,0:T(8,128)S(1)}, s32[1,512]{1,0:T(1,128)S(1)}, f32[104,128]{1,0:T(8,128)S(1)}, f32[104,128]{1,0:T(8,128)S(1)}, bf16[224,176]{1,0:T(8,...) custom-call(s32[2]{0:T(128)S(1)} %pad_add_fusion.role, s32[1,1,32]{2,1,0:T(1,128)} %bitcast.35, ...), custom_call_target="tpu_custom_call" | custom-call | tf_op jit(solution)/shard_map/first/pallas_call | solution.py:485
  3.0 1.0 %collective-permute-start.1 = (f32[29,32,1536]{2,1,0:T(8,128)S(1)}, f32[29,32,1536]{2,1,0:T(8,128)S(1)}, u32[]{:S(2)}, u32[]{:S(2)}) collective-permute-start(f32[29,32,1536]{2,1,0:T(8,128)S(1)} %get-tuple-element.15), channel_id=1, source_target_pairs={{96,64},{97,65},{98,66},{99,67},{100,68},{101,69},{102,70},{103,71... | collective-permute-start | bytes 17104904 | tf_op jit(solution)/shard_map/ppermute | solution.py:506
  4.0 18.8 %all_to_all.10 = f32[32,1,3200]{2,1,0:T(1,128)S(1)} all-to-all(f32[32,1,3200]{2,1,0:T(1,128)S(1)} %bitcast.22), channel_id=1, replica_groups=mesh['grp'=4,'dom'=32] {'dom'}, dimensions={0} | all-to-all | bytes 819200 | tf_op jit(solution)/shard_map/all_to_all | solution.py:508
  22.8 8.6 %collective-permute-start.3 = (f32[800,128]{1,0:T(8,128)S(1)}, f32[800,128]{1,0:T(8,128)S(1)}, u32[]{:S(2)}, u32[]{:S(2)}) collective-permute-start(f32[800,128]{1,0:T(8,128)S(1)} %bitcast.20), channel_id=1, source_target_pairs={{0,96},{32,64},{1,97},{33,65},{2,98},{34,66},{3,99},{35,67},{4,100... | collective-permute-start | bytes 1228808 | tf_op jit(solution)/shard_map/ppermute | solution.py:512
  31.4 0.7 collective-permute-start
  32.1 1.9 %collective-permute-start.4 = (f32[104,128]{1,0:T(8,128)S(1)}, f32[104,128]{1,0:T(8,128)S(1)}, u32[]{:S(2)}, u32[]{:S(2)}) collective-permute-start(f32[104,128]{1,0:T(8,128)S(1)} %get-tuple-element.16), channel_id=1, source_target_pairs={{0,1},{2,3},{4,5},{6,7},{8,9},{10,11},{12,13},{14,15},{16,17},{18,... | collective-permute-start | bytes 159752 | tf_op jit(solution)/shard_map/ppermute | solution.py:531
  34.0 4.2 %collective-permute-start.5 = (f32[104,128]{1,0:T(8,128)S(1)}, f32[104,128]{1,0:T(8,128)S(1)}, u32[]{:S(2)}, u32[]{:S(2)}) collective-permute-start(f32[104,128]{1,0:T(8,128)S(1)} %get-tuple-element.17), channel_id=1, source_target_pairs={{1,2},{3,4},{5,6},{7,8},{9,10},{11,12},{13,14},{15,16},{17,18},{19... | collective-permute-start | bytes 159752 | tf_op jit(solution)/shard_map/ppermute | solution.py:531
  38.3 0.0 collective-permute-done.from_third
  38.3 0.0 collective-permute-done.1.aero_two
  38.3 0.8 soon.1._soon
  39.1 3.5 %collective-permute-done.4._pair.of_pair = f32[104,128]{1,0:T(8,128)S(1)} collective-permute-done((f32[104,128]{1,0:T(8,128)S(1)}, f32[104,128]{1,0:T(8,128)S(1)}, u32[]{:S(2)}, u32[]{:S(2)}) %collective-permute-start.4) | collective-permute-done | bytes 53280 | tf_op jit(solution)/shard_map/ppermute | solution.py:531
  42.6 0.5 collective-permute-done.5._next.of_next
  43.1 0.0 collective-permute-done.3.arrived
  43.1 0.9 %later.1._ = f32[32,8,128]{2,1,0:T(8,128)S(1)} custom-call(s32[2]{0:T(128)S(1)} %pad_add_fusion.role, bf16[224,176]{1,0:T(8,128)(2,1)S(1)} %get-tuple-element.12.weights, f32[112,128]{1,0:T(8,128)S(1)} %get-tuple-element.13.solar, f32[800,128]{1,0:T(8,128)S(1)} %collective-permute-done.3.arrived, f32[104,128]{1,0:T(8,128)S(1)} %collective-permute-done.4._pair.of_pair, ...), custom_call_target="tpu_custom_call" | custom-call | tf_op jit(solution)/shard_map/later/pallas_call | solution.py:537
  44.1 1.3 %collective-permute-start.6 = (f32[32,8,128]{2,1,0:T(8,128)S(1)}, f32[32,8,128]{2,1,0:T(8,128)S(1)}, u32[]{:S(2)}, u32[]{:S(2)}) collective-permute-start(f32[32,8,128]{2,1,0:T(8,128)S(1)} %later.1._), channel_id=1, source_target_pairs={{96,0},{64,32},{97,1},{65,33},{98,2},{66,34},{99,3},{67,35},{100,4... | collective-permute-start | bytes 393224 | tf_op jit(solution)/shard_map/ppermute | solution.py:573
  45.4 0.7 collective-permute-start.2
  46.1 0.0 collective-permute-done.2
  46.1 22.0 %collective-permute-done.6 = f32[32,8,128]{2,1,0:T(8,128)S(1)} collective-permute-done((f32[32,8,128]{2,1,0:T(8,128)S(1)}, f32[32,8,128]{2,1,0:T(8,128)S(1)}, u32[]{:S(2)}, u32[]{:S(2)}) %collective-permute-start.6) | collective-permute-done | bytes 131104 | tf_op jit(solution)/shard_map/ppermute | solution.py:573
  68.1 0.7 maximum_select_fusion
  68.8 5.0 %all-to-all-start.1 = ((f32[32,8,128]{2,1,0:T(8,128)}), f32[32,8,128]{2,1,0:T(8,128)S(1)}, u32[]{:S(2)}, u32[]{:S(2)}) async-start(f32[32,8,128]{2,1,0:T(8,128)} %maximum_select_fusion), calls=%async_computation.1 | async-start | bytes 262144 | tf_op jit(solution)/shard_map/all_to_all | solution.py:576
  73.8 5.0 %diffuse.1.stepped = f32[96,2048]{1,0:T(8,128)} custom-call(s32[2]{0:T(128)S(1)} %pad_add_fusion.role, f32[96,2048]{1,0:T(8,128)} %bitcast.30, f32[1,2048]{1,0:T(1,128)} %kappa.3, s32[3,1,2048]{2,1,0:T(1,128)} %bitcast.33, f32[104,128]{1,0:T(8,128)S(1)} %collective-permute-done.4._pair.of_pair, f32[104,128]{1,0:T(8,128)S(1)} %collective-permute-done.5._next.of_next, ...), custom_call_target="tpu_custom_call" | custom-call | tf_op jit(solution)/shard_map/diffuse/pallas_call | solution.py:557
  78.7 2.4 %all-to-all-done.1.mine = f32[32,8,128]{2,1,0:T(8,128)S(1)} async-done(((f32[32,8,128]{2,1,0:T(8,128)}), f32[32,8,128]{2,1,0:T(8,128)S(1)}, u32[]{:S(2)}, u32[]{:S(2)}) %all-to-all-start.1) | async-done | bytes 131104 | tf_op jit(solution)/shard_map/all_to_all | solution.py:576
  81.1 2.4 %warm.1 = f32[96,2048]{1,0:T(8,128)} custom-call(s32[2]{0:T(128)S(1)} %pad_add_fusion.role, f32[32,8,128]{2,1,0:T(8,128)S(1)} %all-to-all-done.1.mine, s32[1,2048]{1,0:T(1,128)} %parent.3, s32[1,512]{1,0:T(1,128)S(1)} %get-tuple-element.18.slots_in, f32[96,2048]{1,0:T(8,128)} %diffuse.1.stepped), custom_call_target="tpu_custom_call", output_to_operand_aliasing={{}: (4, {})} | custom-call | tf_op jit(solution)/shard_map/warm/pallas_call | solution.py:578
  (1 shorter events, 0.0 us)
Async XLA Ops:
  3.0 35.3 %collective-permute-start.1 = (f32[29,32,1536]{2,1,0:T(8,128)S(1)}, f32[29,32,1536]{2,1,0:T(8,128)S(1)}, u32[]{:S(2)}, u32[]{:S(2)}) collective-permute-start(f32[29,32,1536]{2,1,0:T(8,128)S(1)} %get-tuple-element.15), channel_id=1, source_target_pairs={{96,64},{97,65},{98,66},{99,67},{100,68},{101,69},{102,70},{103,71... | collective-permute-start | bytes 17104904 | tf_op jit(solution)/shard_map/ppermute | solution.py:506
  22.8 20.4 %collective-permute-start.3 = (f32[800,128]{1,0:T(8,128)S(1)}, f32[800,128]{1,0:T(8,128)S(1)}, u32[]{:S(2)}, u32[]{:S(2)}) collective-permute-start(f32[800,128]{1,0:T(8,128)S(1)} %bitcast.20), channel_id=1, source_target_pairs={{0,96},{32,64},{1,97},{33,65},{2,98},{34,66},{3,99},{35,67},{4,100... | collective-permute-start | bytes 1228808 | tf_op jit(solution)/shard_map/ppermute | solution.py:512
  31.4 6.9 %collective-permute-start = (f32[400,128]{1,0:T(8,128)S(1)}, f32[400,128]{1,0:T(8,128)S(1)}, u32[]{:S(2)}, u32[]{:S(2)}) collective-permute-start(f32[400,128]{1,0:T(8,128)S(1)} %bitcast.31), channel_id=1, source_target_pairs={{64,96},{65,97},{66,98},{67,99},{68,100},{69,101},{70,102},{71,103... | collective-permute-start | bytes 614408 | tf_op jit(solution)/shard_map/ppermute | solution.py:511
  32.1 10.5 %collective-permute-start.4 = (f32[104,128]{1,0:T(8,128)S(1)}, f32[104,128]{1,0:T(8,128)S(1)}, u32[]{:S(2)}, u32[]{:S(2)}) collective-permute-start(f32[104,128]{1,0:T(8,128)S(1)} %get-tuple-element.16), channel_id=1, source_target_pairs={{0,1},{2,3},{4,5},{6,7},{8,9},{10,11},{12,13},{14,15},{16,17},{18,... | collective-permute-start | bytes 159752 | tf_op jit(solution)/shard_map/ppermute | solution.py:531
  34.0 9.1 %collective-permute-start.5 = (f32[104,128]{1,0:T(8,128)S(1)}, f32[104,128]{1,0:T(8,128)S(1)}, u32[]{:S(2)}, u32[]{:S(2)}) collective-permute-start(f32[104,128]{1,0:T(8,128)S(1)} %get-tuple-element.17), channel_id=1, source_target_pairs={{1,2},{3,4},{5,6},{7,8},{9,10},{11,12},{13,14},{15,16},{17,18},{19... | collective-permute-start | bytes 159752 | tf_op jit(solution)/shard_map/ppermute | solution.py:531
  44.1 24.0 %collective-permute-start.6 = (f32[32,8,128]{2,1,0:T(8,128)S(1)}, f32[32,8,128]{2,1,0:T(8,128)S(1)}, u32[]{:S(2)}, u32[]{:S(2)}) collective-permute-start(f32[32,8,128]{2,1,0:T(8,128)S(1)} %later.1._), channel_id=1, source_target_pairs={{96,0},{64,32},{97,1},{65,33},{98,2},{66,34},{99,3},{67,35},{100,4... | collective-permute-start | bytes 393224 | tf_op jit(solution)/shard_map/ppermute | solution.py:573
  45.4 0.7 collective-permute-start.2
  68.8 12.3 %all-to-all-start.1 = ((f32[32,8,128]{2,1,0:T(8,128)}), f32[32,8,128]{2,1,0:T(8,128)S(1)}, u32[]{:S(2)}, u32[]{:S(2)}) async-start(f32[32,8,128]{2,1,0:T(8,128)} %maximum_select_fusion), calls=%async_computation.1 | async-start | bytes 262144 | tf_op jit(solution)/shard_map/all_to_all | solution.py:576

commit v6 on v5

--- a/solution.py
+++ b/solution.py
@@ -22,7 +22,7 @@
 TILES = CELLS // LANES
 UNIT = 256
 UNIT_SENDERS = UNIT // SLOT_COLS
-STAY = 16
+STAY = 8
 MOVED = DOMAINS - STAY
 SOON = max(STAY, MOVED) // UNIT_SENDERS
 LATER = DOMAINS // UNIT_SENDERS

time: 83.9 us -> 82.6 us (0.985)
  the two profiles are of different devices: /device:TPU:1 before, /device:TPU:0 now
where the time goes in v6:
time: 82.6 us; the launch traced here: 82.2 us
  waiting for transfers between devices  28.9 us (35%)
  starting transfers between devices  20.9 us (25%)
  blocking collectives  19.4 us (23%)
  Pallas kernels  12.1 us (15%)
    ppermute x1, waiting for transfers between devices, per_device(): back = lax.ppermute(later, 'grp', [(last, 0), (last - 1, 1)])  20.7 us
    all_to_all x1, blocking collectives, per_device(): lax.all_to_all(message.reshape(DOMAINS, 1, LINES * LANES), 'dom', 0, 0, t...  19.4 us
    ppermute x1, starting transfers between devices, per_device(): arrived = lax.ppermute(received, 'grp', [(0, last), (1, last - 1)])  6.92 us
    ppermute x2, starting transfers between devices, swap(): lax.ppermute(edge, ('grp', 'dom'), pairs + [(b, a) for a, b in pairs])  6.53 us
    pallas_call x1, Pallas kernels, per_device(): pl.pallas_call(diffuse_kernel, in_specs=[SMEM] + [VMEM] * 5 + [HBM], out_...  4.96 us
    ppermute x2, waiting for transfers between devices, swap(): lax.ppermute(edge, ('grp', 'dom'), pairs + [(b, a) for a, b in pairs])  4.76 us
    all_to_all x1, starting transfers between devices, per_device(): mine = lax.all_to_all(returning, 'dom', 0, 0, tiled=True)  3.84 us
    all_to_all x1, waiting for transfers between devices, per_device(): mine = lax.all_to_all(returning, 'dom', 0, 0, tiled=True)  3.5 us
  transfers between devices with their start and end apart: 8, of which 4 were waited for; matrix products, arithmetic and copies ran while one was open for 0% of the time, Pallas kernels for 7%

profile of v6, /device:TPU:0, one launch (start us, length us, event | category | flops | bytes accessed | tf_op | source)
XLA Modules:
  0.0 82.2 jit_solution(1138638032699368456)
XLA Ops:
  0.0 0.1 pad_add_fusion.role
  0.1 2.9 %first.1 = (f32[800,128]{1,0:T(8,128)S(1)}, s32[1,512]{1,0:T(1,128)S(1)}, f32[104,128]{1,0:T(8,128)S(1)}, f32[104,128]{1,0:T(8,128)S(1)}, bf16[224,176]{1,0:T(8,...) custom-call(s32[2]{0:T(128)S(1)} %pad_add_fusion.role, s32[1,1,32]{2,1,0:T(1,128)} %bitcast.35, ...), custom_call_target="tpu_custom_call" | custom-call | tf_op jit(solution)/shard_map/first/pallas_call | solution.py:485
  3.0 1.0 %collective-permute-start.1 = (f32[29,32,1280]{2,1,0:T(8,128)S(1)}, f32[29,32,1280]{2,1,0:T(8,128)S(1)}, u32[]{:S(2)}, u32[]{:S(2)}) collective-permute-start(f32[29,32,1280]{2,1,0:T(8,128)S(1)} %get-tuple-element.15), channel_id=1, source_target_pairs={{96,64},{97,65},{98,66},{99,67},{100,68},{101,69},{102,70},{103,71... | collective-permute-start | bytes 14254088 | tf_op jit(solution)/shard_map/ppermute | solution.py:506
  3.9 19.4 %all_to_all.10 = f32[32,1,3200]{2,1,0:T(1,128)S(1)} all-to-all(f32[32,1,3200]{2,1,0:T(1,128)S(1)} %bitcast.22), channel_id=1, replica_groups=mesh['grp'=4,'dom'=32] {'dom'}, dimensions={0} | all-to-all | bytes 819200 | tf_op jit(solution)/shard_map/all_to_all | solution.py:508
  23.3 6.9 %collective-permute-start.3 = (f32[800,128]{1,0:T(8,128)S(1)}, f32[800,128]{1,0:T(8,128)S(1)}, u32[]{:S(2)}, u32[]{:S(2)}) collective-permute-start(f32[800,128]{1,0:T(8,128)S(1)} %bitcast.20), channel_id=1, source_target_pairs={{0,96},{32,64},{1,97},{33,65},{2,98},{34,66},{3,99},{35,67},{4,100... | collective-permute-start | bytes 1228808 | tf_op jit(solution)/shard_map/ppermute | solution.py:512
  30.3 0.7 collective-permute-start
  31.0 2.0 %collective-permute-start.4 = (f32[104,128]{1,0:T(8,128)S(1)}, f32[104,128]{1,0:T(8,128)S(1)}, u32[]{:S(2)}, u32[]{:S(2)}) collective-permute-start(f32[104,128]{1,0:T(8,128)S(1)} %get-tuple-element.16), channel_id=1, source_target_pairs={{0,1},{2,3},{4,5},{6,7},{8,9},{10,11},{12,13},{14,15},{16,17},{18,... | collective-permute-start | bytes 159752 | tf_op jit(solution)/shard_map/ppermute | solution.py:531
  33.0 4.6 %collective-permute-start.5 = (f32[104,128]{1,0:T(8,128)S(1)}, f32[104,128]{1,0:T(8,128)S(1)}, u32[]{:S(2)}, u32[]{:S(2)}) collective-permute-start(f32[104,128]{1,0:T(8,128)S(1)} %get-tuple-element.17), channel_id=1, source_target_pairs={{1,2},{3,4},{5,6},{7,8},{9,10},{11,12},{13,14},{15,16},{17,18},{19... | collective-permute-start | bytes 159752 | tf_op jit(solution)/shard_map/ppermute | solution.py:531
  37.6 0.0 collective-permute-done.from_third
  37.6 0.0 collective-permute-done.1.aero_two
  37.6 0.9 %soon.1._soon = f32[24,8,128]{2,1,0:T(8,128)S(1)} custom-call(s32[2]{0:T(128)S(1)} %pad_add_fusion.role, bf16[224,176]{1,0:T(8,128)(2,1)S(1)} %get-tuple-element.12.weights, f32[112,128]{1,0:T(8,128)S(1)} %get-tuple-element.13.solar, f32[800,128]{1,0:T(8,128)S(1)} %bitcast.21, f32[600,128]{1,0:T(8,128)S(1)} %collective-permute-done.from_third, ...), custom_call_target="tpu_custom_call" | custom-call | tf_op jit(solution)/shard_map/soon/pallas_call | solution.py:537
  38.5 3.6 %collective-permute-done.4._pair.of_pair = f32[104,128]{1,0:T(8,128)S(1)} collective-permute-done((f32[104,128]{1,0:T(8,128)S(1)}, f32[104,128]{1,0:T(8,128)S(1)}, u32[]{:S(2)}, u32[]{:S(2)}) %collective-permute-start.4) | collective-permute-done | bytes 53280 | tf_op jit(solution)/shard_map/ppermute | solution.py:531
  42.1 1.1 %collective-permute-done.5._next.of_next = f32[104,128]{1,0:T(8,128)S(1)} collective-permute-done((f32[104,128]{1,0:T(8,128)S(1)}, f32[104,128]{1,0:T(8,128)S(1)}, u32[]{:S(2)}, u32[]{:S(2)}) %collective-permute-start.5) | collective-permute-done | bytes 53280 | tf_op jit(solution)/shard_map/ppermute | solution.py:531
  43.2 0.0 collective-permute-done.3.arrived
  43.2 0.9 %later.1._ = f32[32,8,128]{2,1,0:T(8,128)S(1)} custom-call(s32[2]{0:T(128)S(1)} %pad_add_fusion.role, bf16[224,176]{1,0:T(8,128)(2,1)S(1)} %get-tuple-element.12.weights, f32[112,128]{1,0:T(8,128)S(1)} %get-tuple-element.13.solar, f32[800,128]{1,0:T(8,128)S(1)} %collective-permute-done.3.arrived, f32[104,128]{1,0:T(8,128)S(1)} %collective-permute-done.4._pair.of_pair, ...), custom_call_target="tpu_custom_call" | custom-call | tf_op jit(solution)/shard_map/later/pallas_call | solution.py:537
  44.2 1.3 %collective-permute-start.6 = (f32[32,8,128]{2,1,0:T(8,128)S(1)}, f32[32,8,128]{2,1,0:T(8,128)S(1)}, u32[]{:S(2)}, u32[]{:S(2)}) collective-permute-start(f32[32,8,128]{2,1,0:T(8,128)S(1)} %later.1._), channel_id=1, source_target_pairs={{96,0},{64,32},{97,1},{65,33},{98,2},{66,34},{99,3},{67,35},{100,4... | collective-permute-start | bytes 393224 | tf_op jit(solution)/shard_map/ppermute | solution.py:573
  45.5 0.7 collective-permute-start.2
  46.2 0.0 collective-permute-done.2
  46.2 20.7 %collective-permute-done.6 = f32[32,8,128]{2,1,0:T(8,128)S(1)} collective-permute-done((f32[32,8,128]{2,1,0:T(8,128)S(1)}, f32[32,8,128]{2,1,0:T(8,128)S(1)}, u32[]{:S(2)}, u32[]{:S(2)}) %collective-permute-start.6) | collective-permute-done | bytes 131104 | tf_op jit(solution)/shard_map/ppermute | solution.py:573
  66.8 0.7 maximum_select_fusion
  67.5 3.8 %all-to-all-start.1 = ((f32[32,8,128]{2,1,0:T(8,128)}), f32[32,8,128]{2,1,0:T(8,128)S(1)}, u32[]{:S(2)}, u32[]{:S(2)}) async-start(f32[32,8,128]{2,1,0:T(8,128)} %maximum_select_fusion), calls=%async_computation.1 | async-start | bytes 262144 | tf_op jit(solution)/shard_map/all_to_all | solution.py:576
  71.4 5.0 %diffuse.1.stepped = f32[96,2048]{1,0:T(8,128)} custom-call(s32[2]{0:T(128)S(1)} %pad_add_fusion.role, f32[96,2048]{1,0:T(8,128)} %bitcast.30, f32[1,2048]{1,0:T(1,128)} %kappa.3, s32[3,1,2048]{2,1,0:T(1,128)} %bitcast.33, f32[104,128]{1,0:T(8,128)S(1)} %collective-permute-done.4._pair.of_pair, f32[104,128]{1,0:T(8,128)S(1)} %collective-permute-done.5._next.of_next, ...), custom_call_target="tpu_custom_call" | custom-call | tf_op jit(solution)/shard_map/diffuse/pallas_call | solution.py:557
  76.3 3.5 %all-to-all-done.1.mine = f32[32,8,128]{2,1,0:T(8,128)S(1)} async-done(((f32[32,8,128]{2,1,0:T(8,128)}), f32[32,8,128]{2,1,0:T(8,128)S(1)}, u32[]{:S(2)}, u32[]{:S(2)}) %all-to-all-start.1) | async-done | bytes 131104 | tf_op jit(solution)/shard_map/all_to_all | solution.py:576
  79.8 2.4 %warm.1 = f32[96,2048]{1,0:T(8,128)} custom-call(s32[2]{0:T(128)S(1)} %pad_add_fusion.role, f32[32,8,128]{2,1,0:T(8,128)S(1)} %all-to-all-done.1.mine, s32[1,2048]{1,0:T(1,128)} %parent.3, s32[1,512]{1,0:T(1,128)S(1)} %get-tuple-element.18.slots_in, f32[96,2048]{1,0:T(8,128)} %diffuse.1.stepped), custom_call_target="tpu_custom_call", output_to_operand_aliasing={{}: (4, {})} | custom-call | tf_op jit(solution)/shard_map/warm/pallas_call | solution.py:578
  (2 shorter events, 0.0 us)
Async XLA Ops:
  3.0 34.6 %collective-permute-start.1 = (f32[29,32,1280]{2,1,0:T(8,128)S(1)}, f32[29,32,1280]{2,1,0:T(8,128)S(1)}, u32[]{:S(2)}, u32[]{:S(2)}) collective-permute-start(f32[29,32,1280]{2,1,0:T(8,128)S(1)} %get-tuple-element.15), channel_id=1, source_target_pairs={{96,64},{97,65},{98,66},{99,67},{100,68},{101,69},{102,70},{103,71... | collective-permute-start | bytes 14254088 | tf_op jit(solution)/shard_map/ppermute | solution.py:506
  23.3 19.9 %collective-permute-start.3 = (f32[800,128]{1,0:T(8,128)S(1)}, f32[800,128]{1,0:T(8,128)S(1)}, u32[]{:S(2)}, u32[]{:S(2)}) collective-permute-start(f32[800,128]{1,0:T(8,128)S(1)} %bitcast.20), channel_id=1, source_target_pairs={{0,96},{32,64},{1,97},{33,65},{2,98},{34,66},{3,99},{35,67},{4,100... | collective-permute-start | bytes 1228808 | tf_op jit(solution)/shard_map/ppermute | solution.py:512
  30.3 7.2 %collective-permute-start = (f32[600,128]{1,0:T(8,128)S(1)}, f32[600,128]{1,0:T(8,128)S(1)}, u32[]{:S(2)}, u32[]{:S(2)}) collective-permute-start(f32[600,128]{1,0:T(8,128)S(1)} %bitcast.31), channel_id=1, source_target_pairs={{64,96},{65,97},{66,98},{67,99},{68,100},{69,101},{70,102},{71,103... | collective-permute-start | bytes 921608 | tf_op jit(solution)/shard_map/ppermute | solution.py:511
  31.0 11.1 %collective-permute-start.4 = (f32[104,128]{1,0:T(8,128)S(1)}, f32[104,128]{1,0:T(8,128)S(1)}, u32[]{:S(2)}, u32[]{:S(2)}) collective-permute-start(f32[104,128]{1,0:T(8,128)S(1)} %get-tuple-element.16), channel_id=1, source_target_pairs={{0,1},{2,3},{4,5},{6,7},{8,9},{10,11},{12,13},{14,15},{16,17},{18,... | collective-permute-start | bytes 159752 | tf_op jit(solution)/shard_map/ppermute | solution.py:531
  33.0 10.3 %collective-permute-start.5 = (f32[104,128]{1,0:T(8,128)S(1)}, f32[104,128]{1,0:T(8,128)S(1)}, u32[]{:S(2)}, u32[]{:S(2)}) collective-permute-start(f32[104,128]{1,0:T(8,128)S(1)} %get-tuple-element.17), channel_id=1, source_target_pairs={{1,2},{3,4},{5,6},{7,8},{9,10},{11,12},{13,14},{15,16},{17,18},{19... | collective-permute-start | bytes 159752 | tf_op jit(solution)/shard_map/ppermute | solution.py:531
  44.2 22.7 %collective-permute-start.6 = (f32[32,8,128]{2,1,0:T(8,128)S(1)}, f32[32,8,128]{2,1,0:T(8,128)S(1)}, u32[]{:S(2)}, u32[]{:S(2)}) collective-permute-start(f32[32,8,128]{2,1,0:T(8,128)S(1)} %later.1._), channel_id=1, source_target_pairs={{96,0},{64,32},{97,1},{65,33},{98,2},{66,34},{99,3},{67,35},{100,4... | collective-permute-start | bytes 393224 | tf_op jit(solution)/shard_map/ppermute | solution.py:573
  45.5 0.7 collective-permute-start.2
  67.5 12.3 %all-to-all-start.1 = ((f32[32,8,128]{2,1,0:T(8,128)}), f32[32,8,128]{2,1,0:T(8,128)S(1)}, u32[]{:S(2)}, u32[]{:S(2)}) async-start(f32[32,8,128]{2,1,0:T(8,128)} %maximum_select_fusion), calls=%async_computation.1 | async-start | bytes 262144 | tf_op jit(solution)/shard_map/all_to_all | solution.py:576

commit v7 on v6

--- a/solution.py
+++ b/solution.py
@@ -27,7 +27,7 @@
 SOON = max(STAY, MOVED) // UNIT_SENDERS
 LATER = DOMAINS // UNIT_SENDERS
 LEVEL_BLOCK = 8
-AERO = 2 * BANDS + 2
+AERO = 2 * BANDS + 3
 PITCH = LEVELS + 8
 LOG2E = 1.4426950408889634
 VMEM_LIMIT = 28 * 1024 * 1024

time: 82.6 us -> 82.6 us (level)
  no operation moved by 1% of the time
where the time goes in v7:
time: 82.6 us; the launch traced here: 82.2 us
  waiting for transfers between devices  28.9 us (35%)
  starting transfers between devices  20.9 us (25%)
  blocking collectives  19.4 us (23%)
  Pallas kernels  12.1 us (15%)
    ppermute x1, waiting for transfers between devices, per_device(): back = lax.ppermute(later, 'grp', [(last, 0), (last - 1, 1)])  20.7 us
    all_to_all x1, blocking collectives, per_device(): lax.all_to_all(message.reshape(DOMAINS, 1, LINES * LANES), 'dom', 0, 0, t...  19.4 us
    ppermute x1, starting transfers between devices, per_device(): arrived = lax.ppermute(received, 'grp', [(0, last), (1, last - 1)])  6.92 us
    ppermute x2, starting transfers between devices, swap(): lax.ppermute(edge, ('grp', 'dom'), pairs + [(b, a) for a, b in pairs])  6.53 us
    pallas_call x1, Pallas kernels, per_device(): pl.pallas_call(diffuse_kernel, in_specs=[SMEM] + [VMEM] * 5 + [HBM], out_...  4.96 us
    ppermute x2, waiting for transfers between devices, swap(): lax.ppermute(edge, ('grp', 'dom'), pairs + [(b, a) for a, b in pairs])  4.76 us
    all_to_all x1, starting transfers between devices, per_device(): mine = lax.all_to_all(returning, 'dom', 0, 0, tiled=True)  3.84 us
    all_to_all x1, waiting for transfers between devices, per_device(): mine = lax.all_to_all(returning, 'dom', 0, 0, tiled=True)  3.5 us
  transfers between devices with their start and end apart: 8, of which 4 were waited for; matrix products, arithmetic and copies ran while one was open for 0% of the time, Pallas kernels for 7%

profile of v7, /device:TPU:0, one launch (start us, length us, event | category | flops | bytes accessed | tf_op | source)
XLA Modules:
  0.0 82.2 jit_solution(678956274531515947)
XLA Ops:
  0.0 0.1 pad_add_fusion.role
  0.1 2.9 %first.1 = (f32[800,128]{1,0:T(8,128)S(1)}, s32[1,512]{1,0:T(1,128)S(1)}, f32[104,128]{1,0:T(8,128)S(1)}, f32[104,128]{1,0:T(8,128)S(1)}, bf16[224,176]{1,0:T(8,...) custom-call(s32[2]{0:T(128)S(1)} %pad_add_fusion.role, s32[1,1,32]{2,1,0:T(1,128)} %bitcast.35, ...), custom_call_target="tpu_custom_call" | custom-call | tf_op jit(solution)/shard_map/first/pallas_call | solution.py:485
  3.0 1.0 %collective-permute-start.1 = (f32[29,32,1280]{2,1,0:T(8,128)S(1)}, f32[29,32,1280]{2,1,0:T(8,128)S(1)}, u32[]{:S(2)}, u32[]{:S(2)}) collective-permute-start(f32[29,32,1280]{2,1,0:T(8,128)S(1)} %get-tuple-element.15), channel_id=1, source_target_pairs={{96,64},{97,65},{98,66},{99,67},{100,68},{101,69},{102,70},{103,71... | collective-permute-start | bytes 14254088 | tf_op jit(solution)/shard_map/ppermute | solution.py:506
  3.9 19.4 %all_to_all.10 = f32[32,1,3200]{2,1,0:T(1,128)S(1)} all-to-all(f32[32,1,3200]{2,1,0:T(1,128)S(1)} %bitcast.22), channel_id=1, replica_groups=mesh['grp'=4,'dom'=32] {'dom'}, dimensions={0} | all-to-all | bytes 819200 | tf_op jit(solution)/shard_map/all_to_all | solution.py:508
  23.3 6.9 %collective-permute-start.3 = (f32[800,128]{1,0:T(8,128)S(1)}, f32[800,128]{1,0:T(8,128)S(1)}, u32[]{:S(2)}, u32[]{:S(2)}) collective-permute-start(f32[800,128]{1,0:T(8,128)S(1)} %bitcast.20), channel_id=1, source_target_pairs={{0,96},{32,64},{1,97},{33,65},{2,98},{34,66},{3,99},{35,67},{4,100... | collective-permute-start | bytes 1228808 | tf_op jit(solution)/shard_map/ppermute | solution.py:512
  30.3 0.7 collective-permute-start
  31.0 2.0 %collective-permute-start.4 = (f32[104,128]{1,0:T(8,128)S(1)}, f32[104,128]{1,0:T(8,128)S(1)}, u32[]{:S(2)}, u32[]{:S(2)}) collective-permute-start(f32[104,128]{1,0:T(8,128)S(1)} %get-tuple-element.16), channel_id=1, source_target_pairs={{0,1},{2,3},{4,5},{6,7},{8,9},{10,11},{12,13},{14,15},{16,17},{18,... | collective-permute-start | bytes 159752 | tf_op jit(solution)/shard_map/ppermute | solution.py:531
  33.0 4.6 %collective-permute-start.5 = (f32[104,128]{1,0:T(8,128)S(1)}, f32[104,128]{1,0:T(8,128)S(1)}, u32[]{:S(2)}, u32[]{:S(2)}) collective-permute-start(f32[104,128]{1,0:T(8,128)S(1)} %get-tuple-element.17), channel_id=1, source_target_pairs={{1,2},{3,4},{5,6},{7,8},{9,10},{11,12},{13,14},{15,16},{17,18},{19... | collective-permute-start | bytes 159752 | tf_op jit(solution)/shard_map/ppermute | solution.py:531
  37.6 0.0 collective-permute-done.from_third
  37.6 0.0 collective-permute-done.1.aero_two
  37.6 0.9 %soon.1._soon = f32[24,8,128]{2,1,0:T(8,128)S(1)} custom-call(s32[2]{0:T(128)S(1)} %pad_add_fusion.role, bf16[224,176]{1,0:T(8,128)(2,1)S(1)} %get-tuple-element.12.weights, f32[112,128]{1,0:T(8,128)S(1)} %get-tuple-element.13.solar, f32[800,128]{1,0:T(8,128)S(1)} %bitcast.21, f32[600,128]{1,0:T(8,128)S(1)} %collective-permute-done.from_third, ...), custom_call_target="tpu_custom_call" | custom-call | tf_op jit(solution)/shard_map/soon/pallas_call | solution.py:537
  38.5 3.6 %collective-permute-done.4._pair.of_pair = f32[104,128]{1,0:T(8,128)S(1)} collective-permute-done((f32[104,128]{1,0:T(8,128)S(1)}, f32[104,128]{1,0:T(8,128)S(1)}, u32[]{:S(2)}, u32[]{:S(2)}) %collective-permute-start.4) | collective-permute-done | bytes 53280 | tf_op jit(solution)/shard_map/ppermute | solution.py:531
  42.1 1.1 %collective-permute-done.5._next.of_next = f32[104,128]{1,0:T(8,128)S(1)} collective-permute-done((f32[104,128]{1,0:T(8,128)S(1)}, f32[104,128]{1,0:T(8,128)S(1)}, u32[]{:S(2)}, u32[]{:S(2)}) %collective-permute-start.5) | collective-permute-done | bytes 53280 | tf_op jit(solution)/shard_map/ppermute | solution.py:531
  43.2 0.0 collective-permute-done.3.arrived
  43.2 0.9 %later.1._ = f32[32,8,128]{2,1,0:T(8,128)S(1)} custom-call(s32[2]{0:T(128)S(1)} %pad_add_fusion.role, bf16[224,176]{1,0:T(8,128)(2,1)S(1)} %get-tuple-element.12.weights, f32[112,128]{1,0:T(8,128)S(1)} %get-tuple-element.13.solar, f32[800,128]{1,0:T(8,128)S(1)} %collective-permute-done.3.arrived, f32[104,128]{1,0:T(8,128)S(1)} %collective-permute-done.4._pair.of_pair, ...), custom_call_target="tpu_custom_call" | custom-call | tf_op jit(solution)/shard_map/later/pallas_call | solution.py:537
  44.2 1.3 %collective-permute-start.6 = (f32[32,8,128]{2,1,0:T(8,128)S(1)}, f32[32,8,128]{2,1,0:T(8,128)S(1)}, u32[]{:S(2)}, u32[]{:S(2)}) collective-permute-start(f32[32,8,128]{2,1,0:T(8,128)S(1)} %later.1._), channel_id=1, source_target_pairs={{96,0},{64,32},{97,1},{65,33},{98,2},{66,34},{99,3},{67,35},{100,4... | collective-permute-start | bytes 393224 | tf_op jit(solution)/shard_map/ppermute | solution.py:573
  45.5 0.7 collective-permute-start.2
  46.2 0.0 collective-permute-done.2
  46.2 20.7 %collective-permute-done.6 = f32[32,8,128]{2,1,0:T(8,128)S(1)} collective-permute-done((f32[32,8,128]{2,1,0:T(8,128)S(1)}, f32[32,8,128]{2,1,0:T(8,128)S(1)}, u32[]{:S(2)}, u32[]{:S(2)}) %collective-permute-start.6) | collective-permute-done | bytes 131104 | tf_op jit(solution)/shard_map/ppermute | solution.py:573
  66.8 0.7 maximum_select_fusion
  67.5 3.8 %all-to-all-start.1 = ((f32[32,8,128]{2,1,0:T(8,128)}), f32[32,8,128]{2,1,0:T(8,128)S(1)}, u32[]{:S(2)}, u32[]{:S(2)}) async-start(f32[32,8,128]{2,1,0:T(8,128)} %maximum_select_fusion), calls=%async_computation.1 | async-start | bytes 262144 | tf_op jit(solution)/shard_map/all_to_all | solution.py:576
  71.4 5.0 %diffuse.1.stepped = f32[96,2048]{1,0:T(8,128)} custom-call(s32[2]{0:T(128)S(1)} %pad_add_fusion.role, f32[96,2048]{1,0:T(8,128)} %bitcast.30, f32[1,2048]{1,0:T(1,128)} %kappa.3, s32[3,1,2048]{2,1,0:T(1,128)} %bitcast.33, f32[104,128]{1,0:T(8,128)S(1)} %collective-permute-done.4._pair.of_pair, f32[104,128]{1,0:T(8,128)S(1)} %collective-permute-done.5._next.of_next, ...), custom_call_target="tpu_custom_call" | custom-call | tf_op jit(solution)/shard_map/diffuse/pallas_call | solution.py:557
  76.3 3.5 %all-to-all-done.1.mine = f32[32,8,128]{2,1,0:T(8,128)S(1)} async-done(((f32[32,8,128]{2,1,0:T(8,128)}), f32[32,8,128]{2,1,0:T(8,128)S(1)}, u32[]{:S(2)}, u32[]{:S(2)}) %all-to-all-start.1) | async-done | bytes 131104 | tf_op jit(solution)/shard_map/all_to_all | solution.py:576
  79.8 2.4 %warm.1 = f32[96,2048]{1,0:T(8,128)} custom-call(s32[2]{0:T(128)S(1)} %pad_add_fusion.role, f32[32,8,128]{2,1,0:T(8,128)S(1)} %all-to-all-done.1.mine, s32[1,2048]{1,0:T(1,128)} %parent.3, s32[1,512]{1,0:T(1,128)S(1)} %get-tuple-element.18.slots_in, f32[96,2048]{1,0:T(8,128)} %diffuse.1.stepped), custom_call_target="tpu_custom_call", output_to_operand_aliasing={{}: (4, {})} | custom-call | tf_op jit(solution)/shard_map/warm/pallas_call | solution.py:578
  (2 shorter events, 0.0 us)
Async XLA Ops:
  3.0 34.6 %collective-permute-start.1 = (f32[29,32,1280]{2,1,0:T(8,128)S(1)}, f32[29,32,1280]{2,1,0:T(8,128)S(1)}, u32[]{:S(2)}, u32[]{:S(2)}) collective-permute-start(f32[29,32,1280]{2,1,0:T(8,128)S(1)} %get-tuple-element.15), channel_id=1, source_target_pairs={{96,64},{97,65},{98,66},{99,67},{100,68},{101,69},{102,70},{103,71... | collective-permute-start | bytes 14254088 | tf_op jit(solution)/shard_map/ppermute | solution.py:506
  23.3 19.9 %collective-permute-start.3 = (f32[800,128]{1,0:T(8,128)S(1)}, f32[800,128]{1,0:T(8,128)S(1)}, u32[]{:S(2)}, u32[]{:S(2)}) collective-permute-start(f32[800,128]{1,0:T(8,128)S(1)} %bitcast.20), channel_id=1, source_target_pairs={{0,96},{32,64},{1,97},{33,65},{2,98},{34,66},{3,99},{35,67},{4,100... | collective-permute-start | bytes 1228808 | tf_op jit(solution)/shard_map/ppermute | solution.py:512
  30.3 7.2 %collective-permute-start = (f32[600,128]{1,0:T(8,128)S(1)}, f32[600,128]{1,0:T(8,128)S(1)}, u32[]{:S(2)}, u32[]{:S(2)}) collective-permute-start(f32[600,128]{1,0:T(8,128)S(1)} %bitcast.31), channel_id=1, source_target_pairs={{64,96},{65,97},{66,98},{67,99},{68,100},{69,101},{70,102},{71,103... | collective-permute-start | bytes 921608 | tf_op jit(solution)/shard_map/ppermute | solution.py:511
  31.0 11.1 %collective-permute-start.4 = (f32[104,128]{1,0:T(8,128)S(1)}, f32[104,128]{1,0:T(8,128)S(1)}, u32[]{:S(2)}, u32[]{:S(2)}) collective-permute-start(f32[104,128]{1,0:T(8,128)S(1)} %get-tuple-element.16), channel_id=1, source_target_pairs={{0,1},{2,3},{4,5},{6,7},{8,9},{10,11},{12,13},{14,15},{16,17},{18,... | collective-permute-start | bytes 159752 | tf_op jit(solution)/shard_map/ppermute | solution.py:531
  33.0 10.3 %collective-permute-start.5 = (f32[104,128]{1,0:T(8,128)S(1)}, f32[104,128]{1,0:T(8,128)S(1)}, u32[]{:S(2)}, u32[]{:S(2)}) collective-permute-start(f32[104,128]{1,0:T(8,128)S(1)} %get-tuple-element.17), channel_id=1, source_target_pairs={{1,2},{3,4},{5,6},{7,8},{9,10},{11,12},{13,14},{15,16},{17,18},{19... | collective-permute-start | bytes 159752 | tf_op jit(solution)/shard_map/ppermute | solution.py:531
  44.2 22.7 %collective-permute-start.6 = (f32[32,8,128]{2,1,0:T(8,128)S(1)}, f32[32,8,128]{2,1,0:T(8,128)S(1)}, u32[]{:S(2)}, u32[]{:S(2)}) collective-permute-start(f32[32,8,128]{2,1,0:T(8,128)S(1)} %later.1._), channel_id=1, source_target_pairs={{96,0},{64,32},{97,1},{65,33},{98,2},{66,34},{99,3},{67,35},{100,4... | collective-permute-start | bytes 393224 | tf_op jit(solution)/shard_map/ppermute | solution.py:573
  45.5 0.7 collective-permute-start.2
  67.5 12.3 %all-to-all-start.1 = ((f32[32,8,128]{2,1,0:T(8,128)}), f32[32,8,128]{2,1,0:T(8,128)S(1)}, u32[]{:S(2)}, u32[]{:S(2)}) async-start(f32[32,8,128]{2,1,0:T(8,128)} %maximum_select_fusion), calls=%async_computation.1 | async-start | bytes 262144 | tf_op jit(solution)/shard_map/all_to_all | solution.py:576
